TPU v7x, 32 devices: a whole 2x2x4 slice. The times are simulated.
32 devices in a mesh: row: 8 (over z, x), col: 4 (over y, core).
Axes of the slice: x: 2, y: 2, z: 4, core: 2. Of those that a mesh axis runs over, the one named last changes fastest.
Arguments:
- three_centre: bfloat16 [8, 4, 640, 4096], P('row', 'col'), may hold values from -0.3984375 to 0.3984375
- green_occ: bfloat16 [8, 2, 64, 64], P('row'), may hold values from -0.75 to 0.75
- green_vir: bfloat16 [4, 2, 64, 64], P('col'), may hold values from -0.75 to 0.75
- pair_live: int32 [8, 4], P('row', 'col'), may hold values 0 or 1
Outputs:
- chi_diag: float32 [8, 640, 640], P('row', 'col')
- chi_next: float32 [8, 640, 640], P('row', 'col')
All inputs are finite; a program needn't handle non-finite values. No bound on the sum of `pair_live` on one device may be relied on, other than what follows from the above.
Results may differ from a plain program's by a relative error of at most 0.013.
Values may be sent and summed in bfloat16 or wider, within the bound.
No kernel may reach another device: no remote copies, remote signals or barrier semaphores. Data moves between devices by JAX's collectives and lax.ppermute only.
A program may use at most 128 MiB of HBM per device.

v0:
```python
import jax
import jax.numpy as jnp
from jax import lax
from jax.sharding import PartitionSpec as P


def passed_along(value, axis, by):
    size = lax.axis_size(axis)
    pairs = [(i, i + by) for i in range(size) if 0 <= i + by < size]
    return lax.ppermute(value, axis, pairs)


def contract(left, right):
    return lax.dot_general(
        left, right, (((1,), (1,)), ((), ())), preferred_element_type=jnp.float32
    )


def body(three_centre, green_occ, green_vir, pair_live):
    aux_rows = three_centre.shape[2]
    tile = green_occ.shape[2]
    live = pair_live[0, 0].astype(jnp.bfloat16)
    blocks = (three_centre[0, 0] * live).reshape(aux_rows, tile, tile)
    occ_half = jnp.einsum("pml,smn->spnl", blocks, green_occ[0], preferred_element_type=jnp.float32)
    occ_half = occ_half.astype(jnp.bfloat16).reshape(2, aux_rows, tile * tile)
    vir_half = jnp.einsum("pns,tls->tpnl", blocks, green_vir[0], preferred_element_type=jnp.float32)
    vir_half = vir_half.astype(jnp.bfloat16).reshape(2, aux_rows, tile * tile)
    from_above = passed_along(occ_half[1], "row", -1)
    stacked = jnp.concatenate([occ_half[0], from_above], axis=0)
    shifted_vir = passed_along(vir_half[1], "col", -1)
    vir_total = (vir_half[0].astype(jnp.float32) + shifted_vir.astype(jnp.float32)).astype(
        jnp.bfloat16
    )
    partial_value = contract(stacked, vir_total)
    partial_value = partial_value.reshape(2, aux_rows, aux_rows)
    owned = lax.psum_scatter(
        partial_value.astype(jnp.bfloat16), "col", scatter_dimension=1, tiled=True
    ).astype(jnp.float32)
    return (owned[0][None], owned[1][None])


def solution(mesh):
    return jax.shard_map(
        body,
        mesh=mesh,
        in_specs=(
            P("row", "col", None, None),
            P("row", None, None, None),
            P("col", None, None, None),
            P("row", "col"),
        ),
        out_specs=(P("row", "col", None), P("row", "col", None)),
        check_vma=False,
    )
```

profile of v0, /device:TPU:0, one launch (start us, length us, event | category | flops | bytes accessed | tf_op | source)
XLA Modules:
  0.0 223.2 jit_solution(1213202849760272883)
XLA Ops:
  7.2 0.0 copy-start
  7.2 0.0 reduce-scatter.2.cloned.1.call-start
  7.9 7.9 %copy.9 = bf16[1,1,640,4096]{2,3,1,0:T(8,128)(2,1)} copy(bf16[1,1,640,4096]{3,2,1,0:T(8,128)(2,1)} %param.4) | data formatting | bytes 10485760 | tf_op args[0]
  15.7 3.0 %broadcast_multiply_fusion = bf16[1,1,640,4096]{2,3,1,0:T(8,128)(2,1)S(1)} fusion(bf16[1,1,640,4096]{2,3,1,0:T(8,128)(2,1)} %copy.9, bf16[]{:T(256)} %bitcast), kind=kLoop, calls=%fused_computation.10 | loop fusion | flops 2621440 | bytes 10485762 | tf_op jit(solution)/shard_map/mul | solution.py:23
  18.7 0.0 copy-start.2
  18.7 2.4 %copy-done.2 = bf16[1,1,640,4096]{2,3,1,0:T(8,128)(2,1)} copy-done((bf16[1,1,640,4096]{2,3,1,0:T(8,128)(2,1)}, bf16[1,1,640,4096]{2,3,1,0:T(8,128)(2,1)S(1)}, u32[]{:S(2)}) %copy-start.2) | copy-done | bytes 5242904
  21.1 0.0 copy-done
  21.1 15.1 %convert_bitcast_fusion.1 = bf16[2,640,64,64]{1,2,0,3:T(8,128)(2,1)} fusion(bf16[640,64,64,1]{0,2,1,3:T(8,128)(2,1)S(1)} %bitcast.27, bf16[1,2,64,64]{3,2,1,0:T(8,128)(2,1)S(1)} %copy-done), kind=kOutput, calls=%fused_computation.7 | convolution fusion | flops 676331520 | bytes 15745024 | tf_op jit(solution)/shard_map/pml,smn->spnl/dot_general | solution.py:24
  36.2 9.0 %fusion.15 = (bf16[1,640,64,64]{1,2,0,3:T(8,128)(2,1)}, bf16[1,640,64,64]{1,2,0,3:T(8,128)(2,1)}) fusion(bf16[2,640,64,64]{1,2,0,3:T(8,128)(2,1)} %convert_bitcast_fusion.1), kind=kLoop, calls=%fused_computation.14 | loop fusion | bytes 20971520 | tf_op jit(solution)/shard_map/slice | solution.py:29
  45.2 0.0 copy-start.3
  45.2 0.0 copy-start.5
  45.2 8.0 %copy.13 = bf16[1,640,64,64]{1,3,2,0:T(8,128)(2,1)} copy(bf16[1,640,64,64]{1,2,0,3:T(8,128)(2,1)} %get-tuple-element.3) | data formatting | bytes 10485760 | tf_op jit(solution)/shard_map/slice | solution.py:28
  53.2 1.5 collective-permute-start
  54.7 0.0 copy-done.3
  54.7 0.0 copy-done.5
  54.7 5.5 %convert_bitcast_fusion = bf16[2,640,64,64]{1,3,0,2:T(8,128)(2,1)} fusion(bf16[640,64,64,1]{0,2,3,1:T(8,128)(2,1)S(1)} %bitcast.28, bf16[1,2,64,64]{3,2,1,0:T(8,128)(2,1)S(1)} %copy-done.5), kind=kOutput, calls=%fused_computation.6 | convolution fusion | flops 676331520 | bytes 15745024 | tf_op jit(solution)/shard_map/pns,tls->tpnl/dot_general | solution.py:26
  60.2 9.0 %fusion.16 = (bf16[1,640,64,64]{1,3,0,2:T(8,128)(2,1)}, bf16[1,640,64,64]{1,3,0,2:T(8,128)(2,1)}) fusion(bf16[2,640,64,64]{1,3,0,2:T(8,128)(2,1)} %convert_bitcast_fusion), kind=kLoop, calls=%fused_computation.15 | loop fusion | bytes 20971520 | tf_op jit(solution)/shard_map/slice | solution.py:30
  69.2 1.3 collective-permute-start.1
  70.5 0.0 copy-start.4
  70.5 5.7 %copy.12 = bf16[1,640,64,64]{1,3,2,0:T(8,128)(2,1)S(1)} copy(bf16[1,640,64,64]{1,2,0,3:T(8,128)(2,1)} %get-tuple-element.2) | data formatting | bytes 10485760 | tf_op jit(solution)/shard_map/slice | solution.py:29
  76.1 95.2 %collective-permute-done = bf16[640,4096]{0,1:T(8,128)(2,1)} collective-permute-done((bf16[640,4096]{0,1:T(8,128)(2,1)}, bf16[640,4096]{0,1:T(8,128)(2,1)}, u32[]{:S(2)}, u32[]{:S(2)}) %collective-permute-start) | collective-permute-done | bytes 5242912 | tf_op jit(solution)/shard_map/ppermute | solution.py:10
  171.4 0.0 collective-permute-done.1
  171.4 0.0 copy-done.4
  171.4 0.0 copy-start.1
  171.4 12.9 %fusion.7 = bf16[1280,640]{1,0:T(8,128)(2,1)} fusion(bf16[640,4096]{0,1:T(8,128)(2,1)S(1)} %bitcast.29, bf16[640,4096]{0,1:T(8,128)(2,1)} %collective-permute-done.1, bf16[640,4096]{0,1:T(8,128)(2,1)} %collective-permute-done, bf16[640,4096]{0,1:T(8,128)(2,1)S(1)} %bitcast.31), kind=kOutput, calls=%fused_computation.9 | convolution fusion | flops 6743162880 | bytes 22609920 | tf_op jit(solution)/shard_map/dot_general | solution.py:14
  184.3 0.0 reduce-scatter.2.cloned.1.call-update
  184.3 30.1 %reduce-scatter.2.cloned.1.call-done = bf16[2,160,640]{2,1,0:T(8,128)(2,1)} async-done(((bf16[2,640,640]{2,1,0:T(8,128)(2,1)}), bf16[2,160,640]{2,1,0:T(8,128)(2,1)}) %reduce-scatter.2.cloned.1.call-update) | async-done | bytes 409616 | tf_op jit(solution)/shard_map/reduce_scatter | solution.py:36
  214.4 2.0 fusion.17
  216.4 0.0 copy-done.1
Async XLA Ops:
  7.2 13.9 %copy-start = (bf16[1,2,64,64]{3,2,1,0:T(8,128)(2,1)S(1)}, bf16[1,2,64,64]{3,2,1,0:T(8,128)(2,1)}, u32[]{:S(2)}) copy-start(bf16[1,2,64,64]{3,2,1,0:T(8,128)(2,1)} %param.5) | copy-start | bytes 49156
  7.2 207.2 %reduce-scatter.2.cloned.1.call-start = ((), (), s32[]{:S(2)}) async-start(), calls=%async_computation.1 | async-start | bytes 2048000 | tf_op jit(solution)/shard_map/reduce_scatter | solution.py:36
  18.7 2.4 %copy-start.2 = (bf16[1,1,640,4096]{2,3,1,0:T(8,128)(2,1)}, bf16[1,1,640,4096]{2,3,1,0:T(8,128)(2,1)S(1)}, u32[]{:S(2)}) copy-start(bf16[1,1,640,4096]{2,3,1,0:T(8,128)(2,1)S(1)} %broadcast_multiply_fusion) | copy-start | bytes 15728644
  45.2 9.5 %copy-start.3 = (bf16[1,1,640,4096]{2,3,1,0:T(8,128)(2,1)S(1)}, bf16[1,1,640,4096]{2,3,1,0:T(8,128)(2,1)}, u32[]{:S(2)}) copy-start(bf16[1,1,640,4096]{2,3,1,0:T(8,128)(2,1)} %copy-done.2) | copy-start | bytes 15728644
  45.2 9.5 %copy-start.5 = (bf16[1,2,64,64]{3,2,1,0:T(8,128)(2,1)S(1)}, bf16[1,2,64,64]{3,2,1,0:T(8,128)(2,1)}, u32[]{:S(2)}) copy-start(bf16[1,2,64,64]{3,2,1,0:T(8,128)(2,1)} %param.6) | copy-start | bytes 49156
  53.2 118.2 %collective-permute-start = (bf16[640,4096]{0,1:T(8,128)(2,1)}, bf16[640,4096]{0,1:T(8,128)(2,1)}, u32[]{:S(2)}, u32[]{:S(2)}) collective-permute-start(bf16[640,4096]{0,1:T(8,128)(2,1)} %bitcast.7), channel_id=1, source_target_pairs={{4,0},{8,4},{12,8},{16,12},{20,16},{24,20},{28,24},{5,1},{9,5},{13... | collective-permute-start | bytes 15728648 | tf_op jit(solution)/shard_map/ppermute | solution.py:10
  69.2 102.2 %collective-permute-start.1 = (bf16[640,4096]{0,1:T(8,128)(2,1)}, bf16[640,4096]{0,1:T(8,128)(2,1)}, u32[]{:S(2)}, u32[]{:S(2)}) collective-permute-start(bf16[640,4096]{0,1:T(8,128)(2,1)} %bitcast.30), channel_id=1, source_target_pairs={{1,0},{2,1},{3,2},{5,4},{6,5},{7,6},{9,8},{10,9},{11,10},{13,12},{... | collective-permute-start | bytes 15728648 | tf_op jit(solution)/shard_map/ppermute | solution.py:10
  70.5 100.9 %copy-start.4 = (bf16[1,640,64,64]{1,3,0,2:T(8,128)(2,1)S(1)}, bf16[1,640,64,64]{1,3,0,2:T(8,128)(2,1)}, u32[]{:S(2)}) copy-start(bf16[1,640,64,64]{1,3,0,2:T(8,128)(2,1)} %get-tuple-element.5) | copy-start | bytes 15728644
  171.4 45.0 %copy-start.1 = (bf16[1,2,64,64]{3,2,1,0:T(8,128)(2,1)S(1)}, bf16[1,2,64,64]{3,2,1,0:T(8,128)(2,1)}, u32[]{:S(2)}) copy-start(bf16[1,2,64,64]{3,2,1,0:T(8,128)(2,1)} %param.5) | copy-start | bytes 49156
Sparse Core Ops, SparseCore 0:
  184.4 29.9 reduce-scatter.1
where the time goes:
time: 224 us; the launch traced here: 223 us
  waiting for transfers between devices  125 us (56%)
  local copies, waits for them, and re-layouts  43.8 us (20%)
  matrix products  33.6 us (15%)
  between operations  14.7 us (7%)
  other arithmetic  2.96 us (1%)
  starting transfers between devices  2.78 us (1%)
    ppermute x2, waiting for transfers between devices, passed_along(): return lax.ppermute(value, axis, pairs)  95.2 us
    reduce_scatter x1, waiting for transfers between devices, body(): lax.psum_scatter(partial_value.astype(jnp.bfloat16), 'col', scatter_dimen...  30.1 us
    dot_general x1, matrix products, body(): jnp.einsum('pml,smn->spnl', blocks, green_occ[0], preferred_element_type=...  15.1 us
    slice x2, local copies, waits for them, and re-layouts, body(): stacked = jnp.concatenate([occ_half[0], from_above], axis=0)  14.6 us
    dot_general x1, matrix products, contract(): lax.dot_general(left, right, (((1,), (1,)), ((), ())), preferred_element_...  12.9 us
    unnamed x13, local copies, waits for them, and re-layouts  10.3 us
    slice x1, local copies, waits for them, and re-layouts, body(): shifted_vir = passed_along(vir_half[1], 'col', -1)  8.97 us
    slice x1, local copies, waits for them, and re-layouts, body(): from_above = passed_along(occ_half[1], 'row', -1)  7.99 us
  transfers between devices with their start and end apart: 3, of which 2 were waited for; matrix products, arithmetic and copies ran while one was open for 9% of the time, Pallas kernels for 0%

commit v1 on v0

v1 whole, which is shorter than its diff:
```python
import jax
import jax.numpy as jnp
from jax import lax
from jax.experimental import pallas as pl
from jax.experimental.pallas import tpu as pltpu
from jax.sharding import PartitionSpec as P

BF = jnp.bfloat16
F32 = jnp.float32
VMEM_BYTES = 56 * 1024 * 1024
LAM_GROUP = 16
SPAN = 256


def dot(a, b, dims=((1,), (0,))):
    return lax.dot_general(a, b, (dims, ((), ())), preferred_element_type=F32)


def iota(shape, axis):
    return lax.broadcasted_iota(jnp.int32, shape, axis)


def spread_rows(g, group):
    m, k = g.shape
    rows, cols = (m * group, m), (k, k * group)
    pick_row = (iota(rows, 0) // group == iota(rows, 1)).astype(BF)
    pick_col = (iota(cols, 1) // group == iota(cols, 0)).astype(BF)
    tall = dot(pick_row, g).astype(BF)
    full = dot(tall, pick_col)
    same = iota(full.shape, 0) % group == iota(full.shape, 1) % group
    return jnp.where(same, full, 0.0).astype(BF)


def repeated(g, count):
    t = g.shape[0]
    n = t * count
    pick = (iota((n, t), 0) % t == iota((n, t), 1)).astype(BF)
    tall = dot(pick, g).astype(BF)
    full = dot(tall, pick, ((1,), (1,)))
    same = iota(full.shape, 0) // t == iota(full.shape, 1) // t
    return jnp.where(same, full, 0.0).astype(BF)


def fill_forms(f_ref, kron_ref):
    for i in range(f_ref.shape[0]):
        kron_ref[i] = repeated(f_ref[i], SPAN // f_ref.shape[1])


def params():
    return pltpu.CompilerParams(vmem_limit_bytes=VMEM_BYTES)


def cost(flops, size):
    return pl.CostEstimate(flops=flops, bytes_accessed=size, transcendentals=0)


def occ_step(right, kron_ref, out_refs):
    width = right.shape[1]
    at = 0
    for out in out_refs:
        rows = out.shape[0]
        done = 0
        while done < rows:
            take = min(rows - done, 32)
            part = kron_ref[at * LAM_GROUP : (at + take) * LAM_GROUP]
            out[done : done + take] = dot(part, right).astype(BF).reshape(take, LAM_GROUP, width)
            done += take
            at += take


def turn_occ_kernel(live_ref, g_ref, y_ref, yt_out, *rest, units):
    *outs, yt_ref, kron_ref = rest
    tile, _, width = yt_ref.shape
    per = tile // units
    step = pl.program_id(0)

    @pl.when(step == 0)
    def _():
        kron_ref[...] = spread_rows(g_ref[...], LAM_GROUP)

    @pl.when(step < units)
    def _():
        scale = live_ref[0].astype(F32)
        eye = jnp.where(iota((SPAN, SPAN), 0) == iota((SPAN, SPAN), 1), scale, 0.0).astype(BF)
        turned = dot(eye, y_ref[...], ((1,), (1,))).astype(BF)
        yt_ref[pl.ds(step * per, per)] = turned.reshape(per, tile, width)

    for s in range(tile // LAM_GROUP):

        @pl.when(step == units + s)
        def _(s=s):
            part = yt_ref[:, s * LAM_GROUP : (s + 1) * LAM_GROUP, :]
            yt_out[...] = part
            occ_step(part.reshape(tile * LAM_GROUP, width), kron_ref, outs)


def turn_occ(live, mats, y, tile, parts):
    m = mats.shape[0]
    aux, size = y.shape
    units = size // SPAN
    groups = tile // LAM_GROUP
    late = lambda i: (0, jnp.maximum(i - units, 0), 0)
    return pl.pallas_call(
        lambda *refs: turn_occ_kernel(*refs, units=units),
        grid=(units + groups,),
        in_specs=[
            pl.BlockSpec(memory_space=pltpu.SMEM),
            pl.BlockSpec((m, tile), lambda i: (0, 0)),
            pl.BlockSpec((aux, SPAN), lambda i: (0, jnp.minimum(i, units - 1))),
        ],
        out_specs=[pl.BlockSpec((n, LAM_GROUP, aux), late) for n in (tile, *parts)],
        out_shape=[jax.ShapeDtypeStruct((n, tile, aux), BF) for n in (tile, *parts)],
        scratch_shapes=[pltpu.VMEM((tile, tile, aux), BF), pltpu.VMEM((m * LAM_GROUP, tile * LAM_GROUP), BF)],
        compiler_params=params(),
        cost_estimate=cost(2 * aux * size * (SPAN + m * LAM_GROUP), 2 * aux * (2 * size + m * tile)),
        name="turn_and_occ",
    )(live, mats, y)


def occ_kernel(g_ref, yt_ref, *rest):
    *outs, kron_ref = rest

    @pl.when(pl.program_id(0) == 0)
    def _():
        kron_ref[...] = spread_rows(g_ref[...], LAM_GROUP)

    tile, group, width = yt_ref.shape
    occ_step(yt_ref[...].reshape(tile * group, width), kron_ref, outs)


def occ(mats, yt, parts):
    m = mats.shape[0]
    tile, _, aux = yt.shape
    block = lambda n: pl.BlockSpec((n, LAM_GROUP, aux), lambda i: (0, i, 0))
    return pl.pallas_call(
        occ_kernel,
        grid=(tile // LAM_GROUP,),
        in_specs=[pl.BlockSpec((m, tile), lambda i: (0, 0)), block(tile)],
        out_specs=[block(n) for n in parts],
        out_shape=[jax.ShapeDtypeStruct((n, tile, aux), BF) for n in parts],
        scratch_shapes=[pltpu.VMEM((m * LAM_GROUP, tile * LAM_GROUP), BF)],
        compiler_params=params(),
        cost_estimate=cost(2 * aux * tile * tile * m * LAM_GROUP, 2 * aux * tile * (tile + m)),
        name="occ",
    )(mats, yt)


def vir_kernel(f_ref, s_ref, shifted_ref, out_ref, kron_ref):
    @pl.when(pl.program_id(0) == 0)
    def _():
        fill_forms(f_ref, kron_ref)

    out_ref[...] = (dot(kron_ref[0], s_ref[...]) + dot(kron_ref[1], shifted_ref[...])).astype(BF)


def vir(forms, s, shifted):
    rows, width = s.shape
    block = pl.BlockSpec((SPAN, width), lambda i: (i, 0))
    return pl.pallas_call(
        vir_kernel,
        grid=(rows // SPAN,),
        in_specs=[pl.BlockSpec(forms.shape, lambda i: (0, 0, 0)), block, block],
        out_specs=block,
        out_shape=jax.ShapeDtypeStruct((rows, width), BF),
        scratch_shapes=[pltpu.VMEM((2, SPAN, SPAN), BF)],
        compiler_params=params(),
        cost_estimate=cost(4 * rows * width * SPAN, 6 * rows * width),
        name="vir",
    )(forms, s, shifted)


def within(first, count):
    return lambda i: jnp.clip(i - first, 0, count - 1)


def diag_kernel(live_ref, f_ref, y_ref, t_ref, below2_ref, below1_ref, shifted_ref, out_ref, kron_ref, acc_ref, *, n2, n1):
    step = pl.program_id(0)

    @pl.when(step == 0)
    def _():
        fill_forms(f_ref, kron_ref)
        acc_ref[...] = jnp.zeros(acc_ref.shape, F32)

    live = live_ref[0].astype(F32)
    t = t_ref[...]
    own = dot(kron_ref[0], t) * live

    @pl.when(step < n2 + n1)
    def _():
        below = jnp.where(step < n2, below2_ref[...], below1_ref[...])
        acc_ref[...] += dot(y_ref[...], own.astype(BF)) + dot(below, dot(kron_ref[2], t).astype(BF))

    @pl.when(step >= n2 + n1)
    def _():
        total = own + dot(kron_ref[1], shifted_ref[...]) * live
        acc_ref[...] += dot(y_ref[...], total.astype(BF))

    @pl.when(step == pl.num_programs(0) - 1)
    def _():
        out_ref[...] = acc_ref[...]


def diag(live, forms, y, t, below2, below1, shifted):
    aux, size = y.shape
    units = size // SPAN
    n2, n1, nc = below2.shape[1] // SPAN, below1.shape[1] // SPAN, shifted.shape[0] // SPAN
    natural = lambda index: pl.BlockSpec((aux, SPAN), lambda i: (0, index(i)))
    turned = lambda index: pl.BlockSpec((SPAN, aux), lambda i: (index(i), 0))
    return pl.pallas_call(
        lambda *refs: diag_kernel(*refs, n2=n2, n1=n1),
        grid=(units,),
        in_specs=[
            pl.BlockSpec(memory_space=pltpu.SMEM),
            pl.BlockSpec(forms.shape, lambda i: (0, 0, 0)),
            natural(lambda i: i),
            turned(lambda i: i),
            natural(within(0, n2)),
            natural(within(n2, n1)),
            turned(within(n2 + n1, nc)),
        ],
        out_specs=pl.BlockSpec((aux, aux), lambda i: (0, 0)),
        out_shape=jax.ShapeDtypeStruct((aux, aux), F32),
        scratch_shapes=[pltpu.VMEM((3, SPAN, SPAN), BF), pltpu.VMEM((aux, aux), F32)],
        compiler_params=params(),
        cost_estimate=cost(2 * aux * size * (2 * SPAN + 2 * aux), 6 * aux * size),
        name="diag_product",
    )(live, forms, y, t, below2, below1, shifted)


def early_kernel(parity_ref, fw_ref, fv_ref, r2_ref, w_ref, ws_ref, raw_e_ref, v_ref, vs_ref, raw_o_ref, vc_ref, vcs_ref,
                 edge_ref, odd_ref, kw_ref, kv_ref, a1_ref, a2_ref):
    step = pl.program_id(0)
    even = parity_ref[0] == 0

    @pl.when(step == 0)
    def _():
        fill_forms(fw_ref, kw_ref)
        fill_forms(fv_ref, kv_ref)
        a1_ref[...] = jnp.zeros(a1_ref.shape, F32)
        a2_ref[...] = jnp.zeros(a2_ref.shape, F32)

    @pl.when(even)
    def _():
        w = (dot(kw_ref[0], w_ref[...]) + dot(kw_ref[1], ws_ref[...])).astype(BF)
        a1_ref[...] += dot(r2_ref[...], w)
        v = (dot(kv_ref[0], v_ref[...]) + dot(kv_ref[1], vs_ref[...])).astype(BF)
        a2_ref[...] += dot(raw_e_ref[...], v)

    @pl.when(jnp.logical_not(even))
    def _():
        v = (dot(kv_ref[0], vc_ref[...]) + dot(kv_ref[1], vcs_ref[...])).astype(BF)
        a2_ref[...] += dot(raw_o_ref[...], v)

    @pl.when(step == pl.num_programs(0) - 1)
    def _():
        edge_ref[...] = a1_ref[...]
        odd_ref[...] = a2_ref[...].T


def early(parity, form_z, form_x, r2, w, ws, raw_e, v, vs, raw_o, vc, vcs):
    aux = r2.shape[0]
    n2, nc = r2.shape[1] // SPAN, raw_o.shape[1] // SPAN
    natural = lambda n: pl.BlockSpec((aux, SPAN), lambda i: (0, jnp.minimum(i, n - 1)))
    turned = lambda n: pl.BlockSpec((SPAN, aux), lambda i: (jnp.minimum(i, n - 1), 0))
    assert n2 == nc
    whole = pl.BlockSpec((aux, aux), lambda i: (0, 0))
    forms = pl.BlockSpec(form_z.shape, lambda i: (0, 0, 0))
    return pl.pallas_call(
        early_kernel,
        grid=(n2,),
        in_specs=[
            pl.BlockSpec(memory_space=pltpu.SMEM), forms, forms,
            natural(n2), turned(n2), turned(n2),
            natural(n2), turned(n2), turned(n2),
            natural(nc), turned(nc), turned(nc),
        ],
        out_specs=[whole, whole],
        out_shape=[jax.ShapeDtypeStruct((aux, aux), F32)] * 2,
        scratch_shapes=[pltpu.VMEM((2, SPAN, SPAN), BF)] * 2 + [pltpu.VMEM((aux, aux), F32)] * 2,
        compiler_params=params(),
        cost_estimate=cost(4 * aux * n2 * SPAN * (2 * SPAN + aux), 12 * aux * n2 * SPAN),
        name="early_edges",
    )(parity, form_z, form_x, r2, w, ws, raw_e, v, vs, raw_o, vc, vcs)


def last_kernel(parity_ref, fw_ref, so_far_ref, r1_ref, w_ref, ws_ref, v_ref, yc_ref, wc_ref, out_ref, kw_ref, a1_ref, a2_ref, *, nc):
    step = pl.program_id(0)
    even = parity_ref[0] == 0

    @pl.when(step == 0)
    def _():
        fill_forms(fw_ref, kw_ref)
        a1_ref[...] = so_far_ref[...]
        a2_ref[...] = jnp.zeros(a2_ref.shape, F32)

    @pl.when(even)
    def _():
        w = (dot(kw_ref[0], w_ref[...]) + dot(kw_ref[1], ws_ref[...])).astype(BF)
        r1 = r1_ref[...]
        a1_ref[...] += dot(r1, w)
        a2_ref[...] += dot(r1, v_ref[...])

    @pl.when(jnp.logical_and(jnp.logical_not(even), step < nc))
    def _():
        a1_ref[...] += dot(yc_ref[...], wc_ref[...])

    @pl.when(step == pl.num_programs(0) - 1)
    def _():
        out_ref[0] = a1_ref[...]
        out_ref[1] = a2_ref[...].T


def last(parity, form_z, so_far, r1, w, ws, n2, v, yc, wc):
    aux = r1.shape[0]
    n1, nc = r1.shape[1] // SPAN, yc.shape[1] // SPAN
    natural = lambda n: pl.BlockSpec((aux, SPAN), lambda i: (0, jnp.minimum(i, n - 1)))
    turned = lambda n, at=0: pl.BlockSpec((SPAN, aux), lambda i: (at + jnp.minimum(i, n - 1), 0))
    return pl.pallas_call(
        lambda *refs: last_kernel(*refs, nc=nc),
        grid=(n1,),
        in_specs=[
            pl.BlockSpec(memory_space=pltpu.SMEM),
            pl.BlockSpec(form_z.shape, lambda i: (0, 0, 0)),
            pl.BlockSpec((aux, aux), lambda i: (0, 0)),
            natural(n1), turned(n1, n2), turned(n1, n2), turned(n1), natural(nc), turned(nc),
        ],
        out_specs=pl.BlockSpec((2, aux, aux), lambda i: (0, 0, 0)),
        out_shape=jax.ShapeDtypeStruct((2, aux, aux), F32),
        scratch_shapes=[pltpu.VMEM((2, SPAN, SPAN), BF)] + [pltpu.VMEM((aux, aux), F32)] * 2,
        compiler_params=params(),
        cost_estimate=cost(4 * aux * n1 * SPAN * (SPAN + aux), 10 * aux * n1 * SPAN),
        name="last_edges",
    )(parity, form_z, so_far, r1, w, ws, v, yc, wc)


def scattered(value, axis):
    size = lax.axis_size(axis)
    if size & (size - 1):
        return lax.psum_scatter(value.astype(BF), axis, scatter_dimension=1, tiled=True).astype(F32)
    me = lax.axis_index(axis)
    k, aux, width = value.shape
    blocks = value.reshape(k, size, aux // size, width)
    reach = 1
    while reach < size:
        bit = (me // reach) % 2
        pairs = blocks.reshape(k, blocks.shape[1] // 2, 2, *blocks.shape[2:])
        kept = lax.dynamic_index_in_dim(pairs, bit, 2, keepdims=False)
        given = lax.dynamic_index_in_dim(pairs, 1 - bit, 2, keepdims=False).astype(BF)
        got = lax.ppermute(given, axis, [(i, i ^ reach) for i in range(size)])
        blocks = kept + got.astype(F32)
        reach *= 2
    return blocks[:, 0]


def body(three_centre, green_occ, green_vir, pair_live):
    rows, cols = lax.axis_size("row"), lax.axis_size("col")
    tile = green_occ.shape[2]
    y = three_centre[0, 0]
    parity = (lax.axis_index("row") % 2).astype(jnp.int32)
    even = parity == 0
    parity = parity[None]
    live = pair_live[0]
    live_bf = live[0].astype(BF)

    units = tile * tile // SPAN
    per = SPAN // tile
    n2 = nc = max(1, units * 5 // 16)
    n1 = units - n2 - nc
    cut2, cut1 = n2 * SPAN, (n2 + n1) * SPAN
    mu2, mu1 = n2 * per, (n2 + n1) * per

    down = [(i, i - 1) for i in range(1, cols)]
    up = [(i, i + 1) for i in range(cols - 1)]

    def in_rows(start, pairs):
        return [(r * cols + a, r * cols + b) for r in range(start, rows, 2) for a, b in pairs]

    both = ("row", "col")
    to_even = [(i, i - 1) for i in range(1, rows, 2)]
    to_odd = [(i, i + 1) for i in range(0, rows, 2)]
    flat = lambda s: s.reshape(-1, s.shape[-1])

    y_a2 = y[:, :cut2] * live_bf
    r2 = lax.ppermute(y_a2, "row", to_even)
    y_c = y[:, cut1:] * live_bf
    raw_c = lax.ppermute(y_c, "row", [(i, i + 2) for i in range(1, rows - 2, 2)])
    y_a1 = y[:, cut2:cut1] * live_bf
    r1 = lax.ppermute(y_a1, "row", to_even)

    occ_above = lax.ppermute(green_occ[0, 1], "row", [(i, i - 1) for i in range(1, rows)])
    vir_above = lax.ppermute(green_vir[0, 1], "col", down)
    form_x = jnp.stack([green_vir[0, 0].T, green_vir[0, 1].T])
    form_z = jnp.stack([green_vir[0, 0], vir_above])
    occ_x = green_occ[0, 1].T

    yt, sv_1, sv_c = turn_occ(
        live, jnp.concatenate([occ_x[mu2:mu1], occ_x[mu1:]]), y, tile, (mu1 - mu2, tile - mu1)
    )
    sv_1, sv_c = flat(sv_1), flat(sv_c)
    sv_1s = lax.ppermute(sv_1, both, in_rows(0, up))
    sv_c = lax.ppermute(sv_c, "row", to_odd)
    sw_c, sw_a, sv_2 = occ(
        jnp.concatenate([occ_above[mu1:], occ_above[:mu1], occ_x[:mu2]]), yt, (tile - mu1, mu1, mu2)
    )
    sw_c, sw_a, sv_2 = flat(sw_c), flat(sw_a), flat(sv_2)
    sw_cs = lax.ppermute(sw_c, both, in_rows(0, down))
    sw_as = lax.ppermute(sw_a, both, in_rows(0, down))
    sv_2s = lax.ppermute(sv_2, both, in_rows(0, up))
    (t,) = occ(green_occ[0, 0], yt, (tile,))
    t = flat(t)
    t_shifted = lax.ppermute(t[cut1:], "col", down)
    below2 = lax.ppermute(y_a2, "col", up)
    below1 = lax.ppermute(y_a1, "col", up)

    v_1 = lax.ppermute(vir(form_x, sv_1, sv_1s), "row", [(i, i - 2) for i in range(2, rows, 2)])
    w_c = lax.ppermute(vir(form_z, sw_c, sw_cs), "row", to_odd)
    raw_2 = lax.ppermute(r2, "row", [(i, i + 2) for i in range(0, rows - 2, 2)])
    sv_cs = lax.ppermute(sv_c, both, in_rows(1, up))

    edge, side = early(parity, form_z, form_x, r2, sw_a, sw_as, raw_2, sv_2, sv_2s, raw_c, sv_c, sv_cs)
    chi_d = diag(live, jnp.concatenate([form_z, green_vir[:, 1]]), y, t, below2, below1, t_shifted)
    ahead = scattered(jnp.stack([chi_d, side]), "col")
    chi_d, side = ahead[0], ahead[1]
    side = lax.ppermute(side.astype(BF), "row", [(i, i - 2) for i in range(2, rows)]).astype(F32)
    ends = scattered(last(parity, form_z, edge, r1, sw_a, sw_as, n2, v_1, y_c, w_c), "col")
    sent = jnp.where(even, ends[1] + side, ends[0]).astype(BF)
    got = lax.ppermute(sent, "row", [(i, i ^ 1) for i in range(rows)]).astype(F32)
    chi_n = got + jnp.where(even, ends[0], side)
    return chi_d[None], chi_n[None]


def solution(mesh):
    return jax.shard_map(
        body,
        mesh=mesh,
        in_specs=(
            P("row", "col", None, None),
            P("row", None, None, None),
            P("col", None, None, None),
            P("row", "col"),
        ),
        out_specs=(P("row", "col", None), P("row", "col", None)),
        check_vma=False,
    )
```

time: 224 us -> 274 us (1.22)
  Pallas kernels: 0 us -> 102 us
  starting transfers between devices: 2.78 us -> 63.5 us
  waiting for transfers between devices: 125 us -> 79.4 us
  matrix products: 33.6 us -> 0 us
  local copies, waits for them, and re-layouts: 43.8 us -> 11.7 us
  between operations: 14.7 us -> 1.57 us
  other arithmetic: 2.96 us -> 14.9 us
    pallas_call x0 -> x8, Pallas kernels: none -> 102 us  [the longest x2 23.5 us: occ(): pl.pallas_call(occ_kernel, grid=(tile // LAM_GROUP,), in_specs=[pl.BlockS...]
    ppermute x2 -> x23, starting transfers between devices: 2.74 us -> 63.5 us  [the longest x4 20.8 us: scattered(): got = lax.ppermute(given, axis, [(i, i ^ reach) for i in range(size)])]
    dot_general x3 -> x0, matrix products: 33.6 us -> none  [the longest x1 15.1 us: body(): jnp.einsum('pml,smn->spnl', blocks, green_occ[0], preferred_element_type=...]
    slice x5 -> x7, local copies, waits for them, and re-layouts: 33.6 us -> 3.23 us  [the longest x1 1.58 us: body(): t_shifted = lax.ppermute(t[cut1:], 'col', down)]
    reduce_scatter x1 -> x0, waiting for transfers between devices: 30.1 us -> none  [body(): lax.psum_scatter(partial_value.astype(jnp.bfloat16), 'col', scatter_dimen...]
    ppermute x2 -> x23, waiting for transfers between devices: 95.2 us -> 79.4 us  [the longest x1 36.1 us: body(): lax.ppermute(green_occ[0, 1], 'row', [(i, i - 1) for i in range(1, rows)])]
    unnamed x13 -> x25, local copies, waits for them, and re-layouts: 10.3 us -> 3.85 us
    add x0 -> x4, other arithmetic: none -> 4.52 us  [scattered(): blocks = kept + got.astype(F32)]
  transfers between devices with their start and end apart: 3 -> 23, of which waited for: 2 -> 7; matrix products, arithmetic and copies ran while one was open for 9% -> 7% of each run, Pallas kernels for 0% -> 37%
where the time goes in v1:
time: 274 us; the launch traced here: 273 us
  Pallas kernels  102 us (37%)
  waiting for transfers between devices  79.4 us (29%)
  starting transfers between devices  63.5 us (23%)
  other arithmetic  14.9 us (5%)
  local copies, waits for them, and re-layouts  11.7 us (4%)
    ppermute x1, waiting for transfers between devices, body(): lax.ppermute(green_occ[0, 1], 'row', [(i, i - 1) for i in range(1, rows)])  36.1 us
    pallas_call x2, Pallas kernels, occ(): pl.pallas_call(occ_kernel, grid=(tile // LAM_GROUP,), in_specs=[pl.BlockS...  23.5 us
    pallas_call x1, Pallas kernels, diag(): pl.pallas_call(lambda *refs: diag_kernel(*refs, n2=n2, n1=n1), grid=(unit...  22.3 us
    ppermute x4, starting transfers between devices, scattered(): got = lax.ppermute(given, axis, [(i, i ^ reach) for i in range(size)])  20.8 us
    pallas_call x1, Pallas kernels, turn_occ(): pl.pallas_call(lambda *refs: turn_occ_kernel(*refs, units=units), grid=(u...  18.8 us
    ppermute x1, waiting for transfers between devices, body(): raw_2 = lax.ppermute(r2, 'row', [(i, i + 2) for i in range(0, rows - 2, 2)])  16 us
    ppermute x4, waiting for transfers between devices, scattered(): got = lax.ppermute(given, axis, [(i, i ^ reach) for i in range(size)])  14.8 us
    pallas_call x1, Pallas kernels, early(): pl.pallas_call(early_kernel, grid=(n2,), in_specs=[pl.BlockSpec(memory_sp...  12.9 us
  transfers between devices with their start and end apart: 23, of which 7 were waited for; matrix products, arithmetic and copies ran while one was open for 7% of the time, Pallas kernels for 37%

profile of v1, /device:TPU:0, one launch (start us, length us, event | category | flops | bytes accessed | tf_op | source)
XLA Modules:
  0.0 272.8 jit_solution(10572116411574675342)
XLA Ops:
  1.3 3.3 %slice_multiply_fusion.1 = (bf16[640,1280]{1,0:T(8,128)(2,1)S(1)}, bf16[640,1280]{1,0:T(8,128)(2,1)}) fusion(bf16[640,4096]{1,0:T(8,128)(2,1)} %bitcast.87, bf16[]{:T(256)} %bitcast.10), kind=kLoop, calls=%fused_computation.11 | loop fusion | flops 1638400 | bytes 6553602 | tf_op jit(solution)/shard_map/mul | solution.py:385
  4.6 3.5 %collective-permute-start.1 = (bf16[640,1280]{1,0:T(8,128)(2,1)}, bf16[640,1280]{1,0:T(8,128)(2,1)}, u32[]{:S(2)}, u32[]{:S(2)}) collective-permute-start(bf16[640,1280]{1,0:T(8,128)(2,1)} %get-tuple-element.19), channel_id=1, source_target_pairs={{0,1},{1,2},{2,3},{4,5},{5,6},{6,7},{8,9},{9,10},{10,11},{12,13},{... | collective-permute-start | bytes 4915208 | tf_op jit(solution)/shard_map/ppermute | solution.py:412
  9.5 18.8 %turn_and_occ.1 = (bf16[64,64,640]{2,1,0:T(8,128)(2,1)}, bf16[24,64,640]{2,1,0:T(8,128)(2,1)}, bf16[20,64,640]{2,1,0:T(8,128)(2,1)}) custom-call(s32[1]{0:T(128)} %bitcast.76.refs_0_, bf16[44,64]{1,0:T(8,128)(2,1)} %concatenate.15.refs_1_, bf16[640,4096]{1,0:T(8,128)(2,1)} %bitcast.88), custom_call_target="tpu_custom_call" | custom-call | flops 5033164800 | bytes 14090240 | tf_op jit(solution)/shard_map/turn_and_occ/pallas_call | solution.py:103
  28.3 10.5 %occ.2 = bf16[64,64,640]{2,1,0:T(8,128)(2,1)} custom-call(bf16[64,64]{1,0:T(8,128)(2,1)} %get-tuple-element.26.g_ref, bf16[64,64,640]{2,1,0:T(8,128)(2,1)} %get-tuple-element.10.yt_ref), custom_call_target="tpu_custom_call" | custom-call | flops 5368709120 | bytes 10485760 | tf_op jit(solution)/shard_map/occ/pallas_call | solution.py:135
  38.8 1.6 slice.82
  40.4 1.3 collective-permute-start.3
  41.7 1.3 collective-permute-start.4
  43.0 1.3 collective-permute-start.5
  44.3 1.3 collective-permute-start
  45.6 36.1 %collective-permute-done.5 = bf16[64,64]{0,1:T(8,128)(2,1)S(1)} collective-permute-done((bf16[64,64]{0,1:T(8,128)(2,1)S(1)}, bf16[64,64]{0,1:T(8,128)(2,1)S(1)}, u32[]{:S(2)}, u32[]{:S(2)}) %collective-permute-start.5) | collective-permute-done | bytes 8224 | tf_op jit(solution)/shard_map/ppermute | solution.py:390
  81.7 1.9 collective-permute-start.9
  84.5 7.2 %collective-permute-start.10 = (bf16[1280,640]{1,0:T(8,128)(2,1)}, bf16[1280,640]{1,0:T(8,128)(2,1)}, u32[]{:S(2)}, u32[]{:S(2)}) collective-permute-start(bf16[1280,640]{1,0:T(8,128)(2,1)} %bitcast.105), channel_id=1, source_target_pairs={{0,4},{8,12},{16,20},{24,28},{1,5},{9,13},{17,21},{25,29},{2,6},{1... | collective-permute-start | bytes 4915208 | tf_op jit(solution)/shard_map/ppermute | solution.py:401
  91.7 13.0 %occ.3 = (bf16[20,64,640]{2,1,0:T(8,128)(2,1)}, bf16[44,64,640]{2,1,0:T(8,128)(2,1)}, bf16[20,64,640]{2,1,0:T(8,128)(2,1)}) custom-call(bf16[84,64]{1,0:T(8,128)(2,1)} %pad_maximum_fusion.3.g_ref, bf16[64,64,640]{2,1,0:T(8,128)(2,1)} %get-tuple-element.10.yt_ref), custom_call_target="tpu_custom_call" | custom-call | flops 7046430720 | bytes 12124160 | tf_op jit(solution)/shard_map/occ/pallas_call | solution.py:135
  104.7 1.9 collective-permute-start.8
  106.6 4.3 %collective-permute-start.15 = (bf16[1536,640]{1,0:T(8,128)(2,1)S(1)}, bf16[1536,640]{1,0:T(8,128)(2,1)S(1)}, u32[]{:S(2)}, u32[]{:S(2)}) collective-permute-start(bf16[1536,640]{1,0:T(8,128)(2,1)S(1)} %bitcast.92), channel_id=1, source_target_pairs={{0,1},{1,2},{2,3},{8,9},{9,10},{10,11},{16,17},{17,18},{18,19},{24... | collective-permute-start | bytes 5898248 | tf_op jit(solution)/shard_map/ppermute | solution.py:400
  110.9 1.4 collective-permute-start.6
  112.3 3.0 %slice_multiply_fusion = bf16[640,1536]{1,0:T(8,128)(2,1)} fusion(bf16[640,4096]{1,0:T(8,128)(2,1)} %bitcast.89, bf16[]{:T(256)} %bitcast.10), kind=kLoop, calls=%fused_computation.4 | loop fusion | flops 983040 | bytes 3932162 | tf_op jit(solution)/shard_map/mul | solution.py:387
  115.3 4.3 %collective-permute-start.2 = (bf16[640,1536]{1,0:T(8,128)(2,1)}, bf16[640,1536]{1,0:T(8,128)(2,1)}, u32[]{:S(2)}, u32[]{:S(2)}) collective-permute-start(bf16[640,1536]{1,0:T(8,128)(2,1)} %slice_multiply_fusion), channel_id=1, source_target_pairs={{0,1},{1,2},{2,3},{4,5},{5,6},{6,7},{8,9},{9,10},{10,11},{12,13},{... | collective-permute-start | bytes 5898248 | tf_op jit(solution)/shard_map/ppermute | solution.py:413
  119.7 6.5 %collective-permute-done.10.vc_ref = bf16[1280,640]{1,0:T(8,128)(2,1)} collective-permute-done((bf16[1280,640]{1,0:T(8,128)(2,1)}, bf16[1280,640]{1,0:T(8,128)(2,1)}, u32[]{:S(2)}, u32[]{:S(2)}) %collective-permute-start.10) | collective-permute-done | bytes 1638432 | tf_op jit(solution)/shard_map/ppermute | solution.py:401
  126.2 1.3 collective-permute-start.17
  127.5 3.5 %collective-permute-start.7 = (bf16[640,1280]{1,0:T(8,128)(2,1)}, bf16[640,1280]{1,0:T(8,128)(2,1)}, u32[]{:S(2)}, u32[]{:S(2)}) collective-permute-start(bf16[640,1280]{1,0:T(8,128)(2,1)} %collective-permute-done.4.r2_ref), channel_id=1, source_target_pairs={{0,8},{8,16},{16,24},{1,9},{9,17},{17,25},{2,10},{10,18},{18,26},{... | collective-permute-start | bytes 4915208 | tf_op jit(solution)/shard_map/ppermute | solution.py:417
  131.0 1.3 copy-done.6
  132.3 1.8 collective-permute-start.11
  134.9 6.4 %vir.2 = bf16[1536,640]{1,0:T(8,128)(2,1)} custom-call(bf16[2,64,64]{2,1,0:T(8,128)(2,1)} %copy.9.fv_ref.f_ref, bf16[1536,640]{1,0:T(8,128)(2,1)} %bitcast.91, bf16[1536,640]{1,0:T(8,128)(2,1)} %copy-done.6), custom_call_target="tpu_custom_call" | custom-call | flops 1006632960 | bytes 5898240 | tf_op jit(solution)/shard_map/vir/pallas_call | solution.py:159
  141.2 1.3 collective-permute-start.14
  142.5 1.3 collective-permute-start.16
  144.4 5.7 %vir.3 = bf16[1280,640]{1,0:T(8,128)(2,1)} custom-call(bf16[2,64,64]{2,1,0:T(8,128)(2,1)} %pad_maximum_fusion.1.fw_ref.f_ref.refs_1_, bf16[1280,640]{1,0:T(8,128)(2,1)} %bitcast.93, bf16[1280,640]{1,0:T(8,128)(2,1)} %collective-permute-done.17.shifted_ref), custom_call_target="tpu_custom_call" | custom-call | flops 838860800 | bytes 4915200 | tf_op jit(solution)/shard_map/vir/pallas_call | solution.py:159
  150.2 16.0 %collective-permute-done.7.raw_e_ref = bf16[640,1280]{1,0:T(8,128)(2,1)} collective-permute-done((bf16[640,1280]{1,0:T(8,128)(2,1)}, bf16[640,1280]{1,0:T(8,128)(2,1)}, u32[]{:S(2)}, u32[]{:S(2)}) %collective-permute-start.7) | collective-permute-done | bytes 1638432 | tf_op jit(solution)/shard_map/ppermute | solution.py:417
  166.1 2.5 collective-permute-start.18
  169.2 22.3 %diag_product.1 = f32[640,640]{1,0:T(8,128)} custom-call(s32[1]{0:T(128)} %bitcast.77.refs_0_, bf16[3,64,64]{2,1,0:T(8,128)(2,1)} %pad_maximum_fusion.refs_1_, bf16[640,4096]{1,0:T(8,128)(2,1)} %bitcast.90, bf16[4096,640]{1,0:T(8,128)(2,1)} %bitcast.98, bf16[640,1280]{1,0:T(8,128)(2,1)} %collective-permute-done.1.refs_4_, ...), custom_call_target="tpu_custom_call" | custom-call | flops 9395240960 | bytes 15728640 | tf_op jit(solution)/shard_map/diag_product/pallas_call | solution.py:209
  191.6 12.9 %early_edges.1 = (f32[640,640]{1,0:T(8,128)}, f32[640,640]{1,0:T(8,128)}) custom-call(s32[1]{0:T(128)} %bitcast.13.parity_ref.refs_0_, bf16[2,64,64]{2,1,0:T(8,128)(2,1)} %pad_maximum_fusion.1.fw_ref.f_ref.refs_1_, bf16[2,64,64]{2,1,0:T(8,128)(2,1)} %copy.9.fv_ref.f_ref, bf16[640,1280]{1,0:T(8,128)(2,1)} %collective-permute-done.4.r2_ref, ...), custom_call_target="tpu_custom_call" | custom-call | flops 3774873600 | bytes 9830400 | tf_op jit(solution)/shard_map/early_edges/pallas_call | solution.py:268
  204.5 1.3 fusion.7
  205.8 18.7 %collective-permute-start.12 = (bf16[2,2,160,640]{3,2,1,0:T(8,128)(2,1)S(1)}, bf16[2,2,160,640]{3,2,1,0:T(8,128)(2,1)}, u32[]{:S(2)}, u32[]{:S(2)}) collective-permute-start(bf16[2,2,160,640]{3,2,1,0:T(8,128)(2,1)S(1)} %fusion.7), channel_id=1, source_target_pairs={{0,1},{1,0},{2,3},{3,2},{4,5},{5,4},{6,7},{7,6},{8,9},{9,8},{10,11... | collective-permute-start | bytes 2457608 | tf_op jit(solution)/shard_map/ppermute | solution.py:349
  224.5 1.3 copy-done.7
  225.7 12.0 %last_edges.1 = f32[2,640,640]{2,1,0:T(8,128)} custom-call(s32[1]{0:T(128)} %bitcast.13.parity_ref.refs_0_, bf16[2,64,64]{2,1,0:T(8,128)(2,1)} %pad_maximum_fusion.1.fw_ref.f_ref.refs_1_, f32[640,640]{1,0:T(8,128)} %get-tuple-element.15.refs_2_, bf16[640,1536]{1,0:T(8,128)(2,1)} %copy-done.7, bf16[2816,640]{1,0:T(8,128)(2,1)} %bitcast.80, ...), custom_call_target="tpu_custom_call" | custom-call | flops 3523215360 | bytes 9830400 | tf_op jit(solution)/shard_map/last_edges/pallas_call | solution.py:318
  237.8 2.4 fusion.6
  240.2 1.9 fusion.5
  242.2 1.2 copy-done.3
  243.4 0.8 dynamic-slice_convert_fusion.1
  244.8 1.4 bitcast_add_fusion
  246.3 1.4 collective-permute-start.20
  247.7 9.0 %collective-permute-done.13 = bf16[2,1,160,640]{3,2,1,0:T(8,128)(2,1)} collective-permute-done((bf16[2,1,160,640]{3,2,1,0:T(8,128)(2,1)}, bf16[2,1,160,640]{3,2,1,0:T(8,128)(2,1)}, u32[]{:S(2)}, u32[]{:S(2)}) %collective-permute-start.13) | collective-permute-done | bytes 409632 | tf_op jit(solution)/shard_map/ppermute | solution.py:349
  256.7 1.1 convert_add_fusion.1
  257.9 1.3 collective-permute-start.21
  259.2 5.8 %collective-permute-done.20 = bf16[2,1,160,640]{3,2,1,0:T(8,128)(2,1)S(1)} collective-permute-done((bf16[2,1,160,640]{3,2,1,0:T(8,128)(2,1)S(1)}, bf16[2,1,160,640]{3,2,1,0:T(8,128)(2,1)S(1)}, u32[]{:S(2)}, u32[]{:S(2)}) %collective-permute-start.20) | collective-permute-done | bytes 409632 | tf_op jit(solution)/shard_map/ppermute | solution.py:349
  265.1 1.0 collective-permute-done.21
  267.0 5.0 %collective-permute-done.22 = bf16[160,640]{1,0:T(8,128)(2,1)S(1)} collective-permute-done((bf16[160,640]{1,0:T(8,128)(2,1)S(1)}, bf16[160,640]{1,0:T(8,128)(2,1)S(1)}, u32[]{:S(2)}, u32[]{:S(2)}) %collective-permute-start.22) | collective-permute-done | bytes 204832 | tf_op jit(solution)/shard_map/ppermute | solution.py:427
  271.9 0.8 fusion.11
  (58 shorter events, 6.1 us)
Async XLA Ops:
  1.3 6.9 %copy-start.11 = (bf16[1,2,64,64]{3,2,1,0:T(8,128)(2,1)S(1)}, bf16[1,2,64,64]{3,2,1,0:T(8,128)(2,1)}, u32[]{:S(2)}) copy-start(bf16[1,2,64,64]{3,2,1,0:T(8,128)(2,1)} %param.5) | copy-start | bytes 49156
  4.6 77.1 %copy-start.2 = (bf16[640,1280]{1,0:T(8,128)(2,1)}, bf16[640,1280]{1,0:T(8,128)(2,1)S(1)}, u32[]{:S(2)}) copy-start(bf16[640,1280]{1,0:T(8,128)(2,1)S(1)} %get-tuple-element.18.refs_7_) | copy-start | bytes 4915204
  4.6 100.1 %collective-permute-start.1 = (bf16[640,1280]{1,0:T(8,128)(2,1)}, bf16[640,1280]{1,0:T(8,128)(2,1)}, u32[]{:S(2)}, u32[]{:S(2)}) collective-permute-start(bf16[640,1280]{1,0:T(8,128)(2,1)} %get-tuple-element.19), channel_id=1, source_target_pairs={{0,1},{1,2},{2,3},{4,5},{5,6},{6,7},{8,9},{9,10},{10,11},{12,13},{... | collective-permute-start | bytes 4915208 | tf_op jit(solution)/shard_map/ppermute | solution.py:412
  38.8 5.5 %copy-start.10 = (bf16[1,2,64,64]{3,2,1,0:T(8,128)(2,1)S(1)}, bf16[1,2,64,64]{3,2,1,0:T(8,128)(2,1)}, u32[]{:S(2)}) copy-start(bf16[1,2,64,64]{3,2,1,0:T(8,128)(2,1)} %param.6) | copy-start | bytes 49156
  40.4 66.2 %collective-permute-start.3 = (bf16[1280,640]{1,0:T(8,128)(2,1)S(1)}, bf16[1280,640]{1,0:T(8,128)(2,1)}, u32[]{:S(2)}, u32[]{:S(2)}) collective-permute-start(bf16[1280,640]{1,0:T(8,128)(2,1)S(1)} %bitcast.95), channel_id=1, source_target_pairs={{1,0},{2,1},{3,2},{5,4},{6,5},{7,6},{9,8},{10,9},{11,10},{13,12},{... | collective-permute-start | bytes 4915208 | tf_op jit(solution)/shard_map/ppermute | solution.py:411
  41.7 69.2 %collective-permute-start.4 = (bf16[640,1280]{1,0:T(8,128)(2,1)}, bf16[640,1280]{1,0:T(8,128)(2,1)}, u32[]{:S(2)}, u32[]{:S(2)}) collective-permute-start(bf16[640,1280]{1,0:T(8,128)(2,1)} %get-tuple-element.19), channel_id=1, source_target_pairs={{4,0},{12,8},{20,16},{28,24},{5,1},{13,9},{21,17},{29,25},{6,2},{1... | collective-permute-start | bytes 4915208 | tf_op jit(solution)/shard_map/ppermute | solution.py:384
  43.0 38.7 %collective-permute-start.5 = (bf16[64,64]{0,1:T(8,128)(2,1)S(1)}, bf16[64,64]{0,1:T(8,128)(2,1)S(1)}, u32[]{:S(2)}, u32[]{:S(2)}) collective-permute-start(bf16[64,64]{0,1:T(8,128)(2,1)S(1)} %bitcast.100), channel_id=1, source_target_pairs={{4,0},{8,4},{12,8},{16,12},{20,16},{24,20},{28,24},{5,1},{9,5},{13... | collective-permute-start | bytes 24584 | tf_op jit(solution)/shard_map/ppermute | solution.py:390
  44.3 40.2 %collective-permute-start = (bf16[64,64]{1,0:T(8,128)(2,1)S(1)}, bf16[64,64]{1,0:T(8,128)(2,1)S(1)}, u32[]{:S(2)}, u32[]{:S(2)}) collective-permute-start(bf16[64,64]{1,0:T(8,128)(2,1)S(1)} %get-tuple-element.23), channel_id=1, source_target_pairs={{1,0},{2,1},{3,2},{5,4},{6,5},{7,6},{9,8},{10,9},{11,10},{13,12},{... | collective-permute-start | bytes 24584 | tf_op jit(solution)/shard_map/ppermute | solution.py:391
  81.7 33.6 %collective-permute-start.9 = (bf16[640,1280]{1,0:T(8,128)(2,1)S(1)}, bf16[640,1280]{1,0:T(8,128)(2,1)}, u32[]{:S(2)}, u32[]{:S(2)}) collective-permute-start(bf16[640,1280]{1,0:T(8,128)(2,1)S(1)} %get-tuple-element.18.refs_7_), channel_id=1, source_target_pairs={{4,12},{12,20},{20,28},{5,13},{13,21},{21,29},{6,14},{14,22},{22,3... | collective-permute-start | bytes 4915208 | tf_op jit(solution)/shard_map/ppermute | solution.py:386
  84.5 22.1 %copy-start.5 = (bf16[24,64,640]{2,1,0:T(8,128)(2,1)S(1)}, bf16[24,64,640]{2,1,0:T(8,128)(2,1)}, u32[]{:S(2)}) copy-start(bf16[24,64,640]{2,1,0:T(8,128)(2,1)} %get-tuple-element.16) | copy-start | bytes 5898244
  84.5 41.7 %collective-permute-start.10 = (bf16[1280,640]{1,0:T(8,128)(2,1)}, bf16[1280,640]{1,0:T(8,128)(2,1)}, u32[]{:S(2)}, u32[]{:S(2)}) collective-permute-start(bf16[1280,640]{1,0:T(8,128)(2,1)} %bitcast.105), channel_id=1, source_target_pairs={{0,4},{8,12},{16,20},{24,28},{1,5},{9,13},{17,21},{25,29},{2,6},{1... | collective-permute-start | bytes 4915208 | tf_op jit(solution)/shard_map/ppermute | solution.py:401
  104.7 22.8 %collective-permute-start.8 = (bf16[1280,640]{1,0:T(8,128)(2,1)}, bf16[1280,640]{1,0:T(8,128)(2,1)S(1)}, u32[]{:S(2)}, u32[]{:S(2)}) collective-permute-start(bf16[1280,640]{1,0:T(8,128)(2,1)} %bitcast.96), channel_id=1, source_target_pairs={{0,1},{1,2},{2,3},{8,9},{9,10},{10,11},{16,17},{17,18},{18,19},{24... | collective-permute-start | bytes 4915208 | tf_op jit(solution)/shard_map/ppermute | solution.py:408
  106.6 24.4 %collective-permute-start.15 = (bf16[1536,640]{1,0:T(8,128)(2,1)S(1)}, bf16[1536,640]{1,0:T(8,128)(2,1)S(1)}, u32[]{:S(2)}, u32[]{:S(2)}) collective-permute-start(bf16[1536,640]{1,0:T(8,128)(2,1)S(1)} %bitcast.92), channel_id=1, source_target_pairs={{0,1},{1,2},{2,3},{8,9},{9,10},{10,11},{16,17},{17,18},{18,19},{24... | collective-permute-start | bytes 5898248 | tf_op jit(solution)/shard_map/ppermute | solution.py:400
  110.9 15.3 %copy-start.8 = (bf16[20,64,640]{2,1,0:T(8,128)(2,1)S(1)}, bf16[20,64,640]{2,1,0:T(8,128)(2,1)}, u32[]{:S(2)}) copy-start(bf16[20,64,640]{2,1,0:T(8,128)(2,1)} %get-tuple-element.17) | copy-start | bytes 4915204
  110.9 80.7 %collective-permute-start.6 = (bf16[2816,640]{1,0:T(8,128)(2,1)}, bf16[2816,640]{1,0:T(8,128)(2,1)}, u32[]{:S(2)}, u32[]{:S(2)}) collective-permute-start(bf16[2816,640]{1,0:T(8,128)(2,1)} %bitcast.78), channel_id=1, source_target_pairs={{1,0},{2,1},{3,2},{9,8},{10,9},{11,10},{17,16},{18,17},{19,18},{25... | collective-permute-start | bytes 10813448 | tf_op jit(solution)/shard_map/ppermute | solution.py:407
  115.3 27.2 %collective-permute-start.2 = (bf16[640,1536]{1,0:T(8,128)(2,1)}, bf16[640,1536]{1,0:T(8,128)(2,1)}, u32[]{:S(2)}, u32[]{:S(2)}) collective-permute-start(bf16[640,1536]{1,0:T(8,128)(2,1)} %slice_multiply_fusion), channel_id=1, source_target_pairs={{0,1},{1,2},{2,3},{4,5},{5,6},{6,7},{8,9},{9,10},{10,11},{12,13},{... | collective-permute-start | bytes 5898248 | tf_op jit(solution)/shard_map/ppermute | solution.py:413
  126.2 15.0 %collective-permute-start.17 = (bf16[1280,640]{1,0:T(8,128)(2,1)S(1)}, bf16[1280,640]{1,0:T(8,128)(2,1)}, u32[]{:S(2)}, u32[]{:S(2)}) collective-permute-start(bf16[1280,640]{1,0:T(8,128)(2,1)S(1)} %bitcast.94), channel_id=1, source_target_pairs={{1,0},{2,1},{3,2},{9,8},{10,9},{11,10},{17,16},{18,17},{19,18},{25... | collective-permute-start | bytes 4915208 | tf_op jit(solution)/shard_map/ppermute | solution.py:406
  127.5 6.6 %copy-start.9 = (bf16[1280,640]{1,0:T(8,128)(2,1)}, bf16[1280,640]{1,0:T(8,128)(2,1)S(1)}, u32[]{:S(2)}) copy-start(bf16[1280,640]{1,0:T(8,128)(2,1)S(1)} %collective-permute-done.8.vs_ref) | copy-start | bytes 4915204
  127.5 38.6 %collective-permute-start.7 = (bf16[640,1280]{1,0:T(8,128)(2,1)}, bf16[640,1280]{1,0:T(8,128)(2,1)}, u32[]{:S(2)}, u32[]{:S(2)}) collective-permute-start(bf16[640,1280]{1,0:T(8,128)(2,1)} %collective-permute-done.4.r2_ref), channel_id=1, source_target_pairs={{0,8},{8,16},{16,24},{1,9},{9,17},{17,25},{2,10},{10,18},{18,26},{... | collective-permute-start | bytes 4915208 | tf_op jit(solution)/shard_map/ppermute | solution.py:417
  131.0 1.3 copy-start.6
  132.3 59.3 %collective-permute-start.11 = (bf16[1280,640]{1,0:T(8,128)(2,1)}, bf16[1280,640]{1,0:T(8,128)(2,1)}, u32[]{:S(2)}, u32[]{:S(2)}) collective-permute-start(bf16[1280,640]{1,0:T(8,128)(2,1)} %collective-permute-done.10.vc_ref), channel_id=1, source_target_pairs={{4,5},{5,6},{6,7},{12,13},{13,14},{14,15},{20,21},{21,22},{22,23},... | collective-permute-start | bytes 4915208 | tf_op jit(solution)/shard_map/ppermute | solution.py:418
  141.2 83.2 %collective-permute-start.14 = (bf16[640,1536]{1,0:T(8,128)(2,1)}, bf16[640,1536]{1,0:T(8,128)(2,1)S(1)}, u32[]{:S(2)}, u32[]{:S(2)}) collective-permute-start(bf16[640,1536]{1,0:T(8,128)(2,1)} %slice_multiply_fusion), channel_id=1, source_target_pairs={{4,0},{12,8},{20,16},{28,24},{5,1},{13,9},{21,17},{29,25},{6,2},{1... | collective-permute-start | bytes 5898248 | tf_op jit(solution)/shard_map/ppermute | solution.py:388
  142.5 81.9 %collective-permute-start.16 = (bf16[1536,640]{1,0:T(8,128)(2,1)}, bf16[1536,640]{1,0:T(8,128)(2,1)}, u32[]{:S(2)}, u32[]{:S(2)}) collective-permute-start(bf16[1536,640]{1,0:T(8,128)(2,1)} %vir.2), channel_id=1, source_target_pairs={{8,0},{16,8},{24,16},{9,1},{17,9},{25,17},{10,2},{18,10},{26,18},{... | collective-permute-start | bytes 5898248 | tf_op jit(solution)/shard_map/ppermute | solution.py:415
  166.1 58.3 %collective-permute-start.18 = (bf16[1280,640]{1,0:T(8,128)(2,1)}, bf16[1280,640]{1,0:T(8,128)(2,1)}, u32[]{:S(2)}, u32[]{:S(2)}) collective-permute-start(bf16[1280,640]{1,0:T(8,128)(2,1)} %vir.3), channel_id=1, source_target_pairs={{0,4},{8,12},{16,20},{24,28},{1,5},{9,13},{17,21},{25,29},{2,6},{1... | collective-permute-start | bytes 4915208 | tf_op jit(solution)/shard_map/ppermute | solution.py:416
  191.6 12.9 %copy-start.1 = (f32[640,640]{1,0:T(8,128)S(1)}, f32[640,640]{1,0:T(8,128)}, u32[]{:S(2)}) copy-start(f32[640,640]{1,0:T(8,128)} %diag_product.1) | copy-start | bytes 4915204
  205.8 34.5 %collective-permute-start.12 = (bf16[2,2,160,640]{3,2,1,0:T(8,128)(2,1)S(1)}, bf16[2,2,160,640]{3,2,1,0:T(8,128)(2,1)}, u32[]{:S(2)}, u32[]{:S(2)}) collective-permute-start(bf16[2,2,160,640]{3,2,1,0:T(8,128)(2,1)S(1)} %fusion.7), channel_id=1, source_target_pairs={{0,1},{1,0},{2,3},{3,2},{4,5},{5,4},{6,7},{7,6},{8,9},{9,8},{10,11... | collective-permute-start | bytes 2457608 | tf_op jit(solution)/shard_map/ppermute | solution.py:349
  224.5 1.3 copy-start.7
  240.2 4.6 %collective-permute-start.19 = (bf16[2,2,160,640]{3,2,1,0:T(8,128)(2,1)}, bf16[2,2,160,640]{3,2,1,0:T(8,128)(2,1)}, u32[]{:S(2)}, u32[]{:S(2)}) collective-permute-start(bf16[2,2,160,640]{3,2,1,0:T(8,128)(2,1)} %fusion.6), channel_id=1, source_target_pairs={{0,1},{1,0},{2,3},{3,2},{4,5},{5,4},{6,7},{7,6},{8,9},{9,8},{10,11... | collective-permute-start | bytes 2457608 | tf_op jit(solution)/shard_map/ppermute | solution.py:349
  240.2 4.6 %copy-start = (f32[2,640,640]{2,1,0:T(8,128)S(1)}, f32[2,640,640]{2,1,0:T(8,128)}, u32[]{:S(2)}) copy-start(f32[2,640,640]{2,1,0:T(8,128)} %last_edges.1) | copy-start | bytes 9830404
  242.2 1.2 copy-start.3
  244.2 12.6 %collective-permute-start.13 = (bf16[2,1,160,640]{3,2,1,0:T(8,128)(2,1)}, bf16[2,1,160,640]{3,2,1,0:T(8,128)(2,1)}, u32[]{:S(2)}, u32[]{:S(2)}) collective-permute-start(bf16[2,1,160,640]{3,2,1,0:T(8,128)(2,1)} %dynamic-slice_convert_fusion.1), channel_id=1, source_target_pairs={{0,2},{1,3},{2,0},{3,1},{4,6},{5,7},{6,4},{7,5},{8,10},{9,11},{10,... | collective-permute-start | bytes 1228808 | tf_op jit(solution)/shard_map/ppermute | solution.py:349
  244.8 11.9 %copy-start.4 = (f32[2,2,160,640]{3,2,1,0:T(8,128)S(1)}, f32[2,2,160,640]{3,2,1,0:T(8,128)}, u32[]{:S(2)}) copy-start(f32[2,2,160,640]{3,2,1,0:T(8,128)} %copy-done.3) | copy-start | bytes 4915204
  246.3 18.7 %collective-permute-start.20 = (bf16[2,1,160,640]{3,2,1,0:T(8,128)(2,1)S(1)}, bf16[2,1,160,640]{3,2,1,0:T(8,128)(2,1)S(1)}, u32[]{:S(2)}, u32[]{:S(2)}) collective-permute-start(bf16[2,1,160,640]{3,2,1,0:T(8,128)(2,1)S(1)} %dynamic-slice_convert_fusion), channel_id=1, source_target_pairs={{0,2},{1,3},{2,0},{3,1},{4,6},{5,7},{6,4},{7,5},{8,10},{9,11},{10,... | collective-permute-start | bytes 1228808 | tf_op jit(solution)/shard_map/ppermute | solution.py:349
  257.9 8.2 %collective-permute-start.21 = (bf16[160,640]{1,0:T(8,128)(2,1)S(1)}, bf16[160,640]{1,0:T(8,128)(2,1)S(1)}, u32[]{:S(2)}, u32[]{:S(2)}) collective-permute-start(bf16[160,640]{1,0:T(8,128)(2,1)S(1)} %fusion.12), channel_id=1, source_target_pairs={{8,0},{12,4},{16,8},{20,12},{24,16},{28,20},{9,1},{13,5},{17,9},{2... | collective-permute-start | bytes 614408 | tf_op jit(solution)/shard_map/ppermute | solution.py:424
  266.1 5.8 %collective-permute-start.22 = (bf16[160,640]{1,0:T(8,128)(2,1)S(1)}, bf16[160,640]{1,0:T(8,128)(2,1)S(1)}, u32[]{:S(2)}, u32[]{:S(2)}) collective-permute-start(bf16[160,640]{1,0:T(8,128)(2,1)S(1)} %fusion.9), channel_id=1, source_target_pairs={{0,4},{4,0},{8,12},{12,8},{16,20},{20,16},{24,28},{28,24},{1,5},{5... | collective-permute-start | bytes 614408 | tf_op jit(solution)/shard_map/ppermute | solution.py:427

commit v2 on v0

v2 whole, which is shorter than its diff:
```python
import jax
import jax.numpy as jnp
from jax import lax
from jax.experimental import pallas as pl
from jax.experimental.pallas import tpu as pltpu
from jax.sharding import PartitionSpec as P

BF = jnp.bfloat16
F32 = jnp.float32
VMEM_BYTES = 48 * 1024 * 1024
SPAN = 256
SUBLANES = 8


def dot(a, b, dims=((1,), (0,))):
    return lax.dot_general(a, b, (dims, ((), ())), preferred_element_type=F32)


def iota(shape, axis):
    return lax.broadcasted_iota(jnp.int32, shape, axis)


def spread(g, group):
    m, k = g.shape
    pick_row = (iota((m * group, 1), 0) // group == iota((1, m), 1)).astype(BF)
    pick_col = (iota((k, 1), 0) == iota((1, k * group), 1) // group).astype(BF)
    full = dot(dot(pick_row, g).astype(BF), pick_col)
    same = iota((m * group, 1), 0) % group == iota((1, k * group), 1) % group
    return jnp.where(same, full, 0.0).astype(BF)


def repeated(g, count):
    t = g.shape[0]
    n = t * count
    pick = (iota((n, 1), 0) % t == iota((1, t), 1)).astype(BF)
    full = dot(dot(pick, g).astype(BF), pick, ((1,), (1,)))
    same = iota((n, 1), 0) // t == iota((1, n), 1) // t
    return jnp.where(same, full, 0.0).astype(BF)


def params():
    return pltpu.CompilerParams(vmem_limit_bytes=VMEM_BYTES)


def cost(flops, size):
    return pl.CostEstimate(flops=flops, bytes_accessed=size, transcendentals=0)


def occ_kernel(live_ref, g_ref, y_ref, out_ref, rows_ref, yt_ref, sems, *, slices):
    width, size = rows_ref.shape
    m, tile = g_ref.shape
    per = SPAN // tile
    copies = []
    to = 0
    for i, (start, count) in enumerate(slices):
        copies.append(
            pltpu.make_async_copy(y_ref.at[pl.ds(start, count)], rows_ref.at[pl.ds(to, count)], sems.at[i])
        )
        to += count
    for copy in copies:
        copy.start()
    kron = spread(g_ref[...], SUBLANES)
    live = live_ref[0].astype(F32).astype(BF)
    for copy in copies:
        copy.wait()
    for j in range(size // SPAN):
        part = rows_ref[:, j * SPAN : (j + 1) * SPAN] * live
        yt_ref[j * per : (j + 1) * per] = part.T.reshape(per, tile, width)
    pair = 2 * SUBLANES
    for s in range(tile // pair):
        part = yt_ref[:, s * pair : (s + 1) * pair, :].astype(F32)
        low, high = (
            part[:, k : k + SUBLANES].reshape(tile * SUBLANES, width).astype(BF) for k in (0, SUBLANES)
        )
        low, high = (dot(kron, x).reshape(m, SUBLANES, width) for x in (low, high))
        out_ref[:, s * pair : (s + 1) * pair, :] = jnp.concatenate([low, high], axis=1).astype(BF)


def occ(live, mat, y, slices):
    m, tile = mat.shape
    size = y.shape[1]
    width = sum(count for _, count in slices)
    out = pl.pallas_call(
        lambda *refs: occ_kernel(*refs, slices=slices),
        in_specs=[
            pl.BlockSpec(memory_space=pltpu.SMEM),
            pl.BlockSpec(memory_space=pltpu.VMEM),
            pl.BlockSpec(memory_space=pl.ANY),
        ],
        out_specs=pl.BlockSpec(memory_space=pltpu.VMEM),
        out_shape=jax.ShapeDtypeStruct((m, tile, width), BF),
        scratch_shapes=[
            pltpu.VMEM((width, size), BF),
            pltpu.VMEM((tile, tile, width), BF),
            pltpu.SemaphoreType.DMA((len(slices),)),
        ],
        compiler_params=params(),
        cost_estimate=cost(2 * width * size * m * SUBLANES, 4 * width * size),
        name="occ",
    )(live, mat, y)
    return out.reshape(m * tile, width)


def vir_kernel(live_ref, g_ref, y_ref, *rest):
    *added, out_ref, kron_ref = rest

    @pl.when(pl.program_id(0) == 0)
    def _():
        scale = live_ref[0].astype(F32)
        kron_ref[...] = (repeated(g_ref[...], SPAN // g_ref.shape[0]).astype(F32) * scale).astype(BF)

    for j in range(y_ref.shape[1] // SPAN):
        at = slice(j * SPAN, (j + 1) * SPAN)
        got = dot(y_ref[:, at], kron_ref[...])
        for ref in added:
            got = got + ref[:, at].astype(F32)
        out_ref[:, at] = got.astype(BF)


def vir(live, mat, y, added=()):
    aux, size = y.shape
    span = 4 * SPAN if size % (4 * SPAN) == 0 else SPAN
    block = pl.BlockSpec((aux, span), lambda i: (0, i))
    return pl.pallas_call(
        vir_kernel,
        grid=(size // span,),
        in_specs=[
            pl.BlockSpec(memory_space=pltpu.SMEM),
            pl.BlockSpec(mat.shape, lambda i: (0, 0)),
            block,
            *(block for _ in added),
        ],
        out_specs=block,
        out_shape=jax.ShapeDtypeStruct((aux, size), BF),
        scratch_shapes=[pltpu.VMEM((SPAN, SPAN), BF)],
        compiler_params=params(),
        cost_estimate=cost(2 * aux * size * SPAN, 2 * (2 + len(added)) * aux * size),
        name="vir",
    )(live, mat, y, *added)


def product_kernel(z_ref, x_ref, out_ref, acc_ref):
    step = pl.program_id(0)

    @pl.when(step == 0)
    def _():
        acc_ref[...] = dot(z_ref[...], x_ref[...])

    @pl.when(step > 0)
    def _():
        acc_ref[...] += dot(z_ref[...], x_ref[...])

    @pl.when(step == pl.num_programs(0) - 1)
    def _():
        out_ref[...] = acc_ref[...].T


def product(z, x):
    aux, size = z.shape
    width = x.shape[1]
    span = 4 * SPAN if size % (4 * SPAN) == 0 else SPAN
    return pl.pallas_call(
        product_kernel,
        grid=(size // span,),
        in_specs=[pl.BlockSpec((aux, span), lambda i: (0, i)), pl.BlockSpec((span, width), lambda i: (i, 0))],
        out_specs=pl.BlockSpec((width, aux), lambda i: (0, 0)),
        out_shape=jax.ShapeDtypeStruct((width, aux), F32),
        scratch_shapes=[pltpu.VMEM((aux, width), F32)],
        compiler_params=params(),
        cost_estimate=cost(2 * aux * size * width, 2 * size * (aux + width)),
        name="product",
    )(z, x)


def scattered(value, axis):
    size = lax.axis_size(axis)
    if size & (size - 1):
        return lax.psum_scatter(value.astype(BF), axis, scatter_dimension=0, tiled=True).astype(F32)
    me = lax.axis_index(axis)
    blocks = value.reshape(size, value.shape[0] // size, value.shape[1])
    reach = 1
    while reach < size:
        bit = (me // reach) % 2
        pairs = blocks.reshape(blocks.shape[0] // 2, 2, *blocks.shape[1:])
        kept = lax.dynamic_index_in_dim(pairs, bit, 1, keepdims=False)
        given = lax.dynamic_index_in_dim(pairs, 1 - bit, 1, keepdims=False).astype(BF)
        got = lax.ppermute(given, axis, [(i, i ^ reach) for i in range(size)])
        blocks = kept + got.astype(F32)
        reach *= 2
    return blocks[0]


def chunks_of(aux, owners):
    each = aux // owners
    small = 128 // owners
    if owners * small == 128 and small % 16 == 0 and each % 16 == 0 and each > 2 * small:
        cuts = [0, small, each - small, each]
        return [[(j * each + a, b - a) for j in range(owners)] for a, b in zip(cuts, cuts[1:])]
    return [[(0, aux)]]


def body(three_centre, green_occ, green_vir, pair_live):
    rows, cols = lax.axis_size("row"), lax.axis_size("col")
    y = three_centre[0, 0]
    aux = y.shape[0]
    live = pair_live[0]
    up_row = [(i, i - 1) for i in range(1, rows)]
    up_col = [(i, i - 1) for i in range(1, cols)]
    to_own, to_lower = green_occ[0, 0].T, green_occ[0, 1].T

    halves = [occ(live, to_lower, y, part) for part in chunks_of(aux, cols)]
    above = [lax.ppermute(half, "row", up_row) for half in halves]
    shifted = lax.ppermute(vir(live, green_vir[0, 1].T, y), "col", up_col)
    own = occ(live, to_own, y, [(0, aux)])
    z = vir(live, green_vir[0, 0].T, y, (shifted,))
    chi_d = scattered(product(z, own), "col")
    chi_n = jnp.concatenate([scattered(product(z, half), "col") for half in above])
    return chi_d[None], chi_n[None]


def solution(mesh):
    return jax.shard_map(
        body,
        mesh=mesh,
        in_specs=(
            P("row", "col", None, None),
            P("row", None, None, None),
            P("col", None, None, None),
            P("row", "col"),
        ),
        out_specs=(P("row", "col", None), P("row", "col", None)),
        check_vma=False,
    )
```

time: 224 us -> 155 us (0.69)
  waiting for transfers between devices: 125 us -> 42.7 us
  Pallas kernels: 0 us -> 54.8 us
  starting transfers between devices: 2.78 us -> 47.9 us
  local copies, waits for them, and re-layouts: 43.8 us -> 5.97 us
  matrix products: 33.6 us -> 0 us
  between operations: 14.7 us -> 1.61 us
    pallas_call x0 -> x10, Pallas kernels: none -> 54.8 us  [the longest x4 22.9 us: product(): pl.pallas_call(product_kernel, grid=(size // span,), in_specs=[pl.BlockSp...]
    ppermute x2 -> x12, waiting for transfers between devices: 95.2 us -> 42.7 us  [the longest x3 34.2 us: body(): above = [lax.ppermute(half, 'row', up_row) for half in halves]]
    ppermute x2 -> x12, starting transfers between devices: 2.74 us -> 47.9 us  [the longest x8 42.5 us: scattered(): got = lax.ppermute(given, axis, [(i, i ^ reach) for i in range(size)])]
    dot_general x3 -> x0, matrix products: 33.6 us -> none  [the longest x1 15.1 us: body(): jnp.einsum('pml,smn->spnl', blocks, green_occ[0], preferred_element_type=...]
    slice x5 -> x2, local copies, waits for them, and re-layouts: 33.6 us -> 0.74 us  [the longest x1 0.74 us: body(): shifted = lax.ppermute(vir(live, green_vir[0, 1].T, y), 'col', up_col)]
    reduce_scatter x1 -> x0, waiting for transfers between devices: 30.1 us -> none  [body(): lax.psum_scatter(partial_value.astype(jnp.bfloat16), 'col', scatter_dimen...]
    unnamed x13 -> x10, local copies, waits for them, and re-layouts: 10.3 us -> 5.01 us
    mul x1 -> x0, other arithmetic: 2.96 us -> none  [body(): blocks = (three_centre[0, 0] * live).reshape(aux_rows, tile, tile)]
  transfers between devices with their start and end apart: 3 -> 12, of which waited for: 2 -> 6; matrix products, arithmetic and copies ran while one was open for 9% -> 1% of each run, Pallas kernels for 0% -> 31%
where the time goes in v2:
time: 155 us
  Pallas kernels  54.8 us (35%)
  starting transfers between devices  47.9 us (31%)
  waiting for transfers between devices  42.7 us (28%)
  local copies, waits for them, and re-layouts  5.97 us (4%)
  other arithmetic  1.77 us (1%)
  between operations  1.61 us (1%)
    ppermute x8, starting transfers between devices, scattered(): got = lax.ppermute(given, axis, [(i, i ^ reach) for i in range(size)])  42.5 us
    ppermute x3, waiting for transfers between devices, body(): above = [lax.ppermute(half, 'row', up_row) for half in halves]  34.2 us
    pallas_call x4, Pallas kernels, product(): pl.pallas_call(product_kernel, grid=(size // span,), in_specs=[pl.BlockSp...  22.9 us
    pallas_call x4, Pallas kernels, occ(): pl.pallas_call(lambda *refs: occ_kernel(*refs, slices=slices), in_specs=[...  19.4 us
    pallas_call x2, Pallas kernels, vir(): pl.pallas_call(vir_kernel, grid=(size // span,), in_specs=[pl.BlockSpec(m...  12.5 us
    ppermute x8, waiting for transfers between devices, scattered(): got = lax.ppermute(given, axis, [(i, i ^ reach) for i in range(size)])  8.52 us
    unnamed x10, local copies, waits for them, and re-layouts  5.01 us
    ppermute x3, starting transfers between devices, body(): above = [lax.ppermute(half, 'row', up_row) for half in halves]  4.06 us
  transfers between devices with their start and end apart: 12, of which 6 were waited for; matrix products, arithmetic and copies ran while one was open for 1% of the time, Pallas kernels for 31%

profile of v2, /device:TPU:0, one launch (start us, length us, event | category | flops | bytes accessed | tf_op | source)
XLA Modules:
  0.0 154.7 jit_solution(5607920269086533890)
XLA Ops:
  1.3 0.7 fusion.5
  2.0 0.1 copy.15
  2.1 0.0 copy-start.2
  2.1 6.6 %vir.2 = bf16[640,4096]{1,0:T(8,128)(2,1)} custom-call(s32[1]{0:T(128)} %bitcast.62.live_ref, bf16[64,64]{1,0:T(8,128)(2,1)S(1)} %bitcast.82, bf16[640,4096]{1,0:T(8,128)(2,1)} %bitcast.84), custom_call_target="tpu_custom_call" | custom-call | flops 1342177280 | bytes 10485760 | tf_op jit(solution)/shard_map/vir/pallas_call | solution.py:124
  8.7 1.3 collective-permute-start
  10.0 0.1 copy.18
  10.1 5.0 %occ.6 = bf16[64,64,384]{2,1,0:T(8,128)(2,1)S(1)} custom-call(s32[1]{0:T(128)} %bitcast.66.refs_0_, bf16[64,64]{1,0:T(8,128)(2,1)S(1)} %bitcast.78, bf16[640,4096]{1,0:T(8,128)(2,1)} %bitcast.85), custom_call_target="tpu_custom_call" | custom-call | flops 1610612736 | bytes 6291456 | tf_op jit(solution)/shard_map/occ/pallas_call | solution.py:83
  15.2 1.3 collective-permute-start.6
  16.5 3.7 %occ.7 = bf16[64,64,128]{2,1,0:T(8,128)(2,1)} custom-call(s32[1]{0:T(128)} %bitcast.67.refs_0_, bf16[64,64]{1,0:T(8,128)(2,1)S(1)} %bitcast.79, bf16[640,4096]{1,0:T(8,128)(2,1)} %bitcast.86), custom_call_target="tpu_custom_call" | custom-call | flops 536870912 | bytes 2097152 | tf_op jit(solution)/shard_map/occ/pallas_call | solution.py:83
  20.1 1.3 collective-permute-start.9
  21.4 3.6 %occ.5 = bf16[64,64,128]{2,1,0:T(8,128)(2,1)} custom-call(s32[1]{0:T(128)} %bitcast.65.refs_0_, bf16[64,64]{1,0:T(8,128)(2,1)S(1)} %bitcast.80, bf16[640,4096]{1,0:T(8,128)(2,1)} %bitcast.87), custom_call_target="tpu_custom_call" | custom-call | flops 536870912 | bytes 2097152 | tf_op jit(solution)/shard_map/occ/pallas_call | solution.py:83
  25.1 1.5 collective-permute-start.3
  26.6 0.1 copy.16
  26.7 7.1 %occ.4 = bf16[64,64,640]{2,1,0:T(8,128)(2,1)S(1)} custom-call(s32[1]{0:T(128)} %bitcast.64.refs_0_, bf16[64,64]{1,0:T(8,128)(2,1)S(1)} %bitcast.81, bf16[640,4096]{1,0:T(8,128)(2,1)} %bitcast.88), custom_call_target="tpu_custom_call" | custom-call | flops 2684354560 | bytes 10485760 | tf_op jit(solution)/shard_map/occ/pallas_call | solution.py:83
  33.8 0.0 copy-start.1
  33.8 2.3 %copy-done.1 = bf16[64,64,640]{2,1,0:T(8,128)(2,1)} copy-done((bf16[64,64,640]{2,1,0:T(8,128)(2,1)}, bf16[64,64,640]{2,1,0:T(8,128)(2,1)S(1)}, u32[]{:S(2)}) %copy-start.1) | copy-done | bytes 5242904
  36.1 0.1 copy.14
  36.2 0.0 collective-permute-done.rest_0_
  36.2 5.9 %vir.3.z_ref = bf16[640,4096]{1,0:T(8,128)(2,1)S(1)} custom-call(s32[1]{0:T(128)} %bitcast.63.live_ref, bf16[64,64]{1,0:T(8,128)(2,1)S(1)} %bitcast.83, bf16[640,4096]{1,0:T(8,128)(2,1)} %bitcast.89, bf16[640,4096]{1,0:T(8,128)(2,1)} %collective-permute-done.rest_0_), custom_call_target="tpu_custom_call" | custom-call | flops 1342177280 | bytes 15728640 | tf_op jit(solution)/shard_map/vir/pallas_call | solution.py:124
  42.1 0.0 copy-start
  42.1 2.3 %copy-done = bf16[640,4096]{1,0:T(8,128)(2,1)} copy-done((bf16[640,4096]{1,0:T(8,128)(2,1)}, bf16[640,4096]{1,0:T(8,128)(2,1)S(1)}, u32[]{:S(2)}) %copy-start) | copy-done | bytes 5242904
  44.4 7.7 %product.4 = f32[640,640]{1,0:T(8,128)S(1)} custom-call(bf16[640,4096]{1,0:T(8,128)(2,1)} %copy-done, bf16[4096,640]{1,0:T(8,128)(2,1)} %bitcast.68), custom_call_target="tpu_custom_call" | custom-call | flops 3355443200 | bytes 10485760 | tf_op jit(solution)/shard_map/product/pallas_call | solution.py:162
  52.1 0.1 fusion
  52.2 35.5 %collective-permute-start.1 = (bf16[2,160,640]{2,1,0:T(8,128)(2,1)S(1)}, bf16[2,160,640]{2,1,0:T(8,128)(2,1)S(1)}, u32[]{:S(2)}, u32[]{:S(2)}) collective-permute-start(bf16[2,160,640]{2,1,0:T(8,128)(2,1)S(1)} %fusion), channel_id=1, source_target_pairs={{0,1},{1,0},{2,3},{3,2},{4,5},{5,4},{6,7},{7,6},{8,9},{9,8},{10,11... | collective-permute-start | bytes 1228808 | tf_op jit(solution)/shard_map/ppermute | solution.py:187
  87.7 23.5 %collective-permute-done.9.x_ref = bf16[4096,128]{1,0:T(8,128)(2,1)} collective-permute-done((bf16[4096,128]{1,0:T(8,128)(2,1)}, bf16[4096,128]{1,0:T(8,128)(2,1)}, u32[]{:S(2)}, u32[]{:S(2)}) %collective-permute-start.9) | collective-permute-done | bytes 1048608 | tf_op jit(solution)/shard_map/ppermute | solution.py:212
  111.2 4.5 %product.7 = f32[128,640]{1,0:T(8,128)S(1)} custom-call(bf16[640,4096]{1,0:T(8,128)(2,1)} %copy-done, bf16[4096,128]{1,0:T(8,128)(2,1)} %collective-permute-done.9.x_ref), custom_call_target="tpu_custom_call" | custom-call | flops 671088640 | bytes 6291456 | tf_op jit(solution)/shard_map/product/pallas_call | solution.py:162
  115.7 0.9 collective-permute-start.10
  116.6 0.0 collective-permute-done.6.x_ref
  116.7 6.2 %product.6 = f32[384,640]{1,0:T(8,128)S(1)} custom-call(bf16[640,4096]{1,0:T(8,128)(2,1)} %copy-done, bf16[4096,384]{1,0:T(8,128)(2,1)} %collective-permute-done.6.x_ref), custom_call_target="tpu_custom_call" | custom-call | flops 2013265920 | bytes 8388608 | tf_op jit(solution)/shard_map/product/pallas_call | solution.py:162
  122.9 0.1 collective-permute-start.7
  122.9 10.7 %collective-permute-done.3.x_ref = bf16[4096,128]{1,0:T(8,128)(2,1)} collective-permute-done((bf16[4096,128]{1,0:T(8,128)(2,1)}, bf16[4096,128]{1,0:T(8,128)(2,1)}, u32[]{:S(2)}, u32[]{:S(2)}) %collective-permute-start.3) | collective-permute-done | bytes 1048608 | tf_op jit(solution)/shard_map/ppermute | solution.py:212
  133.6 4.5 %product.5 = f32[128,640]{1,0:T(8,128)S(1)} custom-call(bf16[640,4096]{1,0:T(8,128)(2,1)} %copy-done, bf16[4096,128]{1,0:T(8,128)(2,1)} %collective-permute-done.3.x_ref), custom_call_target="tpu_custom_call" | custom-call | flops 671088640 | bytes 6291456 | tf_op jit(solution)/shard_map/product/pallas_call | solution.py:162
  138.2 0.2 collective-permute-start.4
  138.5 0.0 collective-permute-done.10
  138.5 2.7 %collective-permute-start.11 = (bf16[1,32,640]{2,1,0:T(8,128)(2,1)S(1)}, bf16[1,32,640]{2,1,0:T(8,128)(2,1)S(1)}, u32[]{:S(2)}, u32[]{:S(2)}) collective-permute-start(bf16[1,32,640]{2,1,0:T(8,128)(2,1)S(1)} %dynamic-slice_convert_fusion.2), channel_id=1, source_target_pairs={{0,2},{1,3},{2,0},{3,1},{4,6},{5,7},{6,4},{7,5},{8,10},{9,11},{10,... | collective-permute-start | bytes 122888 | tf_op jit(solution)/shard_map/ppermute | solution.py:187
  141.3 0.0 collective-permute-done.4
  141.3 0.9 collective-permute-start.5
  142.2 1.1 collective-permute-done.11
  143.2 2.1 %collective-permute-done.5 = bf16[1,32,640]{2,1,0:T(8,128)(2,1)S(1)} collective-permute-done((bf16[1,32,640]{2,1,0:T(8,128)(2,1)S(1)}, bf16[1,32,640]{2,1,0:T(8,128)(2,1)S(1)}, u32[]{:S(2)}, u32[]{:S(2)}) %collective-permute-start.5) | collective-permute-done | bytes 40992 | tf_op jit(solution)/shard_map/ppermute | solution.py:187
  145.4 0.0 collective-permute-done.7
  145.5 0.9 collective-permute-start.8
  146.4 0.0 collective-permute-done.1
  146.4 0.1 bitcast_add_fusion
  146.5 1.3 collective-permute-start.2
  147.8 3.9 %collective-permute-done.8 = bf16[1,96,640]{2,1,0:T(8,128)(2,1)S(1)} collective-permute-done((bf16[1,96,640]{2,1,0:T(8,128)(2,1)S(1)}, bf16[1,96,640]{2,1,0:T(8,128)(2,1)S(1)}, u32[]{:S(2)}, u32[]{:S(2)}) %collective-permute-start.8) | collective-permute-done | bytes 122912 | tf_op jit(solution)/shard_map/ppermute | solution.py:187
  151.7 0.8 maximum_bitcast_fusion
  152.5 1.4 collective-permute-done.2
  153.9 0.8 convert_add_fusion
  (15 shorter events, 0.3 us)
Async XLA Ops:
  2.1 7.9 %copy-start.2 = (bf16[1,2,64,64]{3,2,1,0:T(8,128)(2,1)S(1)}, bf16[1,2,64,64]{3,2,1,0:T(8,128)(2,1)}, u32[]{:S(2)}) copy-start(bf16[1,2,64,64]{3,2,1,0:T(8,128)(2,1)} %param.5) | copy-start | bytes 49156
  8.7 27.5 %collective-permute-start = (bf16[640,4096]{1,0:T(8,128)(2,1)}, bf16[640,4096]{1,0:T(8,128)(2,1)}, u32[]{:S(2)}, u32[]{:S(2)}) collective-permute-start(bf16[640,4096]{1,0:T(8,128)(2,1)} %vir.2), channel_id=1, source_target_pairs={{1,0},{2,1},{3,2},{5,4},{6,5},{7,6},{9,8},{10,9},{11,10},{13,12},{... | collective-permute-start | bytes 15728648 | tf_op jit(solution)/shard_map/ppermute | solution.py:213
  15.2 101.5 %collective-permute-start.6 = (bf16[4096,384]{1,0:T(8,128)(2,1)S(1)}, bf16[4096,384]{1,0:T(8,128)(2,1)}, u32[]{:S(2)}, u32[]{:S(2)}) collective-permute-start(bf16[4096,384]{1,0:T(8,128)(2,1)S(1)} %bitcast.69), channel_id=1, source_target_pairs={{4,0},{8,4},{12,8},{16,12},{20,16},{24,20},{28,24},{5,1},{9,5},{13... | collective-permute-start | bytes 9437192 | tf_op jit(solution)/shard_map/ppermute | solution.py:212
  20.1 91.0 %collective-permute-start.9 = (bf16[4096,128]{1,0:T(8,128)(2,1)}, bf16[4096,128]{1,0:T(8,128)(2,1)}, u32[]{:S(2)}, u32[]{:S(2)}) collective-permute-start(bf16[4096,128]{1,0:T(8,128)(2,1)} %bitcast.25), channel_id=1, source_target_pairs={{4,0},{8,4},{12,8},{16,12},{20,16},{24,20},{28,24},{5,1},{9,5},{13... | collective-permute-start | bytes 3145736 | tf_op jit(solution)/shard_map/ppermute | solution.py:212
  25.1 108.6 %collective-permute-start.3 = (bf16[4096,128]{1,0:T(8,128)(2,1)}, bf16[4096,128]{1,0:T(8,128)(2,1)}, u32[]{:S(2)}, u32[]{:S(2)}) collective-permute-start(bf16[4096,128]{1,0:T(8,128)(2,1)} %bitcast.14), channel_id=1, source_target_pairs={{4,0},{8,4},{12,8},{16,12},{20,16},{24,20},{28,24},{5,1},{9,5},{13... | collective-permute-start | bytes 3145736 | tf_op jit(solution)/shard_map/ppermute | solution.py:212
  33.8 2.4 %copy-start.1 = (bf16[64,64,640]{2,1,0:T(8,128)(2,1)}, bf16[64,64,640]{2,1,0:T(8,128)(2,1)S(1)}, u32[]{:S(2)}) copy-start(bf16[64,64,640]{2,1,0:T(8,128)(2,1)S(1)} %occ.4) | copy-start | bytes 15728644
  42.1 2.3 %copy-start = (bf16[640,4096]{1,0:T(8,128)(2,1)}, bf16[640,4096]{1,0:T(8,128)(2,1)S(1)}, u32[]{:S(2)}) copy-start(bf16[640,4096]{1,0:T(8,128)(2,1)S(1)} %vir.3.z_ref) | copy-start | bytes 15728644
  52.2 94.2 %collective-permute-start.1 = (bf16[2,160,640]{2,1,0:T(8,128)(2,1)S(1)}, bf16[2,160,640]{2,1,0:T(8,128)(2,1)S(1)}, u32[]{:S(2)}, u32[]{:S(2)}) collective-permute-start(bf16[2,160,640]{2,1,0:T(8,128)(2,1)S(1)} %fusion), channel_id=1, source_target_pairs={{0,1},{1,0},{2,3},{3,2},{4,5},{5,4},{6,7},{7,6},{8,9},{9,8},{10,11... | collective-permute-start | bytes 1228808 | tf_op jit(solution)/shard_map/ppermute | solution.py:187
  115.7 22.7 %collective-permute-start.10 = (bf16[2,32,640]{2,1,0:T(8,128)(2,1)S(1)}, bf16[2,32,640]{2,1,0:T(8,128)(2,1)S(1)}, u32[]{:S(2)}, u32[]{:S(2)}) collective-permute-start(bf16[2,32,640]{2,1,0:T(8,128)(2,1)S(1)} %fusion.3), channel_id=1, source_target_pairs={{0,1},{1,0},{2,3},{3,2},{4,5},{5,4},{6,7},{7,6},{8,9},{9,8},{10,11... | collective-permute-start | bytes 245768 | tf_op jit(solution)/shard_map/ppermute | solution.py:187
  122.9 22.5 %collective-permute-start.7 = (bf16[2,96,640]{2,1,0:T(8,128)(2,1)S(1)}, bf16[2,96,640]{2,1,0:T(8,128)(2,1)S(1)}, u32[]{:S(2)}, u32[]{:S(2)}) collective-permute-start(bf16[2,96,640]{2,1,0:T(8,128)(2,1)S(1)} %fusion.1), channel_id=1, source_target_pairs={{0,1},{1,0},{2,3},{3,2},{4,5},{5,4},{6,7},{7,6},{8,9},{9,8},{10,11... | collective-permute-start | bytes 737288 | tf_op jit(solution)/shard_map/ppermute | solution.py:187
  138.2 3.0 %collective-permute-start.4 = (bf16[2,32,640]{2,1,0:T(8,128)(2,1)S(1)}, bf16[2,32,640]{2,1,0:T(8,128)(2,1)S(1)}, u32[]{:S(2)}, u32[]{:S(2)}) collective-permute-start(bf16[2,32,640]{2,1,0:T(8,128)(2,1)S(1)} %fusion.2), channel_id=1, source_target_pairs={{0,1},{1,0},{2,3},{3,2},{4,5},{5,4},{6,7},{7,6},{8,9},{9,8},{10,11... | collective-permute-start | bytes 245768 | tf_op jit(solution)/shard_map/ppermute | solution.py:187
  138.5 4.7 %collective-permute-start.11 = (bf16[1,32,640]{2,1,0:T(8,128)(2,1)S(1)}, bf16[1,32,640]{2,1,0:T(8,128)(2,1)S(1)}, u32[]{:S(2)}, u32[]{:S(2)}) collective-permute-start(bf16[1,32,640]{2,1,0:T(8,128)(2,1)S(1)} %dynamic-slice_convert_fusion.2), channel_id=1, source_target_pairs={{0,2},{1,3},{2,0},{3,1},{4,6},{5,7},{6,4},{7,5},{8,10},{9,11},{10,... | collective-permute-start | bytes 122888 | tf_op jit(solution)/shard_map/ppermute | solution.py:187
  141.3 4.1 %collective-permute-start.5 = (bf16[1,32,640]{2,1,0:T(8,128)(2,1)S(1)}, bf16[1,32,640]{2,1,0:T(8,128)(2,1)S(1)}, u32[]{:S(2)}, u32[]{:S(2)}) collective-permute-start(bf16[1,32,640]{2,1,0:T(8,128)(2,1)S(1)} %dynamic-slice_convert_fusion.3), channel_id=1, source_target_pairs={{0,2},{1,3},{2,0},{3,1},{4,6},{5,7},{6,4},{7,5},{8,10},{9,11},{10,... | collective-permute-start | bytes 122888 | tf_op jit(solution)/shard_map/ppermute | solution.py:187
  145.5 6.2 %collective-permute-start.8 = (bf16[1,96,640]{2,1,0:T(8,128)(2,1)S(1)}, bf16[1,96,640]{2,1,0:T(8,128)(2,1)S(1)}, u32[]{:S(2)}, u32[]{:S(2)}) collective-permute-start(bf16[1,96,640]{2,1,0:T(8,128)(2,1)S(1)} %dynamic-slice_convert_fusion.1), channel_id=1, source_target_pairs={{0,2},{1,3},{2,0},{3,1},{4,6},{5,7},{6,4},{7,5},{8,10},{9,11},{10,... | collective-permute-start | bytes 368648 | tf_op jit(solution)/shard_map/ppermute | solution.py:187
  146.5 7.4 %collective-permute-start.2 = (bf16[1,160,640]{2,1,0:T(8,128)(2,1)S(1)}, bf16[1,160,640]{2,1,0:T(8,128)(2,1)S(1)}, u32[]{:S(2)}, u32[]{:S(2)}) collective-permute-start(bf16[1,160,640]{2,1,0:T(8,128)(2,1)S(1)} %dynamic-slice_convert_fusion), channel_id=1, source_target_pairs={{0,2},{1,3},{2,0},{3,1},{4,6},{5,7},{6,4},{7,5},{8,10},{9,11},{10,... | collective-permute-start | bytes 614408 | tf_op jit(solution)/shard_map/ppermute | solution.py:187

commit v3 on v2

--- a/solution.py
+++ b/solution.py
@@ -10,6 +10,8 @@
 VMEM_BYTES = 48 * 1024 * 1024
 SPAN = 256
 SUBLANES = 8
+SMALL = 128
+PIECES = 2
 
 
 def dot(a, b, dims=((1,), (0,))):
@@ -43,10 +45,15 @@
 
 
 def cost(flops, size):
-    return pl.CostEstimate(flops=flops, bytes_accessed=size, transcendentals=0)
-
-
-def occ_kernel(live_ref, g_ref, y_ref, out_ref, rows_ref, yt_ref, sems, *, slices):
+    return pl.CostEstimate(flops=1, bytes_accessed=1, transcendentals=0)
+
+
+def unused(before):
+    return [pl.BlockSpec(memory_space=pl.ANY)] * len(before)
+
+
+def occ_kernel(live_ref, g_ref, y_ref, *rest, slices):
+    out_ref, rows_ref, yt_ref, sems = rest[-4:]
     width, size = rows_ref.shape
     m, tile = g_ref.shape
     per = SPAN // tile
@@ -76,7 +83,7 @@
         out_ref[:, s * pair : (s + 1) * pair, :] = jnp.concatenate([low, high], axis=1).astype(BF)
 
 
-def occ(live, mat, y, slices):
+def occ(live, mat, y, slices, before=()):
     m, tile = mat.shape
     size = y.shape[1]
     width = sum(count for _, count in slices)
@@ -86,6 +93,7 @@
             pl.BlockSpec(memory_space=pltpu.SMEM),
             pl.BlockSpec(memory_space=pltpu.VMEM),
             pl.BlockSpec(memory_space=pl.ANY),
+            *unused(before),
         ],
         out_specs=pl.BlockSpec(memory_space=pltpu.VMEM),
         out_shape=jax.ShapeDtypeStruct((m, tile, width), BF),
@@ -97,12 +105,13 @@
         compiler_params=params(),
         cost_estimate=cost(2 * width * size * m * SUBLANES, 4 * width * size),
         name="occ",
-    )(live, mat, y)
+    )(live, mat, y, *before)
     return out.reshape(m * tile, width)
 
 
-def vir_kernel(live_ref, g_ref, y_ref, *rest):
-    *added, out_ref, kron_ref = rest
+def vir_kernel(live_ref, g_ref, y_ref, *rest, n_added):
+    added = rest[:n_added]
+    out_ref, kron_ref = rest[-2:]
 
     @pl.when(pl.program_id(0) == 0)
     def _():
@@ -117,18 +126,20 @@
         out_ref[:, at] = got.astype(BF)
 
 
-def vir(live, mat, y, added=()):
-    aux, size = y.shape
+def vir(live, mat, y, piece, added=(), before=()):
+    aux = y.shape[0]
+    size = y.shape[1] // PIECES
     span = 4 * SPAN if size % (4 * SPAN) == 0 else SPAN
     block = pl.BlockSpec((aux, span), lambda i: (0, i))
     return pl.pallas_call(
-        vir_kernel,
+        lambda *refs: vir_kernel(*refs, n_added=len(added)),
         grid=(size // span,),
         in_specs=[
             pl.BlockSpec(memory_space=pltpu.SMEM),
             pl.BlockSpec(mat.shape, lambda i: (0, 0)),
-            block,
+            pl.BlockSpec((aux, span), lambda i: (0, piece * (size // span) + i)),
             *(block for _ in added),
+            *unused(before),
         ],
         out_specs=block,
         out_shape=jax.ShapeDtypeStruct((aux, size), BF),
@@ -136,48 +147,55 @@
         compiler_params=params(),
         cost_estimate=cost(2 * aux * size * SPAN, 2 * (2 + len(added)) * aux * size),
         name="vir",
-    )(live, mat, y, *added)
-
-
-def product_kernel(z_ref, x_ref, out_ref, acc_ref):
+    )(live, mat, y, *added, *before)
+
+
+def product_kernel(x_ref, *rest, steps):
+    z_refs = rest[:PIECES]
+    out_ref, acc_ref = rest[-2:]
     step = pl.program_id(0)
 
     @pl.when(step == 0)
     def _():
-        acc_ref[...] = dot(z_ref[...], x_ref[...])
-
-    @pl.when(step > 0)
-    def _():
-        acc_ref[...] += dot(z_ref[...], x_ref[...])
+        acc_ref[...] = dot(z_refs[0][...], x_ref[...])
+
+    for i, z_ref in enumerate(z_refs):
+
+        @pl.when(jnp.logical_and(step > 0, step // steps == i))
+        def _(z_ref=z_ref):
+            acc_ref[...] += dot(z_ref[...], x_ref[...])
 
     @pl.when(step == pl.num_programs(0) - 1)
     def _():
         out_ref[...] = acc_ref[...].T
 
 
-def product(z, x):
-    aux, size = z.shape
+def product(zs, x, before=()):
+    aux, size = zs[0].shape
     width = x.shape[1]
     span = 4 * SPAN if size % (4 * SPAN) == 0 else SPAN
+    steps = size // span
+    piece = lambda k: pl.BlockSpec((aux, span), lambda i: (0, jnp.clip(i - k * steps, 0, steps - 1)))
     return pl.pallas_call(
-        product_kernel,
-        grid=(size // span,),
-        in_specs=[pl.BlockSpec((aux, span), lambda i: (0, i)), pl.BlockSpec((span, width), lambda i: (i, 0))],
+        lambda *refs: product_kernel(*refs, steps=steps),
+        grid=(len(zs) * steps,),
+        in_specs=[pl.BlockSpec((span, width), lambda i: (i, 0)), *(piece(k) for k in range(len(zs))), *unused(before)],
         out_specs=pl.BlockSpec((width, aux), lambda i: (0, 0)),
         out_shape=jax.ShapeDtypeStruct((width, aux), F32),
         scratch_shapes=[pltpu.VMEM((aux, width), F32)],
         compiler_params=params(),
         cost_estimate=cost(2 * aux * size * width, 2 * size * (aux + width)),
         name="product",
-    )(z, x)
-
-
-def scattered(value, axis):
+    )(x, *zs, *before)
+
+
+def scattered(parts, axis):
     size = lax.axis_size(axis)
+    blocks = [part.reshape(size, part.shape[0] // size, part.shape[1]) for part in parts]
+    blocks = jnp.concatenate(blocks, axis=1) if len(blocks) > 1 else blocks[0]
     if size & (size - 1):
-        return lax.psum_scatter(value.astype(BF), axis, scatter_dimension=0, tiled=True).astype(F32)
+        return lax.psum_scatter(blocks.astype(BF), axis, scatter_dimension=0).astype(F32)
     me = lax.axis_index(axis)
-    blocks = value.reshape(size, value.shape[0] // size, value.shape[1])
     reach = 1
     while reach < size:
         bit = (me // reach) % 2
@@ -192,9 +210,9 @@
 
 def chunks_of(aux, owners):
     each = aux // owners
-    small = 128 // owners
-    if owners * small == 128 and small % 16 == 0 and each % 16 == 0 and each > 2 * small:
-        cuts = [0, small, each - small, each]
+    small = SMALL // owners
+    if owners * small == SMALL and small % 16 == 0 and each % 16 == 0 and each > small:
+        cuts = [0, each - small, each]
         return [[(j * each + a, b - a) for j in range(owners)] for a, b in zip(cuts, cuts[1:])]
     return [[(0, aux)]]
 
@@ -208,13 +226,28 @@
     up_col = [(i, i - 1) for i in range(1, cols)]
     to_own, to_lower = green_occ[0, 0].T, green_occ[0, 1].T
 
-    halves = [occ(live, to_lower, y, part) for part in chunks_of(aux, cols)]
-    above = [lax.ppermute(half, "row", up_row) for half in halves]
-    shifted = lax.ppermute(vir(live, green_vir[0, 1].T, y), "col", up_col)
-    own = occ(live, to_own, y, [(0, aux)])
-    z = vir(live, green_vir[0, 0].T, y, (shifted,))
-    chi_d = scattered(product(z, own), "col")
-    chi_n = jnp.concatenate([scattered(product(z, half), "col") for half in above])
+    first, *others = chunks_of(aux, cols)
+    send = lambda half: lax.ppermute(half, "row", up_row)
+    last = occ(live, to_lower, y, first)
+    above = [send(last)]
+    shifted = []
+    for i in range(PIECES):
+        last = vir(live, green_vir[0, 1].T, y, i, before=(last,))
+        shifted.append(lax.ppermute(last, "col", up_col))
+    for part in others:
+        last = occ(live, to_lower, y, part, before=(last,))
+        above.append(send(last))
+    own = occ(live, to_own, y, [(0, aux)], before=(last,))
+    zs = []
+    for i in range(PIECES):
+        zs.append(vir(live, green_vir[0, 0].T, y, i, (shifted[i],), before=(own,)))
+    chi_d = scattered([product(zs, own)], "col")
+    blocks = []
+    last = chi_d
+    for half in above:
+        last = product(zs, half, before=(last,))
+        blocks.append(last)
+    chi_n = scattered(blocks, "col")
     return chi_d[None], chi_n[None]
 
 

time: 155 us -> 143 us (0.923)
  waiting for transfers between devices: 42.7 us -> 31 us
  Pallas kernels: 54.8 us -> 52.6 us
  starting transfers between devices: 47.9 us -> 49.7 us
    ppermute x4, waiting for transfers between devices: 34.2 us -> 16.3 us  [the longest x2 16.2 us: body(): send = lambda half: lax.ppermute(half, 'row', up_row)]
    ppermute x8 -> x4, waiting for transfers between devices: 8.52 us -> 14.7 us  [scattered(): got = lax.ppermute(given, axis, [(i, i ^ reach) for i in range(size)])]
    pallas_call x6 -> x7, Pallas kernels: 35.4 us -> 31.9 us  [the longest x3 18.8 us: product(): pl.pallas_call(lambda *refs: product_kernel(*refs, steps=steps), grid=(le...]
    add x5 -> x4, other arithmetic: 0.95 us -> 3.18 us  [scattered(): blocks = kept + got.astype(F32)]
    unnamed x10 -> x12, local copies, waits for them, and re-layouts: 5.01 us -> 3.04 us
    ppermute x8 -> x4, starting transfers between devices: 42.5 us -> 44.2 us  [scattered(): got = lax.ppermute(given, axis, [(i, i ^ reach) for i in range(size)])]
    pallas_call x4 -> x3, Pallas kernels: 19.4 us -> 20.7 us  [occ(): pl.pallas_call(lambda *refs: occ_kernel(*refs, slices=slices), in_specs=[...]
  transfers between devices with their start and end apart: 12 -> 8, of which waited for: 6 -> 5; matrix products, arithmetic and copies ran while one was open for 1% -> 2% of each run, Pallas kernels for 31% -> 28%
where the time goes in v3:
time: 143 us
  Pallas kernels  52.6 us (37%)
  starting transfers between devices  49.7 us (35%)
  waiting for transfers between devices  31 us (22%)
  local copies, waits for them, and re-layouts  4.58 us (3%)
  other arithmetic  3.23 us (2%)
  between operations  1.57 us (1%)
    ppermute x4, starting transfers between devices, scattered(): got = lax.ppermute(given, axis, [(i, i ^ reach) for i in range(size)])  44.2 us
    pallas_call x3, Pallas kernels, occ(): pl.pallas_call(lambda *refs: occ_kernel(*refs, slices=slices), in_specs=[...  20.7 us
    pallas_call x3, Pallas kernels, product(): pl.pallas_call(lambda *refs: product_kernel(*refs, steps=steps), grid=(le...  18.8 us
    ppermute x2, waiting for transfers between devices, body(): send = lambda half: lax.ppermute(half, 'row', up_row)  16.2 us
    ppermute x4, waiting for transfers between devices, scattered(): got = lax.ppermute(given, axis, [(i, i ^ reach) for i in range(size)])  14.7 us
    pallas_call x4, Pallas kernels, vir(): pl.pallas_call(lambda *refs: vir_kernel(*refs, n_added=len(added)), grid=...  13.1 us
    add x4, other arithmetic, scattered(): blocks = kept + got.astype(F32)  3.18 us
    unnamed x12, local copies, waits for them, and re-layouts  3.04 us
  transfers between devices with their start and end apart: 8, of which 5 were waited for; matrix products, arithmetic and copies ran while one was open for 2% of the time, Pallas kernels for 28%

profile of v3, /device:TPU:0, one launch (start us, length us, event | category | flops | bytes accessed | tf_op | source)
XLA Modules:
  0.0 142.7 jit_solution(3580705940439560958)
XLA Ops:
  1.3 0.7 fusion.9
  2.0 0.1 copy.21
  2.1 0.0 copy-start.3
  2.1 7.7 %occ.3 = bf16[64,64,512]{2,1,0:T(8,128)(2,1)} custom-call(s32[1]{0:T(128)} %bitcast.43.refs_0_, bf16[64,64]{1,0:T(8,128)(2,1)S(1)} %bitcast.57, bf16[640,4096]{1,0:T(8,128)(2,1)} %bitcast.64), custom_call_target="tpu_custom_call" | custom-call | flops 1 | bytes 1 | tf_op jit(solution)/shard_map/occ/pallas_call | solution.py:90
  9.8 1.3 collective-permute-start.4
  11.1 0.0 copy-done.3
  11.1 0.1 copy.22
  11.2 2.8 %vir.4.refs_3_ = bf16[640,2048]{1,0:T(8,128)(2,1)S(1)} custom-call(s32[1]{0:T(128)} %bitcast.44.refs_0_, bf16[64,64]{1,0:T(8,128)(2,1)S(1)} %bitcast.59, bf16[640,4096]{1,0:T(8,128)(2,1)} %bitcast.65, bf16[4096,512]{1,0:T(8,128)(2,1)} %bitcast.10.refs_3_), custom_call_target="tpu_custom_call" | custom-call | flops 1 | bytes 1 | tf_op jit(solution)/shard_map/vir/pallas_call | solution.py:134
  14.0 3.8 %vir.5.refs_3_ = bf16[640,2048]{1,0:T(8,128)(2,1)} custom-call(s32[1]{0:T(128)} %bitcast.45.refs_0_, bf16[64,64]{1,0:T(8,128)(2,1)S(1)} %bitcast.60, bf16[640,4096]{1,0:T(8,128)(2,1)} %bitcast.66, bf16[640,2048]{1,0:T(8,128)(2,1)S(1)} %vir.4.refs_3_), custom_call_target="tpu_custom_call" | custom-call | flops 1 | bytes 1 | tf_op jit(solution)/shard_map/vir/pallas_call | solution.py:134
  17.8 1.3 collective-permute-start.1
  19.1 1.5 %collective-permute-start = (bf16[640,2048]{1,0:T(8,128)(2,1)S(1)}, bf16[640,2048]{1,0:T(8,128)(2,1)}, u32[]{:S(2)}, u32[]{:S(2)}) collective-permute-start(bf16[640,2048]{1,0:T(8,128)(2,1)S(1)} %vir.4.refs_3_), channel_id=1, source_target_pairs={{1,0},{2,1},{3,2},{5,4},{6,5},{7,6},{9,8},{10,9},{11,10},{13,12},{... | collective-permute-start | bytes 7864328 | tf_op jit(solution)/shard_map/ppermute | solution.py:236
  20.6 3.7 %occ.4 = bf16[64,64,128]{2,1,0:T(8,128)(2,1)} custom-call(s32[1]{0:T(128)} %bitcast.46.refs_0_, bf16[64,64]{1,0:T(8,128)(2,1)S(1)} %bitcast.58, bf16[640,4096]{1,0:T(8,128)(2,1)} %bitcast.67, bf16[640,2048]{1,0:T(8,128)(2,1)} %vir.5.refs_3_), custom_call_target="tpu_custom_call" | custom-call | flops 1 | bytes 1 | tf_op jit(solution)/shard_map/occ/pallas_call | solution.py:90
  24.3 0.1 copy.20
  24.4 9.4 %occ.5 = bf16[64,64,640]{2,1,0:T(8,128)(2,1)} custom-call(s32[1]{0:T(128)} %bitcast.47.refs_0_, bf16[64,64]{1,0:T(8,128)(2,1)S(1)} %bitcast.63, bf16[640,4096]{1,0:T(8,128)(2,1)} %bitcast.68, bf16[4096,128]{1,0:T(8,128)(2,1)} %bitcast.11.refs_3_), custom_call_target="tpu_custom_call" | custom-call | flops 1 | bytes 1 | tf_op jit(solution)/shard_map/occ/pallas_call | solution.py:90
  33.8 0.1 copy.23
  33.9 0.0 collective-permute-done.1.refs_3_
  33.9 3.3 %vir.7.refs_2_ = bf16[640,2048]{1,0:T(8,128)(2,1)S(1)} custom-call(s32[1]{0:T(128)} %bitcast.49.refs_0_, bf16[64,64]{1,0:T(8,128)(2,1)S(1)} %bitcast.61, bf16[640,4096]{1,0:T(8,128)(2,1)} %bitcast.69, bf16[640,2048]{1,0:T(8,128)(2,1)} %collective-permute-done.1.refs_3_, bf16[4096,640]{1,0:T(8,128)(2,1)} %bitcast.71), custom_call_target="tpu_custom_call" | custom-call | flops 1 | bytes 1 | tf_op jit(solution)/shard_map/vir/pallas_call | solution.py:134
  37.1 0.0 copy-start
  37.2 1.5 %copy-done = bf16[640,2048]{1,0:T(8,128)(2,1)} copy-done((bf16[640,2048]{1,0:T(8,128)(2,1)}, bf16[640,2048]{1,0:T(8,128)(2,1)S(1)}, u32[]{:S(2)}) %copy-start) | copy-done | bytes 2621464
  38.6 0.0 collective-permute-done.refs_3_
  38.6 3.2 %vir.6.refs_1_ = bf16[640,2048]{1,0:T(8,128)(2,1)S(1)} custom-call(s32[1]{0:T(128)} %bitcast.48.refs_0_, bf16[64,64]{1,0:T(8,128)(2,1)S(1)} %bitcast.62, bf16[640,4096]{1,0:T(8,128)(2,1)} %bitcast.70, bf16[640,2048]{1,0:T(8,128)(2,1)} %collective-permute-done.refs_3_, bf16[4096,640]{1,0:T(8,128)(2,1)} %bitcast.72), custom_call_target="tpu_custom_call" | custom-call | flops 1 | bytes 1 | tf_op jit(solution)/shard_map/vir/pallas_call | solution.py:134
  41.9 7.7 %product.3 = f32[640,640]{1,0:T(8,128)S(1)} custom-call(bf16[4096,640]{1,0:T(8,128)(2,1)} %bitcast.73, bf16[640,2048]{1,0:T(8,128)(2,1)S(1)} %vir.6.refs_1_, bf16[640,2048]{1,0:T(8,128)(2,1)} %copy-done), custom_call_target="tpu_custom_call" | custom-call | flops 1 | bytes 1 | tf_op jit(solution)/shard_map/product/pallas_call | solution.py:179
  49.6 0.0 copy-start.1
  49.6 1.2 copy-done.1
  50.8 42.3 %collective-permute-start.2 = (bf16[2,160,640]{2,1,0:T(8,128)(2,1)S(1)}, bf16[2,160,640]{2,1,0:T(8,128)(2,1)}, u32[]{:S(2)}, u32[]{:S(2)}) collective-permute-start(bf16[2,160,640]{2,1,0:T(8,128)(2,1)S(1)} %fusion.6), channel_id=1, source_target_pairs={{0,1},{1,0},{2,3},{3,2},{4,5},{5,4},{6,7},{7,6},{8,9},{9,8},{10,11... | collective-permute-start | bytes 1228808 | tf_op jit(solution)/shard_map/ppermute | solution.py:205
  93.1 1.5 %collective-permute-start.5 = (bf16[4096,128]{1,0:T(8,128)(2,1)}, bf16[4096,128]{1,0:T(8,128)(2,1)}, u32[]{:S(2)}, u32[]{:S(2)}) collective-permute-start(bf16[4096,128]{1,0:T(8,128)(2,1)} %bitcast.11.refs_3_), channel_id=1, source_target_pairs={{4,0},{8,4},{12,8},{16,12},{20,16},{24,20},{28,24},{5,1},{9,5},{13... | collective-permute-start | bytes 3145736 | tf_op jit(solution)/shard_map/ppermute | solution.py:230
  94.6 0.0 collective-permute-done.2
  94.6 1.3 bitcast_add_fusion
  96.0 0.7 dynamic-slice_convert_fusion.1
  96.7 0.0 collective-permute-start.3
  96.7 7.6 %collective-permute-done.3 = bf16[1,160,640]{2,1,0:T(8,128)(2,1)} collective-permute-done((bf16[1,160,640]{2,1,0:T(8,128)(2,1)}, bf16[1,160,640]{2,1,0:T(8,128)(2,1)}, u32[]{:S(2)}, u32[]{:S(2)}) %collective-permute-start.3) | collective-permute-done | bytes 204832 | tf_op jit(solution)/shard_map/ppermute | solution.py:205
  104.3 1.0 convert_add_fusion.1
  105.3 0.0 copy-start.2
  105.3 1.1 collective-permute-done.4.refs_0_
  106.3 6.4 %product.4.refs_3_ = f32[512,640]{1,0:T(8,128)S(1)} custom-call(bf16[4096,512]{1,0:T(8,128)(2,1)} %collective-permute-done.4.refs_0_, bf16[640,2048]{1,0:T(8,128)(2,1)S(1)} %vir.6.refs_1_, bf16[640,2048]{1,0:T(8,128)(2,1)} %copy-done, f32[160,640]{1,0:T(8,128)S(1)} %bitcast.56), custom_call_target="tpu_custom_call" | custom-call | flops 1 | bytes 1 | tf_op jit(solution)/shard_map/product/pallas_call | solution.py:179
  112.8 0.0 copy-done.2
  112.8 15.2 %collective-permute-done.5.refs_0_ = bf16[4096,128]{1,0:T(8,128)(2,1)} collective-permute-done((bf16[4096,128]{1,0:T(8,128)(2,1)}, bf16[4096,128]{1,0:T(8,128)(2,1)}, u32[]{:S(2)}, u32[]{:S(2)}) %collective-permute-start.5) | collective-permute-done | bytes 1048608 | tf_op jit(solution)/shard_map/ppermute | solution.py:230
  128.0 4.7 %product.5 = f32[128,640]{1,0:T(8,128)S(1)} custom-call(bf16[4096,128]{1,0:T(8,128)(2,1)} %collective-permute-done.5.refs_0_, bf16[640,2048]{1,0:T(8,128)(2,1)S(1)} %vir.6.refs_1_, bf16[640,2048]{1,0:T(8,128)(2,1)} %copy-done, f32[512,640]{1,0:T(8,128)S(1)} %product.4.refs_3_), custom_call_target="tpu_custom_call" | custom-call | flops 1 | bytes 1 | tf_op jit(solution)/shard_map/product/pallas_call | solution.py:179
  132.7 0.1 fusion.7
  132.7 0.1 collective-permute-start.6
  132.8 1.7 %collective-permute-done.6 = bf16[2,160,640]{2,1,0:T(8,128)(2,1)S(1)} collective-permute-done((bf16[2,160,640]{2,1,0:T(8,128)(2,1)S(1)}, bf16[2,160,640]{2,1,0:T(8,128)(2,1)S(1)}, u32[]{:S(2)}, u32[]{:S(2)}) %collective-permute-start.6) | collective-permute-done | bytes 409632 | tf_op jit(solution)/shard_map/ppermute | solution.py:205
  134.6 0.1 fusion.5
  134.7 1.8 %collective-permute-start.7 = (bf16[1,160,640]{2,1,0:T(8,128)(2,1)S(1)}, bf16[1,160,640]{2,1,0:T(8,128)(2,1)S(1)}, u32[]{:S(2)}, u32[]{:S(2)}) collective-permute-start(bf16[1,160,640]{2,1,0:T(8,128)(2,1)S(1)} %dynamic-slice_convert_fusion), channel_id=1, source_target_pairs={{0,2},{1,3},{2,0},{3,1},{4,6},{5,7},{6,4},{7,5},{8,10},{9,11},{10,... | collective-permute-start | bytes 614408 | tf_op jit(solution)/shard_map/ppermute | solution.py:205
  136.5 5.4 %collective-permute-done.7 = bf16[1,160,640]{2,1,0:T(8,128)(2,1)S(1)} collective-permute-done((bf16[1,160,640]{2,1,0:T(8,128)(2,1)S(1)}, bf16[1,160,640]{2,1,0:T(8,128)(2,1)S(1)}, u32[]{:S(2)}, u32[]{:S(2)}) %collective-permute-start.7) | collective-permute-done | bytes 204832 | tf_op jit(solution)/shard_map/ppermute | solution.py:205
  141.9 0.8 convert_add_fusion
  (3 shorter events, 0.1 us)
Async XLA Ops:
  2.1 9.0 %copy-start.3 = (bf16[1,2,64,64]{3,2,1,0:T(8,128)(2,1)S(1)}, bf16[1,2,64,64]{3,2,1,0:T(8,128)(2,1)}, u32[]{:S(2)}) copy-start(bf16[1,2,64,64]{3,2,1,0:T(8,128)(2,1)} %param.6) | copy-start | bytes 49156
  9.8 96.6 %collective-permute-start.4 = (bf16[4096,512]{1,0:T(8,128)(2,1)}, bf16[4096,512]{1,0:T(8,128)(2,1)}, u32[]{:S(2)}, u32[]{:S(2)}) collective-permute-start(bf16[4096,512]{1,0:T(8,128)(2,1)} %bitcast.10.refs_3_), channel_id=1, source_target_pairs={{4,0},{8,4},{12,8},{16,12},{20,16},{24,20},{28,24},{5,1},{9,5},{13... | collective-permute-start | bytes 12582920 | tf_op jit(solution)/shard_map/ppermute | solution.py:230
  17.8 16.0 %collective-permute-start.1 = (bf16[640,2048]{1,0:T(8,128)(2,1)}, bf16[640,2048]{1,0:T(8,128)(2,1)}, u32[]{:S(2)}, u32[]{:S(2)}) collective-permute-start(bf16[640,2048]{1,0:T(8,128)(2,1)} %vir.5.refs_3_), channel_id=1, source_target_pairs={{1,0},{2,1},{3,2},{5,4},{6,5},{7,6},{9,8},{10,9},{11,10},{13,12},{... | collective-permute-start | bytes 7864328 | tf_op jit(solution)/shard_map/ppermute | solution.py:236
  19.1 19.5 %collective-permute-start = (bf16[640,2048]{1,0:T(8,128)(2,1)S(1)}, bf16[640,2048]{1,0:T(8,128)(2,1)}, u32[]{:S(2)}, u32[]{:S(2)}) collective-permute-start(bf16[640,2048]{1,0:T(8,128)(2,1)S(1)} %vir.4.refs_3_), channel_id=1, source_target_pairs={{1,0},{2,1},{3,2},{5,4},{6,5},{7,6},{9,8},{10,9},{11,10},{13,12},{... | collective-permute-start | bytes 7864328 | tf_op jit(solution)/shard_map/ppermute | solution.py:236
  37.1 1.5 %copy-start = (bf16[640,2048]{1,0:T(8,128)(2,1)}, bf16[640,2048]{1,0:T(8,128)(2,1)S(1)}, u32[]{:S(2)}) copy-start(bf16[640,2048]{1,0:T(8,128)(2,1)S(1)} %vir.7.refs_2_) | copy-start | bytes 7864324
  49.6 1.2 copy-start.1
  50.8 43.8 %collective-permute-start.2 = (bf16[2,160,640]{2,1,0:T(8,128)(2,1)S(1)}, bf16[2,160,640]{2,1,0:T(8,128)(2,1)}, u32[]{:S(2)}, u32[]{:S(2)}) collective-permute-start(bf16[2,160,640]{2,1,0:T(8,128)(2,1)S(1)} %fusion.6), channel_id=1, source_target_pairs={{0,1},{1,0},{2,3},{3,2},{4,5},{5,4},{6,7},{7,6},{8,9},{9,8},{10,11... | collective-permute-start | bytes 1228808 | tf_op jit(solution)/shard_map/ppermute | solution.py:205
  93.1 34.9 %collective-permute-start.5 = (bf16[4096,128]{1,0:T(8,128)(2,1)}, bf16[4096,128]{1,0:T(8,128)(2,1)}, u32[]{:S(2)}, u32[]{:S(2)}) collective-permute-start(bf16[4096,128]{1,0:T(8,128)(2,1)} %bitcast.11.refs_3_), channel_id=1, source_target_pairs={{4,0},{8,4},{12,8},{16,12},{20,16},{24,20},{28,24},{5,1},{9,5},{13... | collective-permute-start | bytes 3145736 | tf_op jit(solution)/shard_map/ppermute | solution.py:230
  96.7 7.6 %collective-permute-start.3 = (bf16[1,160,640]{2,1,0:T(8,128)(2,1)}, bf16[1,160,640]{2,1,0:T(8,128)(2,1)}, u32[]{:S(2)}, u32[]{:S(2)}) collective-permute-start(bf16[1,160,640]{2,1,0:T(8,128)(2,1)} %dynamic-slice_convert_fusion.1), channel_id=1, source_target_pairs={{0,2},{1,3},{2,0},{3,1},{4,6},{5,7},{6,4},{7,5},{8,10},{9,11},{10,... | collective-permute-start | bytes 614408 | tf_op jit(solution)/shard_map/ppermute | solution.py:205
  105.3 7.5 %copy-start.2 = (f32[1,160,640]{2,1,0:T(8,128)}, f32[1,160,640]{2,1,0:T(8,128)S(1)}, u32[]{:S(2)}) copy-start(f32[1,160,640]{2,1,0:T(8,128)S(1)} %convert_add_fusion.1) | copy-start | bytes 1228804
  132.7 1.8 %collective-permute-start.6 = (bf16[2,160,640]{2,1,0:T(8,128)(2,1)S(1)}, bf16[2,160,640]{2,1,0:T(8,128)(2,1)S(1)}, u32[]{:S(2)}, u32[]{:S(2)}) collective-permute-start(bf16[2,160,640]{2,1,0:T(8,128)(2,1)S(1)} %fusion.7), channel_id=1, source_target_pairs={{0,1},{1,0},{2,3},{3,2},{4,5},{5,4},{6,7},{7,6},{8,9},{9,8},{10,11... | collective-permute-start | bytes 1228808 | tf_op jit(solution)/shard_map/ppermute | solution.py:205
  134.7 7.2 %collective-permute-start.7 = (bf16[1,160,640]{2,1,0:T(8,128)(2,1)S(1)}, bf16[1,160,640]{2,1,0:T(8,128)(2,1)S(1)}, u32[]{:S(2)}, u32[]{:S(2)}) collective-permute-start(bf16[1,160,640]{2,1,0:T(8,128)(2,1)S(1)} %dynamic-slice_convert_fusion), channel_id=1, source_target_pairs={{0,2},{1,3},{2,0},{3,1},{4,6},{5,7},{6,4},{7,5},{8,10},{9,11},{10,... | collective-permute-start | bytes 614408 | tf_op jit(solution)/shard_map/ppermute | solution.py:205

commit v4 on v3

--- a/solution.py
+++ b/solution.py
@@ -52,55 +52,89 @@
     return [pl.BlockSpec(memory_space=pl.ANY)] * len(before)
 
 
-def occ_kernel(live_ref, g_ref, y_ref, *rest, slices):
-    out_ref, rows_ref, yt_ref, sems = rest[-4:]
-    width, size = rows_ref.shape
-    m, tile = g_ref.shape
+def occ_kernel(live_ref, g_ref, y_ref, *rest, groups):
+    out_ref, rows_ref, yt_ref, held_ref, in_sems, out_sems = rest[-6:]
+    tile, m = g_ref.shape
+    size = y_ref.shape[1]
     per = SPAN // tile
-    copies = []
+    fetch = []
     to = 0
-    for i, (start, count) in enumerate(slices):
-        copies.append(
-            pltpu.make_async_copy(y_ref.at[pl.ds(start, count)], rows_ref.at[pl.ds(to, count)], sems.at[i])
+    for slices, _ in groups:
+        for start, count in slices:
+            fetch.append(
+                pltpu.make_async_copy(
+                    y_ref.at[pl.ds(start, count)], rows_ref.at[pl.ds(to, count)], in_sems.at[len(fetch)]
+                )
+            )
+            to += count
+    for copy in fetch:
+        copy.start()
+    kron = spread(g_ref[...].T, SUBLANES)
+    live = live_ref[0].astype(F32).astype(BF)
+    pair = 2 * SUBLANES
+    store = []
+    at, done = 0, 0
+    for k, (slices, width) in enumerate(groups):
+        for copy in fetch[done : done + len(slices)]:
+            copy.wait()
+        done += len(slices)
+        lanes = slice(at, at + width)
+        for j in range(size // SPAN):
+            part = rows_ref[lanes, j * SPAN : (j + 1) * SPAN] * live
+            yt_ref[k, j * per : (j + 1) * per, :, :width] = part.T.reshape(per, tile, width)
+        for s in range(tile // pair):
+            part = yt_ref[k, :, s * pair : (s + 1) * pair, :width].astype(F32)
+            low, high = (
+                part[:, i : i + SUBLANES].reshape(tile * SUBLANES, width).astype(BF) for i in (0, SUBLANES)
+            )
+            low, high = (dot(kron, x).reshape(m, SUBLANES, width) for x in (low, high))
+            held_ref[:, s * pair : (s + 1) * pair, lanes] = jnp.concatenate([low, high], axis=1).astype(BF)
+        store.append(
+            pltpu.make_async_copy(
+                held_ref.at[:, :, pl.ds(at, width)], out_ref.at[:, :, pl.ds(at, width)], out_sems.at[k]
+            )
         )
-        to += count
-    for copy in copies:
-        copy.start()
-    kron = spread(g_ref[...], SUBLANES)
-    live = live_ref[0].astype(F32).astype(BF)
-    for copy in copies:
+        store[-1].start()
+        at += width
+    for copy in store:
         copy.wait()
-    for j in range(size // SPAN):
-        part = rows_ref[:, j * SPAN : (j + 1) * SPAN] * live
-        yt_ref[j * per : (j + 1) * per] = part.T.reshape(per, tile, width)
-    pair = 2 * SUBLANES
-    for s in range(tile // pair):
-        part = yt_ref[:, s * pair : (s + 1) * pair, :].astype(F32)
-        low, high = (
-            part[:, k : k + SUBLANES].reshape(tile * SUBLANES, width).astype(BF) for k in (0, SUBLANES)
-        )
-        low, high = (dot(kron, x).reshape(m, SUBLANES, width) for x in (low, high))
-        out_ref[:, s * pair : (s + 1) * pair, :] = jnp.concatenate([low, high], axis=1).astype(BF)
+
+
+def grouped(slices):
+    groups, held = [], []
+    for start, count in slices:
+        held.append((start, count))
+        width = sum(n for _, n in held)
+        if width >= SPAN and width % 128 == 0:
+            groups.append((held, width))
+            held = []
+    if held:
+        groups.append((held, sum(n for _, n in held)))
+    return groups
 
 
 def occ(live, mat, y, slices, before=()):
-    m, tile = mat.shape
+    tile, m = mat.shape
     size = y.shape[1]
-    width = sum(count for _, count in slices)
+    groups = grouped(slices)
+    width = sum(n for _, n in groups)
+    widest = max(n for _, n in groups)
     out = pl.pallas_call(
-        lambda *refs: occ_kernel(*refs, slices=slices),
+        lambda *refs: occ_kernel(*refs, groups=groups),
         in_specs=[
             pl.BlockSpec(memory_space=pltpu.SMEM),
             pl.BlockSpec(memory_space=pltpu.VMEM),
             pl.BlockSpec(memory_space=pl.ANY),
             *unused(before),
         ],
-        out_specs=pl.BlockSpec(memory_space=pltpu.VMEM),
+        out_specs=pl.BlockSpec(memory_space=pl.ANY),
         out_shape=jax.ShapeDtypeStruct((m, tile, width), BF),
         scratch_shapes=[
             pltpu.VMEM((width, size), BF),
-            pltpu.VMEM((tile, tile, width), BF),
+            pltpu.VMEM((len(groups), tile, tile, widest), BF),
+            pltpu.VMEM((m, tile, width), BF),
             pltpu.SemaphoreType.DMA((len(slices),)),
+            pltpu.SemaphoreType.DMA((len(groups),)),
         ],
         compiler_params=params(),
         cost_estimate=cost(2 * width * size * m * SUBLANES, 4 * width * size),
@@ -189,22 +223,27 @@
     )(x, *zs, *before)
 
 
-def scattered(parts, axis):
+def scattered(parts, axis, direct):
     size = lax.axis_size(axis)
     blocks = [part.reshape(size, part.shape[0] // size, part.shape[1]) for part in parts]
     blocks = jnp.concatenate(blocks, axis=1) if len(blocks) > 1 else blocks[0]
     if size & (size - 1):
         return lax.psum_scatter(blocks.astype(BF), axis, scatter_dimension=0).astype(F32)
     me = lax.axis_index(axis)
-    reach = 1
-    while reach < size:
+    reaches = [1 << i for i in range(size.bit_length() - 1)]
+    if direct and size <= 4:
+        total = lax.dynamic_index_in_dim(blocks, me, 0, keepdims=False)
+        for reach in range(1, size):
+            given = lax.dynamic_index_in_dim(blocks, me ^ reach, 0, keepdims=False).astype(BF)
+            total = total + lax.ppermute(given, axis, [(i, i ^ reach) for i in range(size)]).astype(F32)
+        return total
+    for reach in reaches:
         bit = (me // reach) % 2
         pairs = blocks.reshape(blocks.shape[0] // 2, 2, *blocks.shape[1:])
         kept = lax.dynamic_index_in_dim(pairs, bit, 1, keepdims=False)
         given = lax.dynamic_index_in_dim(pairs, 1 - bit, 1, keepdims=False).astype(BF)
         got = lax.ppermute(given, axis, [(i, i ^ reach) for i in range(size)])
         blocks = kept + got.astype(F32)
-        reach *= 2
     return blocks[0]
 
 
@@ -224,7 +263,7 @@
     live = pair_live[0]
     up_row = [(i, i - 1) for i in range(1, rows)]
     up_col = [(i, i - 1) for i in range(1, cols)]
-    to_own, to_lower = green_occ[0, 0].T, green_occ[0, 1].T
+    to_own, to_lower = green_occ[0, 0], green_occ[0, 1]
 
     first, *others = chunks_of(aux, cols)
     send = lambda half: lax.ppermute(half, "row", up_row)
@@ -237,18 +276,17 @@
     for part in others:
         last = occ(live, to_lower, y, part, before=(last,))
         above.append(send(last))
-    own = occ(live, to_own, y, [(0, aux)], before=(last,))
+    own = occ(live, to_own, y, [(i, min(SPAN, aux - i)) for i in range(0, aux, SPAN)], before=(last,))
     zs = []
     for i in range(PIECES):
         zs.append(vir(live, green_vir[0, 0].T, y, i, (shifted[i],), before=(own,)))
-    chi_d = scattered([product(zs, own)], "col")
+    chi_d = scattered([product(zs, own)], "col", True)
     blocks = []
     last = chi_d
     for half in above:
-        last = product(zs, half, before=(last,))
+        last = scattered([product(zs, half, before=(last,))], "col", half is not above[-1])
         blocks.append(last)
-    chi_n = scattered(blocks, "col")
-    return chi_d[None], chi_n[None]
+    return chi_d[None], jnp.concatenate(blocks)[None]
 
 
 def solution(mesh):

time: 143 us -> 138 us (0.965)
  waiting for transfers between devices: 31 us -> 23.8 us
  starting transfers between devices: 49.7 us -> 53.6 us
  Pallas kernels: 52.6 us -> 49.9 us
    ppermute x0 -> x6, starting transfers between devices: none -> 46.6 us  [scattered(): lax.ppermute(given, axis, [(i, i ^ reach) for i in range(size)]).astype(F32)]
    ppermute x4 -> x2, starting transfers between devices: 44.2 us -> 1.9 us  [scattered(): got = lax.ppermute(given, axis, [(i, i ^ reach) for i in range(size)])]
    ppermute x0 -> x6, waiting for transfers between devices: none -> 18.3 us  [scattered(): lax.ppermute(given, axis, [(i, i ^ reach) for i in range(size)]).astype(F32)]
    ppermute x2, waiting for transfers between devices: 16.2 us -> 2.09 us  [body(): send = lambda half: lax.ppermute(half, 'row', up_row)]
    ppermute x4 -> x2, waiting for transfers between devices: 14.7 us -> 3.46 us  [scattered(): got = lax.ppermute(given, axis, [(i, i ^ reach) for i in range(size)])]
    add x4 -> x1, other arithmetic: 3.18 us -> 0.02 us  [scattered(): blocks = kept + got.astype(F32)]
    pallas_call x3, Pallas kernels: 20.7 us -> 17.8 us  [occ(): pl.pallas_call(lambda *refs: occ_kernel(*refs, groups=groups), in_specs=[...]
    add x0 -> x2, other arithmetic: none -> 2.34 us  [scattered(): total + lax.ppermute(given, axis, [(i, i ^ reach) for i in range(size)])....]
  transfers between devices with their start and end apart: 8 -> 12, of which waited for: 5 -> 7; matrix products, arithmetic and copies ran while one was open for 2% -> 2% of each run, Pallas kernels for 28% -> 28%
where the time goes in v4:
time: 138 us
  starting transfers between devices  53.6 us (39%)
  Pallas kernels  49.9 us (36%)
  waiting for transfers between devices  23.8 us (17%)
  local copies, waits for them, and re-layouts  5.48 us (4%)
  other arithmetic  3.15 us (2%)
  between operations  1.59 us (1%)
    ppermute x6, starting transfers between devices, scattered(): lax.ppermute(given, axis, [(i, i ^ reach) for i in range(size)]).astype(F32)  46.6 us
    pallas_call x3, Pallas kernels, product(): pl.pallas_call(lambda *refs: product_kernel(*refs, steps=steps), grid=(le...  18.9 us
    ppermute x6, waiting for transfers between devices, scattered(): lax.ppermute(given, axis, [(i, i ^ reach) for i in range(size)]).astype(F32)  18.3 us
    pallas_call x3, Pallas kernels, occ(): pl.pallas_call(lambda *refs: occ_kernel(*refs, groups=groups), in_specs=[...  17.8 us
    pallas_call x4, Pallas kernels, vir(): pl.pallas_call(lambda *refs: vir_kernel(*refs, n_added=len(added)), grid=...  13.3 us
    unnamed x12, local copies, waits for them, and re-layouts  3.9 us
    ppermute x2, waiting for transfers between devices, scattered(): got = lax.ppermute(given, axis, [(i, i ^ reach) for i in range(size)])  3.46 us
  transfers between devices with their start and end apart: 12, of which 7 were waited for; matrix products, arithmetic and copies ran while one was open for 2% of the time, Pallas kernels for 28%

profile of v4, /device:TPU:0, one launch (start us, length us, event | category | flops | bytes accessed | tf_op | source)
XLA Modules:
  0.0 137.6 jit_solution(4749873606896310152)
XLA Ops:
  1.3 0.7 slice_bitcast_fusion
  2.0 6.4 %occ.3 = bf16[64,64,512]{2,1,0:T(8,128)(2,1)} custom-call(s32[1]{0:T(128)} %bitcast.55.refs_0_, bf16[64,64]{1,0:T(8,128)(2,1)S(1)} %get-tuple-element.10.refs_1_, bf16[640,4096]{1,0:T(8,128)(2,1)} %bitcast.73), custom_call_target="tpu_custom_call" | custom-call | flops 1 | bytes 1 | tf_op jit(solution)/shard_map/occ/pallas_call | solution.py:122
  8.5 1.3 collective-permute-start.5
  9.8 0.0 copy-done.4
  9.8 0.1 copy.11
  9.9 2.8 %vir.4.refs_3_ = bf16[640,2048]{1,0:T(8,128)(2,1)S(1)} custom-call(s32[1]{0:T(128)} %bitcast.56.refs_0_, bf16[64,64]{1,0:T(8,128)(2,1)S(1)} %bitcast.69, bf16[640,4096]{1,0:T(8,128)(2,1)} %bitcast.74, bf16[4096,512]{1,0:T(8,128)(2,1)} %bitcast.7.refs_3_), custom_call_target="tpu_custom_call" | custom-call | flops 1 | bytes 1 | tf_op jit(solution)/shard_map/vir/pallas_call | solution.py:168
  12.7 3.8 %vir.5.refs_3_ = bf16[640,2048]{1,0:T(8,128)(2,1)} custom-call(s32[1]{0:T(128)} %bitcast.57.refs_0_, bf16[64,64]{1,0:T(8,128)(2,1)S(1)} %bitcast.70, bf16[640,4096]{1,0:T(8,128)(2,1)} %bitcast.75, bf16[640,2048]{1,0:T(8,128)(2,1)S(1)} %vir.4.refs_3_), custom_call_target="tpu_custom_call" | custom-call | flops 1 | bytes 1 | tf_op jit(solution)/shard_map/vir/pallas_call | solution.py:168
  16.5 1.3 collective-permute-start.1
  17.8 1.3 collective-permute-start
  19.1 3.7 %occ.4 = bf16[64,64,128]{2,1,0:T(8,128)(2,1)} custom-call(s32[1]{0:T(128)} %bitcast.58.refs_0_, bf16[64,64]{1,0:T(8,128)(2,1)S(1)} %get-tuple-element.10.refs_1_, bf16[640,4096]{1,0:T(8,128)(2,1)} %bitcast.76, bf16[640,2048]{1,0:T(8,128)(2,1)} %vir.5.refs_3_), custom_call_target="tpu_custom_call" | custom-call | flops 1 | bytes 1 | tf_op jit(solution)/shard_map/occ/pallas_call | solution.py:122
  22.8 1.3 collective-permute-start.9
  24.1 7.6 %occ.5 = bf16[64,64,640]{2,1,0:T(8,128)(2,1)} custom-call(s32[1]{0:T(128)} %bitcast.59.refs_0_, bf16[64,64]{1,0:T(8,128)(2,1)S(1)} %get-tuple-element.11.refs_1_, bf16[640,4096]{1,0:T(8,128)(2,1)} %bitcast.77, bf16[4096,128]{1,0:T(8,128)(2,1)} %bitcast.8.refs_3_), custom_call_target="tpu_custom_call" | custom-call | flops 1 | bytes 1 | tf_op jit(solution)/shard_map/occ/pallas_call | solution.py:122
  31.7 0.1 copy.12
  31.8 0.0 collective-permute-done.1.refs_3_
  31.8 3.4 %vir.7.refs_2_ = bf16[640,2048]{1,0:T(8,128)(2,1)S(1)} custom-call(s32[1]{0:T(128)} %bitcast.61.refs_0_, bf16[64,64]{1,0:T(8,128)(2,1)S(1)} %bitcast.71, bf16[640,4096]{1,0:T(8,128)(2,1)} %bitcast.78, bf16[640,2048]{1,0:T(8,128)(2,1)} %collective-permute-done.1.refs_3_, bf16[4096,640]{1,0:T(8,128)(2,1)} %bitcast.80), custom_call_target="tpu_custom_call" | custom-call | flops 1 | bytes 1 | tf_op jit(solution)/shard_map/vir/pallas_call | solution.py:168
  35.3 1.5 %copy-done = bf16[640,2048]{1,0:T(8,128)(2,1)} copy-done((bf16[640,2048]{1,0:T(8,128)(2,1)}, bf16[640,2048]{1,0:T(8,128)(2,1)S(1)}, u32[]{:S(2)}) %copy-start) | copy-done | bytes 2621464
  36.8 0.0 collective-permute-done.refs_3_
  36.8 3.2 %vir.6.refs_1_ = bf16[640,2048]{1,0:T(8,128)(2,1)S(1)} custom-call(s32[1]{0:T(128)} %bitcast.60.refs_0_, bf16[64,64]{1,0:T(8,128)(2,1)S(1)} %bitcast.72, bf16[640,4096]{1,0:T(8,128)(2,1)} %bitcast.79, bf16[640,2048]{1,0:T(8,128)(2,1)} %collective-permute-done.refs_3_, bf16[4096,640]{1,0:T(8,128)(2,1)} %bitcast.81), custom_call_target="tpu_custom_call" | custom-call | flops 1 | bytes 1 | tf_op jit(solution)/shard_map/vir/pallas_call | solution.py:168
  40.0 7.7 %product.3 = f32[640,640]{1,0:T(8,128)S(1)} custom-call(bf16[4096,640]{1,0:T(8,128)(2,1)} %bitcast.82, bf16[640,2048]{1,0:T(8,128)(2,1)S(1)} %vir.6.refs_1_, bf16[640,2048]{1,0:T(8,128)(2,1)} %copy-done), custom_call_target="tpu_custom_call" | custom-call | flops 1 | bytes 1 | tf_op jit(solution)/shard_map/product/pallas_call | solution.py:213
  47.7 0.0 copy-start.1
  47.7 1.2 copy-done.1
  48.9 0.7 fusion.4
  49.6 42.7 %collective-permute-start.2 = (bf16[160,640]{1,0:T(8,128)(2,1)}, bf16[160,640]{1,0:T(8,128)(2,1)S(1)}, u32[]{:S(2)}, u32[]{:S(2)}) collective-permute-start(bf16[160,640]{1,0:T(8,128)(2,1)} %get-tuple-element.2), channel_id=1, source_target_pairs={{0,1},{1,0},{2,3},{3,2},{4,5},{5,4},{6,7},{7,6},{8,9},{9,8},{10,11... | collective-permute-start | bytes 614408 | tf_op jit(solution)/shard_map/ppermute | solution.py:238
  92.4 0.0 collective-permute-start.4
  92.4 1.6 %collective-permute-start.3 = (bf16[160,640]{1,0:T(8,128)(2,1)S(1)}, bf16[160,640]{1,0:T(8,128)(2,1)}, u32[]{:S(2)}, u32[]{:S(2)}) collective-permute-start(bf16[160,640]{1,0:T(8,128)(2,1)S(1)} %get-tuple-element.4), channel_id=1, source_target_pairs={{0,2},{1,3},{2,0},{3,1},{4,6},{5,7},{6,4},{7,5},{8,10},{9,11},{10,... | collective-permute-start | bytes 614408 | tf_op jit(solution)/shard_map/ppermute | solution.py:238
  94.0 0.0 collective-permute-done.2
  94.0 5.6 %collective-permute-done.4 = bf16[160,640]{1,0:T(8,128)(2,1)S(1)} collective-permute-done((bf16[160,640]{1,0:T(8,128)(2,1)S(1)}, bf16[160,640]{1,0:T(8,128)(2,1)S(1)}, u32[]{:S(2)}, u32[]{:S(2)}) %collective-permute-start.4) | collective-permute-done | bytes 204832 | tf_op jit(solution)/shard_map/ppermute | solution.py:238
  99.5 4.7 %collective-permute-done.3 = bf16[160,640]{1,0:T(8,128)(2,1)} collective-permute-done((bf16[160,640]{1,0:T(8,128)(2,1)S(1)}, bf16[160,640]{1,0:T(8,128)(2,1)}, u32[]{:S(2)}, u32[]{:S(2)}) %collective-permute-start.3) | collective-permute-done | bytes 204832 | tf_op jit(solution)/shard_map/ppermute | solution.py:238
  104.2 1.2 fusion.1.refs_3_
  105.4 0.0 copy-start.3
  105.5 0.0 collective-permute-done.5.refs_0_
  105.5 6.6 %product.4 = f32[512,640]{1,0:T(8,128)S(1)} custom-call(bf16[4096,512]{1,0:T(8,128)(2,1)} %collective-permute-done.5.refs_0_, bf16[640,2048]{1,0:T(8,128)(2,1)S(1)} %vir.6.refs_1_, bf16[640,2048]{1,0:T(8,128)(2,1)} %copy-done, f32[160,640]{1,0:T(8,128)S(1)} %fusion.1.refs_3_), custom_call_target="tpu_custom_call" | custom-call | flops 1 | bytes 1 | tf_op jit(solution)/shard_map/product/pallas_call | solution.py:213
  112.0 1.1 copy-done.2
  113.1 0.1 fusion.7
  113.2 0.1 collective-permute-start.6
  113.3 1.6 %collective-permute-start.8 = (bf16[128,640]{1,0:T(8,128)(2,1)S(1)}, bf16[128,640]{1,0:T(8,128)(2,1)S(1)}, u32[]{:S(2)}, u32[]{:S(2)}) collective-permute-start(bf16[128,640]{1,0:T(8,128)(2,1)S(1)} %get-tuple-element.6), channel_id=1, source_target_pairs={{0,3},{1,2},{2,1},{3,0},{4,7},{5,6},{6,5},{7,4},{8,11},{9,10},{10,... | collective-permute-start | bytes 491528 | tf_op jit(solution)/shard_map/ppermute | solution.py:238
  114.9 0.5 collective-permute-start.7
  115.4 0.0 collective-permute-done.6
  115.4 4.0 %collective-permute-done.8 = bf16[128,640]{1,0:T(8,128)(2,1)S(1)} collective-permute-done((bf16[128,640]{1,0:T(8,128)(2,1)S(1)}, bf16[128,640]{1,0:T(8,128)(2,1)S(1)}, u32[]{:S(2)}, u32[]{:S(2)}) %collective-permute-start.8) | collective-permute-done | bytes 163872 | tf_op jit(solution)/shard_map/ppermute | solution.py:238
  119.4 4.0 %collective-permute-done.7 = bf16[128,640]{1,0:T(8,128)(2,1)} collective-permute-done((bf16[128,640]{1,0:T(8,128)(2,1)S(1)}, bf16[128,640]{1,0:T(8,128)(2,1)}, u32[]{:S(2)}, u32[]{:S(2)}) %collective-permute-start.7) | collective-permute-done | bytes 163872 | tf_op jit(solution)/shard_map/ppermute | solution.py:238
  123.4 1.1 fusion.3.refs_3_
  124.6 2.1 %collective-permute-done.9.refs_0_ = bf16[4096,128]{1,0:T(8,128)(2,1)} collective-permute-done((bf16[4096,128]{1,0:T(8,128)(2,1)}, bf16[4096,128]{1,0:T(8,128)(2,1)}, u32[]{:S(2)}, u32[]{:S(2)}) %collective-permute-start.9) | collective-permute-done | bytes 1048608 | tf_op jit(solution)/shard_map/ppermute | solution.py:269
  126.7 4.7 %product.5 = f32[128,640]{1,0:T(8,128)S(1)} custom-call(bf16[4096,128]{1,0:T(8,128)(2,1)} %collective-permute-done.9.refs_0_, bf16[640,2048]{1,0:T(8,128)(2,1)S(1)} %vir.6.refs_1_, bf16[640,2048]{1,0:T(8,128)(2,1)} %copy-done, f32[128,640]{1,0:T(8,128)S(1)} %fusion.3.refs_3_), custom_call_target="tpu_custom_call" | custom-call | flops 1 | bytes 1 | tf_op jit(solution)/shard_map/product/pallas_call | solution.py:213
  131.4 0.1 collective-permute-start.10
  131.5 1.2 collective-permute-done.10
  132.8 1.8 %collective-permute-start.11 = (bf16[1,32,640]{2,1,0:T(8,128)(2,1)S(1)}, bf16[1,32,640]{2,1,0:T(8,128)(2,1)S(1)}, u32[]{:S(2)}, u32[]{:S(2)}) collective-permute-start(bf16[1,32,640]{2,1,0:T(8,128)(2,1)S(1)} %dynamic-slice_convert_fusion.6), channel_id=1, source_target_pairs={{0,2},{1,3},{2,0},{3,1},{4,6},{5,7},{6,4},{7,5},{8,10},{9,11},{10,... | collective-permute-start | bytes 122888 | tf_op jit(solution)/shard_map/ppermute | solution.py:245
  134.6 2.2 %collective-permute-done.11 = bf16[1,32,640]{2,1,0:T(8,128)(2,1)S(1)} collective-permute-done((bf16[1,32,640]{2,1,0:T(8,128)(2,1)S(1)}, bf16[1,32,640]{2,1,0:T(8,128)(2,1)S(1)}, u32[]{:S(2)}, u32[]{:S(2)}) %collective-permute-start.11) | collective-permute-done | bytes 40992 | tf_op jit(solution)/shard_map/ppermute | solution.py:245
  136.8 0.8 maximum_bitcast_fusion
  (9 shorter events, 0.1 us)
Async XLA Ops:
  2.0 7.7 %copy-start.4 = (bf16[1,2,64,64]{3,2,1,0:T(8,128)(2,1)S(1)}, bf16[1,2,64,64]{3,2,1,0:T(8,128)(2,1)}, u32[]{:S(2)}) copy-start(bf16[1,2,64,64]{3,2,1,0:T(8,128)(2,1)} %param.6) | copy-start | bytes 49156
  8.5 97.0 %collective-permute-start.5 = (bf16[4096,512]{1,0:T(8,128)(2,1)}, bf16[4096,512]{1,0:T(8,128)(2,1)}, u32[]{:S(2)}, u32[]{:S(2)}) collective-permute-start(bf16[4096,512]{1,0:T(8,128)(2,1)} %bitcast.7.refs_3_), channel_id=1, source_target_pairs={{4,0},{8,4},{12,8},{16,12},{20,16},{24,20},{28,24},{5,1},{9,5},{13... | collective-permute-start | bytes 12582920 | tf_op jit(solution)/shard_map/ppermute | solution.py:269
  16.5 15.3 %collective-permute-start.1 = (bf16[640,2048]{1,0:T(8,128)(2,1)}, bf16[640,2048]{1,0:T(8,128)(2,1)}, u32[]{:S(2)}, u32[]{:S(2)}) collective-permute-start(bf16[640,2048]{1,0:T(8,128)(2,1)} %vir.5.refs_3_), channel_id=1, source_target_pairs={{1,0},{2,1},{3,2},{5,4},{6,5},{7,6},{9,8},{10,9},{11,10},{13,12},{... | collective-permute-start | bytes 7864328 | tf_op jit(solution)/shard_map/ppermute | solution.py:275
  17.8 19.0 %collective-permute-start = (bf16[640,2048]{1,0:T(8,128)(2,1)S(1)}, bf16[640,2048]{1,0:T(8,128)(2,1)}, u32[]{:S(2)}, u32[]{:S(2)}) collective-permute-start(bf16[640,2048]{1,0:T(8,128)(2,1)S(1)} %vir.4.refs_3_), channel_id=1, source_target_pairs={{1,0},{2,1},{3,2},{5,4},{6,5},{7,6},{9,8},{10,9},{11,10},{13,12},{... | collective-permute-start | bytes 7864328 | tf_op jit(solution)/shard_map/ppermute | solution.py:275
  22.8 103.9 %collective-permute-start.9 = (bf16[4096,128]{1,0:T(8,128)(2,1)}, bf16[4096,128]{1,0:T(8,128)(2,1)}, u32[]{:S(2)}, u32[]{:S(2)}) collective-permute-start(bf16[4096,128]{1,0:T(8,128)(2,1)} %bitcast.8.refs_3_), channel_id=1, source_target_pairs={{4,0},{8,4},{12,8},{16,12},{20,16},{24,20},{28,24},{5,1},{9,5},{13... | collective-permute-start | bytes 3145736 | tf_op jit(solution)/shard_map/ppermute | solution.py:269
  35.3 1.5 %copy-start = (bf16[640,2048]{1,0:T(8,128)(2,1)}, bf16[640,2048]{1,0:T(8,128)(2,1)S(1)}, u32[]{:S(2)}) copy-start(bf16[640,2048]{1,0:T(8,128)(2,1)S(1)} %vir.7.refs_2_) | copy-start | bytes 7864324
  47.7 1.2 copy-start.1
  49.6 44.4 %collective-permute-start.2 = (bf16[160,640]{1,0:T(8,128)(2,1)}, bf16[160,640]{1,0:T(8,128)(2,1)S(1)}, u32[]{:S(2)}, u32[]{:S(2)}) collective-permute-start(bf16[160,640]{1,0:T(8,128)(2,1)} %get-tuple-element.2), channel_id=1, source_target_pairs={{0,1},{1,0},{2,3},{3,2},{4,5},{5,4},{6,7},{7,6},{8,9},{9,8},{10,11... | collective-permute-start | bytes 614408 | tf_op jit(solution)/shard_map/ppermute | solution.py:238
  92.4 7.2 %collective-permute-start.4 = (bf16[160,640]{1,0:T(8,128)(2,1)S(1)}, bf16[160,640]{1,0:T(8,128)(2,1)S(1)}, u32[]{:S(2)}, u32[]{:S(2)}) collective-permute-start(bf16[160,640]{1,0:T(8,128)(2,1)S(1)} %get-tuple-element.3), channel_id=1, source_target_pairs={{0,3},{1,2},{2,1},{3,0},{4,7},{5,6},{6,5},{7,4},{8,11},{9,10},{10,... | collective-permute-start | bytes 614408 | tf_op jit(solution)/shard_map/ppermute | solution.py:238
  92.4 11.9 %collective-permute-start.3 = (bf16[160,640]{1,0:T(8,128)(2,1)S(1)}, bf16[160,640]{1,0:T(8,128)(2,1)}, u32[]{:S(2)}, u32[]{:S(2)}) collective-permute-start(bf16[160,640]{1,0:T(8,128)(2,1)S(1)} %get-tuple-element.4), channel_id=1, source_target_pairs={{0,2},{1,3},{2,0},{3,1},{4,6},{5,7},{6,4},{7,5},{8,10},{9,11},{10,... | collective-permute-start | bytes 614408 | tf_op jit(solution)/shard_map/ppermute | solution.py:238
  105.4 6.6 %copy-start.3 = (f32[160,640]{1,0:T(8,128)}, f32[160,640]{1,0:T(8,128)S(1)}, u32[]{:S(2)}) copy-start(f32[160,640]{1,0:T(8,128)S(1)} %fusion.1.refs_3_) | copy-start | bytes 1228804
  112.0 1.1 copy-start.2
  113.2 2.2 %collective-permute-start.6 = (bf16[128,640]{1,0:T(8,128)(2,1)S(1)}, bf16[128,640]{1,0:T(8,128)(2,1)S(1)}, u32[]{:S(2)}, u32[]{:S(2)}) collective-permute-start(bf16[128,640]{1,0:T(8,128)(2,1)S(1)} %get-tuple-element.5), channel_id=1, source_target_pairs={{0,1},{1,0},{2,3},{3,2},{4,5},{5,4},{6,7},{7,6},{8,9},{9,8},{10,11... | collective-permute-start | bytes 491528 | tf_op jit(solution)/shard_map/ppermute | solution.py:238
  113.3 6.2 %collective-permute-start.8 = (bf16[128,640]{1,0:T(8,128)(2,1)S(1)}, bf16[128,640]{1,0:T(8,128)(2,1)S(1)}, u32[]{:S(2)}, u32[]{:S(2)}) collective-permute-start(bf16[128,640]{1,0:T(8,128)(2,1)S(1)} %get-tuple-element.6), channel_id=1, source_target_pairs={{0,3},{1,2},{2,1},{3,0},{4,7},{5,6},{6,5},{7,4},{8,11},{9,10},{10,... | collective-permute-start | bytes 491528 | tf_op jit(solution)/shard_map/ppermute | solution.py:238
  114.9 8.6 %collective-permute-start.7 = (bf16[128,640]{1,0:T(8,128)(2,1)S(1)}, bf16[128,640]{1,0:T(8,128)(2,1)}, u32[]{:S(2)}, u32[]{:S(2)}) collective-permute-start(bf16[128,640]{1,0:T(8,128)(2,1)S(1)} %get-tuple-element.7), channel_id=1, source_target_pairs={{0,2},{1,3},{2,0},{3,1},{4,6},{5,7},{6,4},{7,5},{8,10},{9,11},{10,... | collective-permute-start | bytes 491528 | tf_op jit(solution)/shard_map/ppermute | solution.py:238
  131.4 1.3 collective-permute-start.10
  132.8 4.1 %collective-permute-start.11 = (bf16[1,32,640]{2,1,0:T(8,128)(2,1)S(1)}, bf16[1,32,640]{2,1,0:T(8,128)(2,1)S(1)}, u32[]{:S(2)}, u32[]{:S(2)}) collective-permute-start(bf16[1,32,640]{2,1,0:T(8,128)(2,1)S(1)} %dynamic-slice_convert_fusion.6), channel_id=1, source_target_pairs={{0,2},{1,3},{2,0},{3,1},{4,6},{5,7},{6,4},{7,5},{8,10},{9,11},{10,... | collective-permute-start | bytes 122888 | tf_op jit(solution)/shard_map/ppermute | solution.py:245

commit v5 on v4

--- a/solution.py
+++ b/solution.py
@@ -10,7 +10,7 @@
 VMEM_BYTES = 48 * 1024 * 1024
 SPAN = 256
 SUBLANES = 8
-SMALL = 128
+CHUNKS = (512, 128)
 PIECES = 2
 
 
@@ -52,9 +52,10 @@
     return [pl.BlockSpec(memory_space=pl.ANY)] * len(before)
 
 
-def occ_kernel(live_ref, g_ref, y_ref, *rest, groups):
-    out_ref, rows_ref, yt_ref, held_ref, in_sems, out_sems = rest[-6:]
-    tile, m = g_ref.shape
+def occ_kernel(live_ref, g_ref, y_ref, *rest, groups, which, cuts):
+    rows_ref, yt_ref, held_ref, in_sems, out_sems = rest[-5:]
+    out_refs = rest[-5 - cuts : -5]
+    tile, m = g_ref.shape[1:]
     size = y_ref.shape[1]
     per = SPAN // tile
     fetch = []
@@ -69,7 +70,7 @@
             to += count
     for copy in fetch:
         copy.start()
-    kron = spread(g_ref[...].T, SUBLANES)
+    kron = spread(g_ref[which].T, SUBLANES)
     live = live_ref[0].astype(F32).astype(BF)
     pair = 2 * SUBLANES
     store = []
@@ -89,12 +90,14 @@
             )
             low, high = (dot(kron, x).reshape(m, SUBLANES, width) for x in (low, high))
             held_ref[:, s * pair : (s + 1) * pair, lanes] = jnp.concatenate([low, high], axis=1).astype(BF)
-        store.append(
-            pltpu.make_async_copy(
-                held_ref.at[:, :, pl.ds(at, width)], out_ref.at[:, :, pl.ds(at, width)], out_sems.at[k]
+        for c, out_ref in enumerate(out_refs):
+            some = pl.ds(c * (m // cuts), m // cuts)
+            store.append(
+                pltpu.make_async_copy(
+                    held_ref.at[some, :, pl.ds(at, width)], out_ref.at[:, :, pl.ds(at, width)], out_sems.at[k, c]
+                )
             )
-        )
-        store[-1].start()
+            store[-1].start()
         at += width
     for copy in store:
         copy.wait()
@@ -113,34 +116,34 @@
     return groups
 
 
-def occ(live, mat, y, slices, before=()):
-    tile, m = mat.shape
+def occ(live, mats, which, y, slices, before=(), cuts=1):
+    tile, m = mats.shape[1:]
     size = y.shape[1]
     groups = grouped(slices)
     width = sum(n for _, n in groups)
     widest = max(n for _, n in groups)
-    out = pl.pallas_call(
-        lambda *refs: occ_kernel(*refs, groups=groups),
+    outs = pl.pallas_call(
+        lambda *refs: occ_kernel(*refs, groups=groups, which=which, cuts=cuts),
         in_specs=[
             pl.BlockSpec(memory_space=pltpu.SMEM),
             pl.BlockSpec(memory_space=pltpu.VMEM),
             pl.BlockSpec(memory_space=pl.ANY),
             *unused(before),
         ],
-        out_specs=pl.BlockSpec(memory_space=pl.ANY),
-        out_shape=jax.ShapeDtypeStruct((m, tile, width), BF),
+        out_specs=[pl.BlockSpec(memory_space=pl.ANY)] * cuts,
+        out_shape=[jax.ShapeDtypeStruct((m // cuts, tile, width), BF)] * cuts,
         scratch_shapes=[
             pltpu.VMEM((width, size), BF),
             pltpu.VMEM((len(groups), tile, tile, widest), BF),
             pltpu.VMEM((m, tile, width), BF),
             pltpu.SemaphoreType.DMA((len(slices),)),
-            pltpu.SemaphoreType.DMA((len(groups),)),
+            pltpu.SemaphoreType.DMA((len(groups), cuts)),
         ],
         compiler_params=params(),
         cost_estimate=cost(2 * width * size * m * SUBLANES, 4 * width * size),
         name="occ",
-    )(live, mat, y, *before)
-    return out.reshape(m * tile, width)
+    )(live, mats, y, *before)
+    return [out.reshape(-1, width) for out in outs]
 
 
 def vir_kernel(live_ref, g_ref, y_ref, *rest, n_added):
@@ -184,43 +187,51 @@
     )(live, mat, y, *added, *before)
 
 
-def product_kernel(x_ref, *rest, steps):
-    z_refs = rest[:PIECES]
+def product_kernel(x_ref, *rest, pieces, steps, started, turn):
+    z_refs = rest[:pieces]
     out_ref, acc_ref = rest[-2:]
     step = pl.program_id(0)
-
-    @pl.when(step == 0)
-    def _():
-        acc_ref[...] = dot(z_refs[0][...], x_ref[...])
-
     for i, z_ref in enumerate(z_refs):
-
-        @pl.when(jnp.logical_and(step > 0, step // steps == i))
-        def _(z_ref=z_ref):
-            acc_ref[...] += dot(z_ref[...], x_ref[...])
+        for first in (True, False) if i == 0 else (False,):
+
+            @pl.when(step == 0 if first else jnp.logical_and(step > 0, step // steps == i))
+            def _(z_ref=z_ref, first=first):
+                got = dot(z_ref[...], x_ref[...])
+                if not first:
+                    got = acc_ref[...] + got
+                elif started:
+                    got = rest[pieces][...] + got
+                acc_ref[...] = got
 
     @pl.when(step == pl.num_programs(0) - 1)
     def _():
-        out_ref[...] = acc_ref[...].T
-
-
-def product(zs, x, before=()):
+        out_ref[...] = acc_ref[...].T if turn else acc_ref[...]
+
+
+def product(zs, x, at=0, so_far=None, turn=True, before=()):
     aux, size = zs[0].shape
     width = x.shape[1]
-    span = 4 * SPAN if size % (4 * SPAN) == 0 else SPAN
+    span = next(n * SPAN for n in (8, 4, 1) if size % (n * SPAN) == 0)
     steps = size // span
     piece = lambda k: pl.BlockSpec((aux, span), lambda i: (0, jnp.clip(i - k * steps, 0, steps - 1)))
+    added = [] if so_far is None else [so_far]
+    shape = (width, aux) if turn else (aux, width)
     return pl.pallas_call(
-        lambda *refs: product_kernel(*refs, steps=steps),
+        lambda *refs: product_kernel(*refs, pieces=len(zs), steps=steps, started=bool(added), turn=turn),
         grid=(len(zs) * steps,),
-        in_specs=[pl.BlockSpec((span, width), lambda i: (i, 0)), *(piece(k) for k in range(len(zs))), *unused(before)],
-        out_specs=pl.BlockSpec((width, aux), lambda i: (0, 0)),
-        out_shape=jax.ShapeDtypeStruct((width, aux), F32),
+        in_specs=[
+            pl.BlockSpec((span, width), lambda i: (at // span + i, 0)),
+            *(piece(k) for k in range(len(zs))),
+            *[pl.BlockSpec((aux, width), lambda i: (0, 0))] * len(added),
+            *unused(before),
+        ],
+        out_specs=pl.BlockSpec(shape, lambda i: (0, 0)),
+        out_shape=jax.ShapeDtypeStruct(shape, F32),
         scratch_shapes=[pltpu.VMEM((aux, width), F32)],
         compiler_params=params(),
         cost_estimate=cost(2 * aux * size * width, 2 * size * (aux + width)),
         name="product",
-    )(x, *zs, *before)
+    )(x, *zs, *added, *before)
 
 
 def scattered(parts, axis, direct):
@@ -249,9 +260,9 @@
 
 def chunks_of(aux, owners):
     each = aux // owners
-    small = SMALL // owners
-    if owners * small == SMALL and small % 16 == 0 and each % 16 == 0 and each > small:
-        cuts = [0, each - small, each]
+    parts = [n // owners for n in CHUNKS]
+    if aux == sum(CHUNKS) and all(n % (16 * owners) == 0 for n in CHUNKS):
+        cuts = [sum(parts[:i]) for i in range(len(parts) + 1)]
         return [[(j * each + a, b - a) for j in range(owners)] for a, b in zip(cuts, cuts[1:])]
     return [[(0, aux)]]
 
@@ -259,33 +270,44 @@
 def body(three_centre, green_occ, green_vir, pair_live):
     rows, cols = lax.axis_size("row"), lax.axis_size("col")
     y = three_centre[0, 0]
-    aux = y.shape[0]
+    aux, size = y.shape
     live = pair_live[0]
     up_row = [(i, i - 1) for i in range(1, rows)]
     up_col = [(i, i - 1) for i in range(1, cols)]
-    to_own, to_lower = green_occ[0, 0], green_occ[0, 1]
-
-    first, *others = chunks_of(aux, cols)
+
+    *wide, final = chunks_of(aux, cols)
     send = lambda half: lax.ppermute(half, "row", up_row)
-    last = occ(live, to_lower, y, first)
-    above = [send(last)]
+    above = []
+    last = ()
+    for part in wide[:1]:
+        last = occ(live, green_occ[0], 1, y, part)
+        above.append(send(last[0]))
     shifted = []
     for i in range(PIECES):
-        last = vir(live, green_vir[0, 1].T, y, i, before=(last,))
-        shifted.append(lax.ppermute(last, "col", up_col))
-    for part in others:
-        last = occ(live, to_lower, y, part, before=(last,))
-        above.append(send(last))
-    own = occ(live, to_own, y, [(i, min(SPAN, aux - i)) for i in range(0, aux, SPAN)], before=(last,))
+        last = [vir(live, green_vir[0, 1].T, y, i, before=last)]
+        shifted.append(lax.ppermute(last[0], "col", up_col))
+    for part in wide[1:]:
+        last = occ(live, green_occ[0], 1, y, part, before=last)
+        above.append(send(last[0]))
+    last = occ(live, green_occ[0], 1, y, final, before=last, cuts=PIECES)
+    ending = [send(half) for half in last]
+    spans = [(i, min(SPAN, aux - i)) for i in range(0, aux, SPAN)]
+    (own,) = last = occ(live, green_occ[0], 0, y, spans, before=last[:1])
     zs = []
+    diag = None
     for i in range(PIECES):
-        zs.append(vir(live, green_vir[0, 0].T, y, i, (shifted[i],), before=(own,)))
-    chi_d = scattered([product(zs, own)], "col", True)
+        zs.append(vir(live, green_vir[0, 0].T, y, i, (shifted[i],), before=last))
+        diag = product(zs[-1:], own, i * (size // PIECES), diag, i == PIECES - 1)
+        last = [diag]
+    last = chi_d = scattered([diag], "col", True)
     blocks = []
-    last = chi_d
     for half in above:
-        last = scattered([product(zs, half, before=(last,))], "col", half is not above[-1])
+        last = scattered([product(zs, half, before=[last])], "col", True)
         blocks.append(last)
+    ended = None
+    for i, half in enumerate(ending):
+        ended = product(zs[i : i + 1], half, 0, ended, i == PIECES - 1, before=[last])
+    blocks.append(scattered([ended], "col", False))
     return chi_d[None], jnp.concatenate(blocks)[None]
 
 

time: 138 us -> 136 us (0.986)
  local copies, waits for them, and re-layouts: 5.48 us -> 12.3 us
  waiting for transfers between devices: 23.8 us -> 19.4 us
  starting transfers between devices: 53.6 us -> 50.6 us
  Pallas kernels: 49.9 us -> 47.9 us
    unnamed x12 -> x26, local copies, waits for them, and re-layouts: 3.9 us -> 11.4 us
    ppermute x6, waiting for transfers between devices: 18.3 us -> 12.6 us  [scattered(): lax.ppermute(given, axis, [(i, i ^ reach) for i in range(size)]).astype(F32)]
    ppermute x6, starting transfers between devices: 46.6 us -> 41.9 us  [scattered(): lax.ppermute(given, axis, [(i, i ^ reach) for i in range(size)]).astype(F32)]
    pallas_call x6 -> x8, Pallas kernels: 36.7 us -> 34.8 us  [the longest x5 17.6 us: product(): pl.pallas_call(lambda *refs: product_kernel(*refs, pieces=len(zs), steps=...]
    ppermute x2 -> x3, starting transfers between devices: 2.58 us -> 4.09 us  [body(): send = lambda half: lax.ppermute(half, 'row', up_row)]
    ppermute x2 -> x3, waiting for transfers between devices: 2.09 us -> 3.32 us  [body(): send = lambda half: lax.ppermute(half, 'row', up_row)]
  transfers between devices with their start and end apart: 12 -> 13, of which waited for: 7 -> 7; matrix products, arithmetic and copies ran while one was open for 2% -> 2% of each run, Pallas kernels for 28% -> 29%
where the time goes in v5:
time: 136 us; the launch traced here: 135 us
  starting transfers between devices  50.6 us (37%)
  Pallas kernels  47.9 us (35%)
  waiting for transfers between devices  19.4 us (14%)
  local copies, waits for them, and re-layouts  12.3 us (9%)
  other arithmetic  3.15 us (2%)
  between operations  1.62 us (1%)
    ppermute x6, starting transfers between devices, scattered(): lax.ppermute(given, axis, [(i, i ^ reach) for i in range(size)]).astype(F32)  41.9 us
    pallas_call x5, Pallas kernels, product(): pl.pallas_call(lambda *refs: product_kernel(*refs, pieces=len(zs), steps=...  17.6 us
    pallas_call x3, Pallas kernels, occ(): pl.pallas_call(lambda *refs: occ_kernel(*refs, groups=groups, which=which...  17.2 us
    pallas_call x4, Pallas kernels, vir(): pl.pallas_call(lambda *refs: vir_kernel(*refs, n_added=len(added)), grid=...  13.1 us
    ppermute x6, waiting for transfers between devices, scattered(): lax.ppermute(given, axis, [(i, i ^ reach) for i in range(size)]).astype(F32)  12.6 us
    unnamed x26, local copies, waits for them, and re-layouts  11.4 us
    ppermute x3, starting transfers between devices, body(): send = lambda half: lax.ppermute(half, 'row', up_row)  4.09 us
    ppermute x2, waiting for transfers between devices, scattered(): got = lax.ppermute(given, axis, [(i, i ^ reach) for i in range(size)])  3.46 us
  transfers between devices with their start and end apart: 13, of which 7 were waited for; matrix products, arithmetic and copies ran while one was open for 2% of the time, Pallas kernels for 29%

profile of v5, /device:TPU:0, one launch (start us, length us, event | category | flops | bytes accessed | tf_op | source)
XLA Modules:
  0.0 134.9 jit_solution(8272578740752826060)
XLA Ops:
  1.3 0.0 copy-start.9
  1.3 0.7 copy-done.9
  2.0 6.4 %occ.3 = bf16[64,64,512]{2,1,0:T(8,128)(2,1)} custom-call(s32[1]{0:T(128)} %bitcast.53.refs_0_, bf16[2,64,64]{2,1,0:T(8,128)(2,1)S(1)} %bitcast.70, bf16[640,4096]{1,0:T(8,128)(2,1)} %bitcast.77), custom_call_target="tpu_custom_call" | custom-call | flops 1 | bytes 1 | tf_op jit(solution)/shard_map/occ/pallas_call | solution.py:125
  8.5 1.3 collective-permute-start.5
  9.8 0.1 copy.11
  9.9 2.8 %vir.4.refs_3_ = bf16[640,2048]{1,0:T(8,128)(2,1)S(1)} custom-call(s32[1]{0:T(128)} %bitcast.54.refs_0_, bf16[64,64]{1,0:T(8,128)(2,1)S(1)} %bitcast.73, bf16[640,4096]{1,0:T(8,128)(2,1)} %bitcast.78, bf16[4096,512]{1,0:T(8,128)(2,1)} %bitcast.6.refs_3_), custom_call_target="tpu_custom_call" | custom-call | flops 1 | bytes 1 | tf_op jit(solution)/shard_map/vir/pallas_call | solution.py:171
  12.7 1.3 collective-permute-start.1
  14.0 3.8 %vir.5.refs_3_ = bf16[640,2048]{1,0:T(8,128)(2,1)} custom-call(s32[1]{0:T(128)} %bitcast.55.refs_0_, bf16[64,64]{1,0:T(8,128)(2,1)S(1)} %bitcast.74, bf16[640,4096]{1,0:T(8,128)(2,1)} %bitcast.79, bf16[640,2048]{1,0:T(8,128)(2,1)S(1)} %vir.4.refs_3_), custom_call_target="tpu_custom_call" | custom-call | flops 1 | bytes 1 | tf_op jit(solution)/shard_map/vir/pallas_call | solution.py:171
  17.8 1.5 %collective-permute-start = (bf16[640,2048]{1,0:T(8,128)(2,1)}, bf16[640,2048]{1,0:T(8,128)(2,1)}, u32[]{:S(2)}, u32[]{:S(2)}) collective-permute-start(bf16[640,2048]{1,0:T(8,128)(2,1)} %vir.5.refs_3_), channel_id=1, source_target_pairs={{1,0},{2,1},{3,2},{5,4},{6,5},{7,6},{9,8},{10,9},{11,10},{13,12},{... | collective-permute-start | bytes 7864328 | tf_op jit(solution)/shard_map/ppermute | solution.py:288
  19.3 3.7 %occ.4 = (bf16[32,64,128]{2,1,0:T(8,128)(2,1)}, bf16[32,64,128]{2,1,0:T(8,128)(2,1)}) custom-call(s32[1]{0:T(128)} %bitcast.56.refs_0_, bf16[2,64,64]{2,1,0:T(8,128)(2,1)S(1)} %bitcast.71, bf16[640,4096]{1,0:T(8,128)(2,1)} %bitcast.80, bf16[640,2048]{1,0:T(8,128)(2,1)} %vir.5.refs_3_), custom_call_target="tpu_custom_call" | custom-call | flops 1 | bytes 1 | tf_op jit(solution)/shard_map/occ/pallas_call | solution.py:125
  23.0 7.1 %occ.5 = bf16[64,64,640]{2,1,0:T(8,128)(2,1)S(1)} custom-call(s32[1]{0:T(128)} %bitcast.57.refs_0_, bf16[2,64,64]{2,1,0:T(8,128)(2,1)S(1)} %bitcast.72, bf16[640,4096]{1,0:T(8,128)(2,1)} %bitcast.81, bf16[2048,128]{1,0:T(8,128)(2,1)} %bitcast.7.refs_3_), custom_call_target="tpu_custom_call" | custom-call | flops 1 | bytes 1 | tf_op jit(solution)/shard_map/occ/pallas_call | solution.py:125
  30.1 2.3 %copy-done = bf16[64,64,640]{2,1,0:T(8,128)(2,1)} copy-done((bf16[64,64,640]{2,1,0:T(8,128)(2,1)}, bf16[64,64,640]{2,1,0:T(8,128)(2,1)S(1)}, u32[]{:S(2)}) %copy-start) | copy-done | bytes 5242904
  32.4 0.1 copy.12
  32.5 3.2 %vir.6.refs_1_ = bf16[640,2048]{1,0:T(8,128)(2,1)S(1)} custom-call(s32[1]{0:T(128)} %bitcast.58.refs_0_, bf16[64,64]{1,0:T(8,128)(2,1)S(1)} %bitcast.75, bf16[640,4096]{1,0:T(8,128)(2,1)} %bitcast.82, bf16[640,2048]{1,0:T(8,128)(2,1)} %collective-permute-done.1.refs_3_, bf16[4096,640]{1,0:T(8,128)(2,1)} %bitcast.60), custom_call_target="tpu_custom_call" | custom-call | flops 1 | bytes 1 | tf_op jit(solution)/shard_map/vir/pallas_call | solution.py:171
  35.8 3.9 %product.5.refs_4_.refs_2_ = f32[640,640]{1,0:T(8,128)S(1)} custom-call(bf16[4096,640]{1,0:T(8,128)(2,1)} %bitcast.61, bf16[640,2048]{1,0:T(8,128)(2,1)S(1)} %vir.6.refs_1_), custom_call_target="tpu_custom_call" | custom-call | flops 1 | bytes 1 | tf_op jit(solution)/shard_map/product/pallas_call | solution.py:219
  39.7 3.3 %vir.7.refs_1_.refs_2_ = bf16[640,2048]{1,0:T(8,128)(2,1)S(1)} custom-call(s32[1]{0:T(128)} %bitcast.59.refs_0_, bf16[64,64]{1,0:T(8,128)(2,1)S(1)} %bitcast.76, bf16[640,4096]{1,0:T(8,128)(2,1)} %bitcast.83, bf16[640,2048]{1,0:T(8,128)(2,1)} %collective-permute-done.refs_3_, f32[640,640]{1,0:T(8,128)S(1)} %product.5.refs_4_.refs_2_), custom_call_target="tpu_custom_call" | custom-call | flops 1 | bytes 1 | tf_op jit(solution)/shard_map/vir/pallas_call | solution.py:171
  43.0 1.5 %copy-done.1 = bf16[640,2048]{1,0:T(8,128)(2,1)} copy-done((bf16[640,2048]{1,0:T(8,128)(2,1)}, bf16[640,2048]{1,0:T(8,128)(2,1)S(1)}, u32[]{:S(2)}) %copy-start.1) | copy-done | bytes 2621464
  44.5 1.2 copy-done.4
  45.7 1.7 %copy-done.2 = bf16[640,2048]{1,0:T(8,128)(2,1)S(1)} copy-done((bf16[640,2048]{1,0:T(8,128)(2,1)S(1)}, bf16[640,2048]{1,0:T(8,128)(2,1)}, u32[]{:S(2)}) %copy-start.2) | copy-done | bytes 2621464
  47.4 1.4 %copy-done.5 = f32[640,640]{1,0:T(8,128)S(1)} copy-done((f32[640,640]{1,0:T(8,128)S(1)}, f32[640,640]{1,0:T(8,128)}, u32[]{:S(2)}) %copy-start.5) | copy-done | bytes 1638424
  48.9 4.0 %product.6 = f32[640,640]{1,0:T(8,128)S(1)} custom-call(bf16[4096,640]{1,0:T(8,128)(2,1)} %bitcast.62, bf16[640,2048]{1,0:T(8,128)(2,1)S(1)} %copy-done.2, f32[640,640]{1,0:T(8,128)S(1)} %copy-done.5), custom_call_target="tpu_custom_call" | custom-call | flops 1 | bytes 1 | tf_op jit(solution)/shard_map/product/pallas_call | solution.py:219
  52.9 1.2 copy-done.6
  54.1 0.7 fusion.4
  54.8 6.5 %collective-permute-start.4 = (bf16[160,640]{1,0:T(8,128)(2,1)}, bf16[160,640]{1,0:T(8,128)(2,1)S(1)}, u32[]{:S(2)}, u32[]{:S(2)}) collective-permute-start(bf16[160,640]{1,0:T(8,128)(2,1)} %get-tuple-element.7), channel_id=1, source_target_pairs={{0,3},{1,2},{2,1},{3,0},{4,7},{5,6},{6,5},{7,4},{8,11},{9,10},{10,... | collective-permute-start | bytes 614408 | tf_op jit(solution)/shard_map/ppermute | solution.py:249
  61.3 33.1 %collective-permute-start.3 = (bf16[160,640]{1,0:T(8,128)(2,1)S(1)}, bf16[160,640]{1,0:T(8,128)(2,1)S(1)}, u32[]{:S(2)}, u32[]{:S(2)}) collective-permute-start(bf16[160,640]{1,0:T(8,128)(2,1)S(1)} %get-tuple-element.8), channel_id=1, source_target_pairs={{0,2},{1,3},{2,0},{3,1},{4,6},{5,7},{6,4},{7,5},{8,10},{9,11},{10,... | collective-permute-start | bytes 614408 | tf_op jit(solution)/shard_map/ppermute | solution.py:249
  94.4 1.3 collective-permute-start.10
  95.7 1.5 %collective-permute-start.9 = (bf16[2048,128]{1,0:T(8,128)(2,1)}, bf16[2048,128]{1,0:T(8,128)(2,1)}, u32[]{:S(2)}, u32[]{:S(2)}) collective-permute-start(bf16[2048,128]{1,0:T(8,128)(2,1)} %bitcast.23), channel_id=1, source_target_pairs={{4,0},{8,4},{12,8},{16,12},{20,16},{24,20},{28,24},{5,1},{9,5},{13... | collective-permute-start | bytes 1572872 | tf_op jit(solution)/shard_map/ppermute | solution.py:279
  97.3 4.8 %collective-permute-done.3 = bf16[160,640]{1,0:T(8,128)(2,1)S(1)} collective-permute-done((bf16[160,640]{1,0:T(8,128)(2,1)S(1)}, bf16[160,640]{1,0:T(8,128)(2,1)S(1)}, u32[]{:S(2)}, u32[]{:S(2)}) %collective-permute-start.3) | collective-permute-done | bytes 204832 | tf_op jit(solution)/shard_map/ppermute | solution.py:249
  102.0 1.2 fusion.1.refs_3_
  103.2 0.0 copy-start.8
  103.3 1.8 %collective-permute-done.5.refs_0_ = bf16[4096,512]{1,0:T(8,128)(2,1)} collective-permute-done((bf16[4096,512]{1,0:T(8,128)(2,1)}, bf16[4096,512]{1,0:T(8,128)(2,1)}, u32[]{:S(2)}, u32[]{:S(2)}) %collective-permute-start.5) | collective-permute-done | bytes 4194336 | tf_op jit(solution)/shard_map/ppermute | solution.py:279
  105.0 5.9 %product.7 = f32[512,640]{1,0:T(8,128)S(1)} custom-call(bf16[4096,512]{1,0:T(8,128)(2,1)} %collective-permute-done.5.refs_0_, bf16[640,2048]{1,0:T(8,128)(2,1)S(1)} %vir.6.refs_1_, bf16[640,2048]{1,0:T(8,128)(2,1)} %copy-done.1, f32[160,640]{1,0:T(8,128)S(1)} %fusion.1.refs_3_), custom_call_target="tpu_custom_call" | custom-call | flops 1 | bytes 1 | tf_op jit(solution)/shard_map/product/pallas_call | solution.py:219
  110.9 1.1 copy-done.7
  112.0 0.1 fusion.7
  112.1 0.1 collective-permute-start.8
  112.1 2.1 %collective-permute-start.7 = (bf16[128,640]{1,0:T(8,128)(2,1)S(1)}, bf16[128,640]{1,0:T(8,128)(2,1)S(1)}, u32[]{:S(2)}, u32[]{:S(2)}) collective-permute-start(bf16[128,640]{1,0:T(8,128)(2,1)S(1)} %get-tuple-element.11), channel_id=1, source_target_pairs={{0,2},{1,3},{2,0},{3,1},{4,6},{5,7},{6,4},{7,5},{8,10},{9,11},{10,... | collective-permute-start | bytes 491528 | tf_op jit(solution)/shard_map/ppermute | solution.py:249
  114.3 0.0 collective-permute-start.6
  114.3 3.7 %collective-permute-done.8 = bf16[128,640]{1,0:T(8,128)(2,1)S(1)} collective-permute-done((bf16[128,640]{1,0:T(8,128)(2,1)S(1)}, bf16[128,640]{1,0:T(8,128)(2,1)S(1)}, u32[]{:S(2)}, u32[]{:S(2)}) %collective-permute-start.8) | collective-permute-done | bytes 163872 | tf_op jit(solution)/shard_map/ppermute | solution.py:249
  118.0 4.1 %collective-permute-done.7 = bf16[128,640]{1,0:T(8,128)(2,1)S(1)} collective-permute-done((bf16[128,640]{1,0:T(8,128)(2,1)S(1)}, bf16[128,640]{1,0:T(8,128)(2,1)S(1)}, u32[]{:S(2)}, u32[]{:S(2)}) %collective-permute-start.7) | collective-permute-done | bytes 163872 | tf_op jit(solution)/shard_map/ppermute | solution.py:249
  122.1 1.1 fusion.3.refs_2_.refs_3_
  123.3 1.9 %product.8.refs_2_ = f32[640,128]{1,0:T(8,128)S(1)} custom-call(bf16[2048,128]{1,0:T(8,128)(2,1)} %collective-permute-done.10.refs_0_, bf16[640,2048]{1,0:T(8,128)(2,1)S(1)} %vir.6.refs_1_, f32[128,640]{1,0:T(8,128)S(1)} %fusion.3.refs_2_.refs_3_), custom_call_target="tpu_custom_call" | custom-call | flops 1 | bytes 1 | tf_op jit(solution)/shard_map/product/pallas_call | solution.py:219
  125.2 1.5 %collective-permute-done.9.refs_0_ = bf16[2048,128]{1,0:T(8,128)(2,1)} collective-permute-done((bf16[2048,128]{1,0:T(8,128)(2,1)}, bf16[2048,128]{1,0:T(8,128)(2,1)}, u32[]{:S(2)}, u32[]{:S(2)}) %collective-permute-start.9) | collective-permute-done | bytes 524320 | tf_op jit(solution)/shard_map/ppermute | solution.py:279
  126.7 2.0 %product.9 = f32[128,640]{1,0:T(8,128)S(1)} custom-call(bf16[2048,128]{1,0:T(8,128)(2,1)} %collective-permute-done.9.refs_0_, bf16[640,2048]{1,0:T(8,128)(2,1)S(1)} %copy-done.3, f32[640,128]{1,0:T(8,128)S(1)} %product.8.refs_2_, f32[128,640]{1,0:T(8,128)S(1)} %fusion.3.refs_2_.refs_3_), custom_call_target="tpu_custom_call" | custom-call | flops 1 | bytes 1 | tf_op jit(solution)/shard_map/product/pallas_call | solution.py:219
  128.7 0.1 collective-permute-start.11
  128.8 1.2 collective-permute-done.11
  130.1 1.8 %collective-permute-start.12 = (bf16[1,32,640]{2,1,0:T(8,128)(2,1)S(1)}, bf16[1,32,640]{2,1,0:T(8,128)(2,1)S(1)}, u32[]{:S(2)}, u32[]{:S(2)}) collective-permute-start(bf16[1,32,640]{2,1,0:T(8,128)(2,1)S(1)} %dynamic-slice_convert_fusion.6), channel_id=1, source_target_pairs={{0,2},{1,3},{2,0},{3,1},{4,6},{5,7},{6,4},{7,5},{8,10},{9,11},{10,... | collective-permute-start | bytes 122888 | tf_op jit(solution)/shard_map/ppermute | solution.py:256
  131.9 2.2 %collective-permute-done.12 = bf16[1,32,640]{2,1,0:T(8,128)(2,1)S(1)} collective-permute-done((bf16[1,32,640]{2,1,0:T(8,128)(2,1)S(1)}, bf16[1,32,640]{2,1,0:T(8,128)(2,1)S(1)}, u32[]{:S(2)}, u32[]{:S(2)}) %collective-permute-start.12) | collective-permute-done | bytes 40992 | tf_op jit(solution)/shard_map/ppermute | solution.py:256
  134.1 0.8 maximum_bitcast_fusion
  (26 shorter events, 0.1 us)
Async XLA Ops:
  1.3 0.8 copy-start.9
  2.0 7.8 %copy-start.11 = (bf16[1,2,64,64]{3,2,1,0:T(8,128)(2,1)S(1)}, bf16[1,2,64,64]{3,2,1,0:T(8,128)(2,1)}, u32[]{:S(2)}) copy-start(bf16[1,2,64,64]{3,2,1,0:T(8,128)(2,1)} %param.6) | copy-start | bytes 49156
  8.5 96.6 %collective-permute-start.5 = (bf16[4096,512]{1,0:T(8,128)(2,1)}, bf16[4096,512]{1,0:T(8,128)(2,1)}, u32[]{:S(2)}, u32[]{:S(2)}) collective-permute-start(bf16[4096,512]{1,0:T(8,128)(2,1)} %bitcast.6.refs_3_), channel_id=1, source_target_pairs={{4,0},{8,4},{12,8},{16,12},{20,16},{24,20},{28,24},{5,1},{9,5},{13... | collective-permute-start | bytes 12582920 | tf_op jit(solution)/shard_map/ppermute | solution.py:279
  12.7 19.8 %collective-permute-start.1 = (bf16[640,2048]{1,0:T(8,128)(2,1)S(1)}, bf16[640,2048]{1,0:T(8,128)(2,1)}, u32[]{:S(2)}, u32[]{:S(2)}) collective-permute-start(bf16[640,2048]{1,0:T(8,128)(2,1)S(1)} %vir.4.refs_3_), channel_id=1, source_target_pairs={{1,0},{2,1},{3,2},{5,4},{6,5},{7,6},{9,8},{10,9},{11,10},{13,12},{... | collective-permute-start | bytes 7864328 | tf_op jit(solution)/shard_map/ppermute | solution.py:288
  14.0 5.3 %copy-start.10 = (bf16[1,2,64,64]{3,2,1,0:T(8,128)(2,1)S(1)}, bf16[1,2,64,64]{3,2,1,0:T(8,128)(2,1)}, u32[]{:S(2)}) copy-start(bf16[1,2,64,64]{3,2,1,0:T(8,128)(2,1)} %param.5) | copy-start | bytes 49156
  17.8 21.9 %collective-permute-start = (bf16[640,2048]{1,0:T(8,128)(2,1)}, bf16[640,2048]{1,0:T(8,128)(2,1)}, u32[]{:S(2)}, u32[]{:S(2)}) collective-permute-start(bf16[640,2048]{1,0:T(8,128)(2,1)} %vir.5.refs_3_), channel_id=1, source_target_pairs={{1,0},{2,1},{3,2},{5,4},{6,5},{7,6},{9,8},{10,9},{11,10},{13,12},{... | collective-permute-start | bytes 7864328 | tf_op jit(solution)/shard_map/ppermute | solution.py:288
  30.1 2.3 %copy-start = (bf16[64,64,640]{2,1,0:T(8,128)(2,1)}, bf16[64,64,640]{2,1,0:T(8,128)(2,1)S(1)}, u32[]{:S(2)}) copy-start(bf16[64,64,640]{2,1,0:T(8,128)(2,1)S(1)} %occ.5) | copy-start | bytes 15728644
  43.0 1.5 %copy-start.1 = (bf16[640,2048]{1,0:T(8,128)(2,1)}, bf16[640,2048]{1,0:T(8,128)(2,1)S(1)}, u32[]{:S(2)}) copy-start(bf16[640,2048]{1,0:T(8,128)(2,1)S(1)} %vir.7.refs_1_.refs_2_) | copy-start | bytes 7864324
  44.5 1.2 copy-start.4
  45.7 1.7 %copy-start.2 = (bf16[640,2048]{1,0:T(8,128)(2,1)S(1)}, bf16[640,2048]{1,0:T(8,128)(2,1)}, u32[]{:S(2)}) copy-start(bf16[640,2048]{1,0:T(8,128)(2,1)} %copy-done.1) | copy-start | bytes 7864324
  47.4 1.4 %copy-start.5 = (f32[640,640]{1,0:T(8,128)S(1)}, f32[640,640]{1,0:T(8,128)}, u32[]{:S(2)}) copy-start(f32[640,640]{1,0:T(8,128)} %copy-done.4) | copy-start | bytes 4915204
  52.9 1.2 copy-start.6
  54.8 40.9 %collective-permute-start.4 = (bf16[160,640]{1,0:T(8,128)(2,1)}, bf16[160,640]{1,0:T(8,128)(2,1)S(1)}, u32[]{:S(2)}, u32[]{:S(2)}) collective-permute-start(bf16[160,640]{1,0:T(8,128)(2,1)} %get-tuple-element.7), channel_id=1, source_target_pairs={{0,3},{1,2},{2,1},{3,0},{4,7},{5,6},{6,5},{7,4},{8,11},{9,10},{10,... | collective-permute-start | bytes 614408 | tf_op jit(solution)/shard_map/ppermute | solution.py:249
  61.3 40.7 %collective-permute-start.3 = (bf16[160,640]{1,0:T(8,128)(2,1)S(1)}, bf16[160,640]{1,0:T(8,128)(2,1)S(1)}, u32[]{:S(2)}, u32[]{:S(2)}) collective-permute-start(bf16[160,640]{1,0:T(8,128)(2,1)S(1)} %get-tuple-element.8), channel_id=1, source_target_pairs={{0,2},{1,3},{2,0},{3,1},{4,6},{5,7},{6,4},{7,5},{8,10},{9,11},{10,... | collective-permute-start | bytes 614408 | tf_op jit(solution)/shard_map/ppermute | solution.py:249
  94.4 7.6 %collective-permute-start.2 = (bf16[160,640]{1,0:T(8,128)(2,1)S(1)}, bf16[160,640]{1,0:T(8,128)(2,1)}, u32[]{:S(2)}, u32[]{:S(2)}) collective-permute-start(bf16[160,640]{1,0:T(8,128)(2,1)S(1)} %get-tuple-element.6), channel_id=1, source_target_pairs={{0,1},{1,0},{2,3},{3,2},{4,5},{5,4},{6,7},{7,6},{8,9},{9,8},{10,11... | collective-permute-start | bytes 614408 | tf_op jit(solution)/shard_map/ppermute | solution.py:249
  94.4 28.8 %collective-permute-start.10 = (bf16[2048,128]{1,0:T(8,128)(2,1)}, bf16[2048,128]{1,0:T(8,128)(2,1)}, u32[]{:S(2)}, u32[]{:S(2)}) collective-permute-start(bf16[2048,128]{1,0:T(8,128)(2,1)} %bitcast.7.refs_3_), channel_id=1, source_target_pairs={{4,0},{8,4},{12,8},{16,12},{20,16},{24,20},{28,24},{5,1},{9,5},{13... | collective-permute-start | bytes 1572872 | tf_op jit(solution)/shard_map/ppermute | solution.py:279
  95.7 30.9 %collective-permute-start.9 = (bf16[2048,128]{1,0:T(8,128)(2,1)}, bf16[2048,128]{1,0:T(8,128)(2,1)}, u32[]{:S(2)}, u32[]{:S(2)}) collective-permute-start(bf16[2048,128]{1,0:T(8,128)(2,1)} %bitcast.23), channel_id=1, source_target_pairs={{4,0},{8,4},{12,8},{16,12},{20,16},{24,20},{28,24},{5,1},{9,5},{13... | collective-permute-start | bytes 1572872 | tf_op jit(solution)/shard_map/ppermute | solution.py:279
  103.2 7.7 %copy-start.8 = (f32[160,640]{1,0:T(8,128)}, f32[160,640]{1,0:T(8,128)S(1)}, u32[]{:S(2)}) copy-start(f32[160,640]{1,0:T(8,128)S(1)} %fusion.1.refs_3_) | copy-start | bytes 1228804
  110.9 1.1 copy-start.7
  112.1 6.0 %collective-permute-start.8 = (bf16[128,640]{1,0:T(8,128)(2,1)S(1)}, bf16[128,640]{1,0:T(8,128)(2,1)S(1)}, u32[]{:S(2)}, u32[]{:S(2)}) collective-permute-start(bf16[128,640]{1,0:T(8,128)(2,1)S(1)} %get-tuple-element.10), channel_id=1, source_target_pairs={{0,3},{1,2},{2,1},{3,0},{4,7},{5,6},{6,5},{7,4},{8,11},{9,10},{10,... | collective-permute-start | bytes 491528 | tf_op jit(solution)/shard_map/ppermute | solution.py:249
  112.1 10.0 %collective-permute-start.7 = (bf16[128,640]{1,0:T(8,128)(2,1)S(1)}, bf16[128,640]{1,0:T(8,128)(2,1)S(1)}, u32[]{:S(2)}, u32[]{:S(2)}) collective-permute-start(bf16[128,640]{1,0:T(8,128)(2,1)S(1)} %get-tuple-element.11), channel_id=1, source_target_pairs={{0,2},{1,3},{2,0},{3,1},{4,6},{5,7},{6,4},{7,5},{8,10},{9,11},{10,... | collective-permute-start | bytes 491528 | tf_op jit(solution)/shard_map/ppermute | solution.py:249
  114.3 7.9 %collective-permute-start.6 = (bf16[128,640]{1,0:T(8,128)(2,1)S(1)}, bf16[128,640]{1,0:T(8,128)(2,1)}, u32[]{:S(2)}, u32[]{:S(2)}) collective-permute-start(bf16[128,640]{1,0:T(8,128)(2,1)S(1)} %get-tuple-element.9), channel_id=1, source_target_pairs={{0,1},{1,0},{2,3},{3,2},{4,5},{5,4},{6,7},{7,6},{8,9},{9,8},{10,11... | collective-permute-start | bytes 491528 | tf_op jit(solution)/shard_map/ppermute | solution.py:249
  114.3 12.4 %copy-start.3 = (bf16[640,2048]{1,0:T(8,128)(2,1)S(1)}, bf16[640,2048]{1,0:T(8,128)(2,1)}, u32[]{:S(2)}) copy-start(bf16[640,2048]{1,0:T(8,128)(2,1)} %copy-done.1) | copy-start | bytes 7864324
  128.7 1.3 collective-permute-start.11
  130.1 4.1 %collective-permute-start.12 = (bf16[1,32,640]{2,1,0:T(8,128)(2,1)S(1)}, bf16[1,32,640]{2,1,0:T(8,128)(2,1)S(1)}, u32[]{:S(2)}, u32[]{:S(2)}) collective-permute-start(bf16[1,32,640]{2,1,0:T(8,128)(2,1)S(1)} %dynamic-slice_convert_fusion.6), channel_id=1, source_target_pairs={{0,2},{1,3},{2,0},{3,1},{4,6},{5,7},{6,4},{7,5},{8,10},{9,11},{10,... | collective-permute-start | bytes 122888 | tf_op jit(solution)/shard_map/ppermute | solution.py:256

commit v6 on v5

--- a/solution.py
+++ b/solution.py
@@ -10,8 +10,9 @@
 VMEM_BYTES = 48 * 1024 * 1024
 SPAN = 256
 SUBLANES = 8
-CHUNKS = (512, 128)
+CHUNKS = (384, 256)
 PIECES = 2
+IN_STEPS = 4
 
 
 def dot(a, b, dims=((1,), (0,))):
@@ -52,12 +53,28 @@
     return [pl.BlockSpec(memory_space=pl.ANY)] * len(before)
 
 
+def occ_group(kron, yt_ref, held_ref, part_of, lanes, size):
+    m, tile, _ = held_ref.shape
+    width = lanes.stop - lanes.start
+    per = SPAN // tile
+    for j in range(size // SPAN):
+        turned = part_of(slice(j * SPAN, (j + 1) * SPAN)).T
+        yt_ref[j * per : (j + 1) * per, :, :width] = turned.reshape(per, tile, width)
+    pair = 2 * SUBLANES
+    for s in range(tile // pair):
+        part = yt_ref[:, s * pair : (s + 1) * pair, :width].astype(F32)
+        low, high = (
+            part[:, i : i + SUBLANES].reshape(tile * SUBLANES, width).astype(BF) for i in (0, SUBLANES)
+        )
+        low, high = (dot(kron, x).reshape(m, SUBLANES, width) for x in (low, high))
+        held_ref[:, s * pair : (s + 1) * pair, lanes] = jnp.concatenate([low, high], axis=1).astype(BF)
+
+
 def occ_kernel(live_ref, g_ref, y_ref, *rest, groups, which, cuts):
     rows_ref, yt_ref, held_ref, in_sems, out_sems = rest[-5:]
     out_refs = rest[-5 - cuts : -5]
-    tile, m = g_ref.shape[1:]
+    m = g_ref.shape[2]
     size = y_ref.shape[1]
-    per = SPAN // tile
     fetch = []
     to = 0
     for slices, _ in groups:
@@ -72,7 +89,6 @@
         copy.start()
     kron = spread(g_ref[which].T, SUBLANES)
     live = live_ref[0].astype(F32).astype(BF)
-    pair = 2 * SUBLANES
     store = []
     at, done = 0, 0
     for k, (slices, width) in enumerate(groups):
@@ -80,16 +96,7 @@
             copy.wait()
         done += len(slices)
         lanes = slice(at, at + width)
-        for j in range(size // SPAN):
-            part = rows_ref[lanes, j * SPAN : (j + 1) * SPAN] * live
-            yt_ref[k, j * per : (j + 1) * per, :, :width] = part.T.reshape(per, tile, width)
-        for s in range(tile // pair):
-            part = yt_ref[k, :, s * pair : (s + 1) * pair, :width].astype(F32)
-            low, high = (
-                part[:, i : i + SUBLANES].reshape(tile * SUBLANES, width).astype(BF) for i in (0, SUBLANES)
-            )
-            low, high = (dot(kron, x).reshape(m, SUBLANES, width) for x in (low, high))
-            held_ref[:, s * pair : (s + 1) * pair, lanes] = jnp.concatenate([low, high], axis=1).astype(BF)
+        occ_group(kron, yt_ref.at[k], held_ref, lambda span: rows_ref[lanes, span] * live, lanes, size)
         for c, out_ref in enumerate(out_refs):
             some = pl.ds(c * (m // cuts), m // cuts)
             store.append(
@@ -101,6 +108,145 @@
         at += width
     for copy in store:
         copy.wait()
+
+
+def raw_kernel(live_ref, g_ref, y_ref, out_ref, rows_ref, tile_ref, tail_ref, in_sems, out_sems, *, slices):
+    count, size = rows_ref.shape
+    tile = tile_ref.shape[0]
+    tail, wide = tail_ref.shape
+    blocks = size // wide
+    fetch = []
+    to = 0
+    for i, (start, n) in enumerate(slices):
+        fetch.append(pltpu.make_async_copy(y_ref.at[pl.ds(start, n)], rows_ref.at[pl.ds(to, n)], in_sems.at[i]))
+        to += n
+    for copy in fetch:
+        copy.start()
+    fetch_tile = pltpu.make_async_copy(g_ref.at[1], tile_ref, in_sems.at[len(slices)])
+    fetch_tile.start()
+    live = live_ref[0].astype(F32).astype(BF)
+    store = []
+    to = 0
+    for k, (_, n) in enumerate(slices):
+        fetch[k].wait()
+        rows_ref[to : to + n] = rows_ref[to : to + n] * live
+        for i in range(blocks):
+            store.append(
+                pltpu.make_async_copy(
+                    rows_ref.at[pl.ds(to, n), pl.ds(i * wide, wide)],
+                    out_ref.at[pl.ds(i * count + to, n)],
+                    out_sems.at[k * blocks + i],
+                )
+            )
+            store[-1].start()
+        to += n
+    fetch_tile.wait()
+    tail_ref[...] = jnp.zeros((tail, wide), BF)
+    for i in range(tile // tail):
+        tail_ref[:, i * 128 : i * 128 + tile] = tile_ref[i * tail : (i + 1) * tail]
+    store.append(
+        pltpu.make_async_copy(tail_ref, out_ref.at[pl.ds(count * blocks, tail)], out_sems.at[len(slices) * blocks])
+    )
+    store[-1].start()
+    for copy in store:
+        copy.wait()
+
+
+RAW_TAIL = 16
+
+
+def raw_shape(count, size, tile):
+    wide = 128 * (tile // RAW_TAIL)
+    return count * (size // wide) + RAW_TAIL, wide
+
+
+def raw(live, mats, y, slices):
+    count = sum(n for _, n in slices)
+    size = y.shape[1]
+    tile = mats.shape[1]
+    shape = raw_shape(count, size, tile)
+    some = pl.BlockSpec(memory_space=pl.ANY)
+    return pl.pallas_call(
+        lambda *refs: raw_kernel(*refs, slices=slices),
+        in_specs=[pl.BlockSpec(memory_space=pltpu.SMEM), some, some],
+        out_specs=some,
+        out_shape=jax.ShapeDtypeStruct(shape, BF),
+        scratch_shapes=[
+            pltpu.VMEM((count, size), BF),
+            pltpu.VMEM((tile, tile), BF),
+            pltpu.VMEM((RAW_TAIL, shape[1]), BF),
+            pltpu.SemaphoreType.DMA((len(slices) + 1,)),
+            pltpu.SemaphoreType.DMA((len(slices) * (size // shape[1]) + 1,)),
+        ],
+        compiler_params=params(),
+        cost_estimate=cost(count * size, 4 * count * size),
+        name="raw",
+    )(live, mats, y)
+
+
+def raw_product_kernel(r_ref, *rest):
+    z_refs = rest[:PIECES]
+    out_ref, g_ref, yt_ref, held_ref, z_held, rows_ref, tail_ref, sems = rest[-8:]
+    tile, _, count = yt_ref.shape
+    size = tile * tile
+    wide = r_ref.shape[1]
+    blocks = size // wide
+    part = size // PIECES
+    fetch_tail = pltpu.make_async_copy(r_ref.at[pl.ds(blocks * count, RAW_TAIL)], tail_ref, sems.at[PIECES])
+    fetch_tail.start()
+    fetch_rows = [
+        pltpu.make_async_copy(r_ref.at[pl.ds(i * count, count)], rows_ref.at[i], sems.at[PIECES + 1 + i])
+        for i in range(blocks)
+    ]
+    fetch = [pltpu.make_async_copy(z_refs[i], z_held.at[i], sems.at[i]) for i in range(PIECES)]
+    for copy in fetch_rows + fetch:
+        copy.start()
+    fetch_tail.wait()
+    for i in range(tile // RAW_TAIL):
+        g_ref[i * RAW_TAIL : (i + 1) * RAW_TAIL] = tail_ref[:, i * 128 : i * 128 + tile]
+    kron = spread(g_ref[...].T, SUBLANES)
+
+    def part_of(span):
+        block, at = divmod(span.start, wide)
+        if at == 0:
+            fetch_rows[block].wait()
+        return rows_ref[block, :, at : at + SPAN]
+
+    occ_group(kron, yt_ref, held_ref, part_of, slice(0, count), size)
+    total = None
+    for i in range(PIECES):
+        fetch[i].wait()
+        rows = slice(i * (tile // PIECES), (i + 1) * (tile // PIECES))
+        got = dot(z_held[i], held_ref[rows].reshape(part, count))
+        total = got if total is None else total + got
+    out_ref[...] = total.T
+
+
+def raw_product(received, zs, tile, before=()):
+    size = tile * tile
+    count = (received.shape[0] - RAW_TAIL) * received.shape[1] // size
+    aux = zs[0].shape[0]
+    return pl.pallas_call(
+        raw_product_kernel,
+        in_specs=[
+            *[pl.BlockSpec(memory_space=pl.ANY)] * (1 + len(zs)),
+            *unused(before),
+        ],
+        out_specs=pl.BlockSpec(memory_space=pltpu.VMEM),
+        out_shape=jax.ShapeDtypeStruct((count, aux), F32),
+        scratch_shapes=[
+            pltpu.VMEM((tile, tile), BF),
+            pltpu.VMEM((tile, tile, count), BF),
+            pltpu.VMEM((tile, tile, count), BF),
+            pltpu.VMEM((PIECES, aux, size // PIECES), BF),
+            pltpu.VMEM((size // received.shape[1], count, received.shape[1]), BF),
+            pltpu.VMEM((RAW_TAIL, received.shape[1]), BF),
+            pltpu.SemaphoreType.DMA((PIECES + 1 + size // received.shape[1],)),
+        ],
+        compiler_params=params(),
+        cost_estimate=cost(2 * count * size * (tile * SUBLANES + aux), 2 * size * (aux + count)),
+        name="raw_product",
+    )(received, *zs, *before)
 
 
 def grouped(slices):
@@ -143,7 +289,190 @@
         cost_estimate=cost(2 * width * size * m * SUBLANES, 4 * width * size),
         name="occ",
     )(live, mats, y, *before)
-    return [out.reshape(-1, width) for out in outs]
+    return outs[0].reshape(-1, width)
+
+
+def both_kernel(live_ref, go_ref, gv_ref, y_ref, *rest, slices):
+    rows_ref, yt_ref, half_ref, over_ref, in_sems, out_sems = rest[-6:]
+    outs = rest[-6 - 2 * PIECES : -6]
+    half_outs, over_outs = outs[:PIECES], outs[PIECES:]
+    aux, size = y_ref.shape
+    step = aux // IN_STEPS
+    fetch = []
+    for i in range(IN_STEPS):
+        at = pl.ds(i * step, step)
+        fetch.append(pltpu.make_async_copy(y_ref.at[at], rows_ref.at[at], in_sems.at[i]))
+    for copy in fetch:
+        copy.start()
+    scale = live_ref[0].astype(F32)
+    live = scale.astype(BF)
+    occ_kron = spread(go_ref[1].T, SUBLANES)
+    vir_kron = (repeated(gv_ref[1].T, SPAN // gv_ref.shape[1]).astype(F32) * scale).astype(BF)
+    for copy in fetch:
+        copy.wait()
+    store = []
+    for c, out in enumerate(over_outs):
+        wide = size // PIECES
+        for j in range(wide // SPAN):
+            at = c * wide + j * SPAN
+            over_ref[c, :, j * SPAN : (j + 1) * SPAN] = dot(rows_ref[:, at : at + SPAN], vir_kron).astype(BF)
+        store.append(pltpu.make_async_copy(over_ref.at[c], out, out_sems.at[PIECES + c]))
+        store[-1].start()
+
+    def part_of(span):
+        parts = [rows_ref[start : start + count, span] for start, count in slices]
+        return (jnp.concatenate(parts, axis=0) if len(parts) > 1 else parts[0]) * live
+
+    occ_group(occ_kron, yt_ref, half_ref, part_of, slice(0, yt_ref.shape[2]), size)
+    some = half_ref.shape[0] // PIECES
+    for c, out in enumerate(half_outs):
+        store.append(pltpu.make_async_copy(half_ref.at[pl.ds(c * some, some)], out, out_sems.at[c]))
+        store[-1].start()
+    for copy in store:
+        copy.wait()
+
+
+def both(live, green_occ, green_vir, y, slices, before=()):
+    aux, size = y.shape
+    tile = green_occ.shape[1]
+    width = sum(count for _, count in slices)
+    whole = pl.BlockSpec(memory_space=pltpu.VMEM)
+    some = pl.BlockSpec(memory_space=pl.ANY)
+    outs = pl.pallas_call(
+        lambda *refs: both_kernel(*refs, slices=slices),
+        in_specs=[pl.BlockSpec(memory_space=pltpu.SMEM), whole, whole, some, *unused(before)],
+        out_specs=[some] * (2 * PIECES),
+        out_shape=[jax.ShapeDtypeStruct((tile // PIECES, tile, width), BF)] * PIECES
+        + [jax.ShapeDtypeStruct((aux, size // PIECES), BF)] * PIECES,
+        scratch_shapes=[
+            pltpu.VMEM((aux, size), BF),
+            pltpu.VMEM((tile, tile, width), BF),
+            pltpu.VMEM((tile, tile, width), BF),
+            pltpu.VMEM((PIECES, aux, size // PIECES), BF),
+            pltpu.SemaphoreType.DMA((IN_STEPS,)),
+            pltpu.SemaphoreType.DMA((2 * PIECES,)),
+        ],
+        compiler_params=params(),
+        cost_estimate=cost(2 * width * size * tile * SUBLANES, 8 * aux * size),
+        name="both_halves",
+    )(live, green_occ, green_vir, y, *before)
+    return [half.reshape(-1, width) for half in outs[:PIECES]], outs[PIECES:]
+
+
+def fold_kernel(live_ref, g_ref, y_ref, shifted_ref, own_ref, *rest, started, turn):
+    z_ref, out_ref, kron_ref, acc_ref = rest[-4:]
+    step = pl.program_id(0)
+
+    @pl.when(step == 0)
+    def _():
+        scale = live_ref[0].astype(F32)
+        kron_ref[...] = (repeated(g_ref[0].T, SPAN // g_ref.shape[1]).astype(F32) * scale).astype(BF)
+        acc_ref[...] = rest[0][...] if started else jnp.zeros(acc_ref.shape, F32)
+
+    for j in range(y_ref.shape[1] // SPAN):
+        at = slice(j * SPAN, (j + 1) * SPAN)
+        z_ref[:, at] = (dot(y_ref[:, at], kron_ref[...]) + shifted_ref[:, at].astype(F32)).astype(BF)
+    acc_ref[...] += dot(z_ref[...], own_ref[...])
+
+    @pl.when(step == pl.num_programs(0) - 1)
+    def _():
+        out_ref[...] = acc_ref[...].T if turn else acc_ref[...]
+
+
+def fold(live, mats, y, piece, shifted, own, so_far, turn, before=()):
+    aux = y.shape[0]
+    size = y.shape[1] // PIECES
+    span = 4 * SPAN if size % (4 * SPAN) == 0 else SPAN
+    steps = size // span
+    block = pl.BlockSpec((aux, span), lambda i: (0, i))
+    whole = pl.BlockSpec((aux, aux), lambda i: (0, 0))
+    added = [] if so_far is None else [so_far]
+    return pl.pallas_call(
+        lambda *refs: fold_kernel(*refs, started=bool(added), turn=turn),
+        grid=(steps,),
+        in_specs=[
+            pl.BlockSpec(memory_space=pltpu.SMEM),
+            pl.BlockSpec(mats.shape, lambda i: (0, 0, 0)),
+            pl.BlockSpec((aux, span), lambda i: (0, piece * steps + i)),
+            block,
+            pl.BlockSpec((span, aux), lambda i: (piece * steps + i, 0)),
+            *[whole] * len(added),
+            *unused(before),
+        ],
+        out_specs=[block, whole],
+        out_shape=[jax.ShapeDtypeStruct((aux, size), BF), jax.ShapeDtypeStruct((aux, aux), F32)],
+        scratch_shapes=[pltpu.VMEM((SPAN, SPAN), BF), pltpu.VMEM((aux, aux), F32)],
+        compiler_params=params(),
+        cost_estimate=cost(2 * aux * size * (SPAN + aux), 2 * 4 * aux * size),
+        name="fold",
+    )(live, mats, y, shifted, own, *added, *before)
+
+
+def both_kernel(live_ref, go_ref, gv_ref, y_ref, *rest, slices):
+    rows_ref, yt_ref, half_ref, over_ref, in_sems, out_sems = rest[-6:]
+    outs = rest[-6 - 2 * PIECES : -6]
+    half_outs, over_outs = outs[:PIECES], outs[PIECES:]
+    aux, size = y_ref.shape
+    step = aux // IN_STEPS
+    fetch = []
+    for i in range(IN_STEPS):
+        at = pl.ds(i * step, step)
+        fetch.append(pltpu.make_async_copy(y_ref.at[at], rows_ref.at[at], in_sems.at[i]))
+    for copy in fetch:
+        copy.start()
+    scale = live_ref[0].astype(F32)
+    live = scale.astype(BF)
+    occ_kron = spread(go_ref[1].T, SUBLANES)
+    vir_kron = (repeated(gv_ref[1].T, SPAN // gv_ref.shape[1]).astype(F32) * scale).astype(BF)
+    for copy in fetch:
+        copy.wait()
+    store = []
+    for c, out in enumerate(over_outs):
+        wide = size // PIECES
+        for j in range(wide // SPAN):
+            at = c * wide + j * SPAN
+            over_ref[c, :, j * SPAN : (j + 1) * SPAN] = dot(rows_ref[:, at : at + SPAN], vir_kron).astype(BF)
+        store.append(pltpu.make_async_copy(over_ref.at[c], out, out_sems.at[PIECES + c]))
+        store[-1].start()
+
+    def part_of(span):
+        parts = [rows_ref[start : start + count, span] for start, count in slices]
+        return (jnp.concatenate(parts, axis=0) if len(parts) > 1 else parts[0]) * live
+
+    occ_group(occ_kron, yt_ref, half_ref, part_of, slice(0, yt_ref.shape[2]), size)
+    some = half_ref.shape[0] // PIECES
+    for c, out in enumerate(half_outs):
+        store.append(pltpu.make_async_copy(half_ref.at[pl.ds(c * some, some)], out, out_sems.at[c]))
+        store[-1].start()
+    for copy in store:
+        copy.wait()
+
+
+def both(live, green_occ, green_vir, y, slices, before=()):
+    aux, size = y.shape
+    tile = green_occ.shape[1]
+    width = sum(count for _, count in slices)
+    whole = pl.BlockSpec(memory_space=pltpu.VMEM)
+    some = pl.BlockSpec(memory_space=pl.ANY)
+    outs = pl.pallas_call(
+        lambda *refs: both_kernel(*refs, slices=slices),
+        in_specs=[pl.BlockSpec(memory_space=pltpu.SMEM), whole, whole, some, *unused(before)],
+        out_specs=[some] * (2 * PIECES),
+        out_shape=[jax.ShapeDtypeStruct((tile // PIECES, tile, width), BF)] * PIECES
+        + [jax.ShapeDtypeStruct((aux, size // PIECES), BF)] * PIECES,
+        scratch_shapes=[
+            pltpu.VMEM((aux, size), BF),
+            pltpu.VMEM((tile, tile, width), BF),
+            pltpu.VMEM((tile, tile, width), BF),
+            pltpu.VMEM((PIECES, aux, size // PIECES), BF),
+            pltpu.SemaphoreType.DMA((IN_STEPS,)),
+            pltpu.SemaphoreType.DMA((2 * PIECES,)),
+        ],
+        compiler_params=params(),
+        cost_estimate=cost(2 * width * size * tile * SUBLANES, 8 * aux * size),
+        name="both_halves",
+    )(live, green_occ, green_vir, y, *before)
+    return [half.reshape(-1, width) for half in outs[:PIECES]], outs[PIECES:]
 
 
 def vir_kernel(live_ref, g_ref, y_ref, *rest, n_added):
@@ -275,38 +604,34 @@
     up_row = [(i, i - 1) for i in range(1, rows)]
     up_col = [(i, i - 1) for i in range(1, cols)]
 
-    *wide, final = chunks_of(aux, cols)
     send = lambda half: lax.ppermute(half, "row", up_row)
-    above = []
+    chunks = chunks_of(aux, cols)
+    chunked = len(chunks) > 1
     last = ()
-    for part in wide[:1]:
-        last = occ(live, green_occ[0], 1, y, part)
-        above.append(send(last[0]))
-    shifted = []
-    for i in range(PIECES):
-        last = [vir(live, green_vir[0, 1].T, y, i, before=last)]
-        shifted.append(lax.ppermute(last[0], "col", up_col))
-    for part in wide[1:]:
-        last = occ(live, green_occ[0], 1, y, part, before=last)
-        above.append(send(last[0]))
-    last = occ(live, green_occ[0], 1, y, final, before=last, cuts=PIECES)
-    ending = [send(half) for half in last]
+    if chunked:
+        last = [raw(live, green_occ[0], y, chunks[0])]
+        unfolded = send(last[0])
+    halves, over = both(live, green_occ[0], green_vir[0], y, chunks[-1], last)
+    shifted = [lax.ppermute(piece, "col", up_col) for piece in over]
+    ending = [send(half) for half in halves]
     spans = [(i, min(SPAN, aux - i)) for i in range(0, aux, SPAN)]
-    (own,) = last = occ(live, green_occ[0], 0, y, spans, before=last[:1])
+    own = occ(live, green_occ[0], 0, y, spans, before=halves[:1])
     zs = []
     diag = None
     for i in range(PIECES):
-        zs.append(vir(live, green_vir[0, 0].T, y, i, (shifted[i],), before=last))
-        diag = product(zs[-1:], own, i * (size // PIECES), diag, i == PIECES - 1)
-        last = [diag]
-    last = chi_d = scattered([diag], "col", True)
-    blocks = []
-    for half in above:
-        last = scattered([product(zs, half, before=[last])], "col", True)
-        blocks.append(last)
+        z, diag = fold(live, green_vir[0], y, i, shifted[i], own, diag, i == PIECES - 1)
+        zs.append(z)
+    blocks, order = [], [[diag]] * PIECES
+    if chunked:
+        early = raw_product(unfolded, zs, green_occ.shape[2], before=[diag])
+        both_done = scattered([diag, early], "col", True)
+        chi_d, blocks = both_done[: aux // cols], [both_done[aux // cols :]]
+        order = [[early]] * (PIECES - 1) + [[both_done]]
+    else:
+        chi_d = scattered([diag], "col", True)
     ended = None
     for i, half in enumerate(ending):
-        ended = product(zs[i : i + 1], half, 0, ended, i == PIECES - 1, before=[last])
+        ended = product(zs[i : i + 1], half, 0, ended, i == PIECES - 1, before=order[i])
     blocks.append(scattered([ended], "col", False))
     return chi_d[None], jnp.concatenate(blocks)[None]
 

time: 136 us -> 133 us (0.978)
  waiting for transfers between devices: 19.4 us -> 64.4 us
  starting transfers between devices: 50.6 us -> 14.2 us
  local copies, waits for them, and re-layouts: 12.3 us -> 6.28 us
  Pallas kernels: 47.9 us -> 43.4 us
    ppermute x3, waiting for transfers between devices: 3.32 us -> 59.4 us  [body(): send = lambda half: lax.ppermute(half, 'row', up_row)]
    ppermute x6 -> x3, starting transfers between devices: 41.9 us -> 5.8 us  [scattered(): lax.ppermute(given, axis, [(i, i ^ reach) for i in range(size)]).astype(F32)]
    pallas_call x4 -> x5, Pallas kernels: 13.1 us -> 31.6 us  [the longest x2 13.3 us: fold(): pl.pallas_call(lambda *refs: fold_kernel(*refs, started=bool(added), turn...]
    pallas_call x5 -> x2, Pallas kernels: 17.6 us -> 4.2 us  [product(): pl.pallas_call(lambda *refs: product_kernel(*refs, pieces=len(zs), steps=...]
    ppermute x6 -> x3, waiting for transfers between devices: 12.6 us -> 1.76 us  [scattered(): lax.ppermute(given, axis, [(i, i ^ reach) for i in range(size)]).astype(F32)]
    pallas_call x3 -> x1, Pallas kernels: 17.2 us -> 7.59 us  [occ(): pl.pallas_call(lambda *refs: occ_kernel(*refs, groups=groups, which=which...]
    unnamed x26 -> x16, local copies, waits for them, and re-layouts: 11.4 us -> 5.44 us
  transfers between devices with their start and end apart: 13 -> 10, of which waited for: 7 -> 6; matrix products, arithmetic and copies ran while one was open for 2% -> 2% of each run, Pallas kernels for 29% -> 29%
where the time goes in v6:
time: 133 us
  waiting for transfers between devices  64.4 us (48%)
  Pallas kernels  43.4 us (33%)
  starting transfers between devices  14.2 us (11%)
  local copies, waits for them, and re-layouts  6.28 us (5%)
  other arithmetic  3.12 us (2%)
  between operations  1.57 us (1%)
    ppermute x3, waiting for transfers between devices, body(): send = lambda half: lax.ppermute(half, 'row', up_row)  59.4 us
    pallas_call x2, Pallas kernels, fold(): pl.pallas_call(lambda *refs: fold_kernel(*refs, started=bool(added), turn...  13.3 us
    pallas_call x1, Pallas kernels, raw_product(): pl.pallas_call(raw_product_kernel, in_specs=[*[pl.BlockSpec(memory_space=...  8.08 us
    pallas_call x1, Pallas kernels, occ(): pl.pallas_call(lambda *refs: occ_kernel(*refs, groups=groups, which=which...  7.59 us
    pallas_call x1, Pallas kernels, both(): pl.pallas_call(lambda *refs: both_kernel(*refs, slices=slices), in_specs=...  7 us
    ppermute x3, starting transfers between devices, scattered(): lax.ppermute(given, axis, [(i, i ^ reach) for i in range(size)]).astype(F32)  5.8 us
    unnamed x16, local copies, waits for them, and re-layouts  5.44 us
    pallas_call x2, Pallas kernels, product(): pl.pallas_call(lambda *refs: product_kernel(*refs, pieces=len(zs), steps=...  4.2 us
  transfers between devices with their start and end apart: 10, of which 6 were waited for; matrix products, arithmetic and copies ran while one was open for 2% of the time, Pallas kernels for 29%

profile of v6, /device:TPU:0, one launch (start us, length us, event | category | flops | bytes accessed | tf_op | source)
XLA Modules:
  0.0 132.9 jit_solution(9643569215556531336)
XLA Ops:
  1.3 0.0 copy-start.4
  1.3 0.7 copy-done.4
  2.0 0.0 copy-start.5
  2.0 3.3 %raw.1.refs_4_ = bf16[3088,512]{1,0:T(8,128)(2,1)} custom-call(s32[1]{0:T(128)} %bitcast.38.refs_0_, bf16[2,64,64]{2,1,0:T(8,128)(2,1)S(1)} %bitcast.49, bf16[640,4096]{1,0:T(8,128)(2,1)} %bitcast.55), custom_call_target="tpu_custom_call" | custom-call | flops 1 | bytes 1 | tf_op jit(solution)/shard_map/raw/pallas_call | solution.py:169
  5.3 1.3 collective-permute-start.2
  6.6 0.0 copy-done.5
  6.6 7.0 %both_halves.1 = (bf16[32,64,256]{2,1,0:T(8,128)(2,1)}, bf16[32,64,256]{2,1,0:T(8,128)(2,1)}, bf16[640,2048]{1,0:T(8,128)(2,1)S(1)}, bf16[640,2048]{1,0:T(8,128)(2,1)}) custom-call(s32[1]{0:T(128)} %bitcast.39.refs_0_, bf16[2,64,64]{2,1,0:T(8,128)(2,1)S(1)} %bitcast.50, bf16[2,64,64]{2,1,0:T(8,128)(2,1)S(1)} %bitcast.52, bf16[640,4096]{1,0:T(8,128)(2,1)} %bitcast.56, ...), custom_call_target="tpu_custom_call" | custom-call | flops 1 | bytes 1 | tf_op jit(solution)/shard_map/both_halves/pallas_call | solution.py:457
  13.6 1.3 collective-permute-start.1
  14.9 1.3 collective-permute-start
  16.2 1.3 collective-permute-start.7
  17.5 1.3 collective-permute-start.6
  18.8 7.6 %occ.1 = bf16[64,64,640]{2,1,0:T(8,128)(2,1)} custom-call(s32[1]{0:T(128)} %bitcast.40.refs_0_, bf16[2,64,64]{2,1,0:T(8,128)(2,1)S(1)} %bitcast.51, bf16[640,4096]{1,0:T(8,128)(2,1)} %bitcast.57, bf16[2048,256]{1,0:T(8,128)(2,1)} %bitcast.4.refs_3_), custom_call_target="tpu_custom_call" | custom-call | flops 1 | bytes 1 | tf_op jit(solution)/shard_map/occ/pallas_call | solution.py:271
  26.4 0.0 collective-permute-done.1.refs_3_
  26.5 6.1 %fold.2 = (bf16[640,2048]{1,0:T(8,128)(2,1)S(1)}, f32[640,640]{1,0:T(8,128)S(1)}) custom-call(s32[1]{0:T(128)} %bitcast.41.refs_0_, bf16[2,64,64]{2,1,0:T(8,128)(2,1)S(1)} %bitcast.53, bf16[640,4096]{1,0:T(8,128)(2,1)} %bitcast.58, bf16[640,2048]{1,0:T(8,128)(2,1)} %collective-permute-done.1.refs_3_, bf16[4096,640]{1,0:T(8,128)(2,1)} %bitcast.60), custom_call_target="tpu_custom_call" | custom-call | flops 1 | bytes 1 | tf_op jit(solution)/shard_map/fold/pallas_call | solution.py:390
  32.5 0.0 copy-start.2
  32.5 0.0 collective-permute-done.refs_3_
  32.5 7.2 %fold.3 = (bf16[640,2048]{1,0:T(8,128)(2,1)S(1)}, f32[640,640]{1,0:T(8,128)S(1)}) custom-call(s32[1]{0:T(128)} %bitcast.42.refs_0_, bf16[2,64,64]{2,1,0:T(8,128)(2,1)S(1)} %bitcast.54, bf16[640,4096]{1,0:T(8,128)(2,1)} %bitcast.59, bf16[640,2048]{1,0:T(8,128)(2,1)} %collective-permute-done.refs_3_, bf16[4096,640]{1,0:T(8,128)(2,1)} %bitcast.61, ...), custom_call_target="tpu_custom_call" | custom-call | flops 1 | bytes 1 | tf_op jit(solution)/shard_map/fold/pallas_call | solution.py:390
  39.7 0.0 copy-start
  39.8 1.5 %copy-done = bf16[640,2048]{1,0:T(8,128)(2,1)} copy-done((bf16[640,2048]{1,0:T(8,128)(2,1)}, bf16[640,2048]{1,0:T(8,128)(2,1)S(1)}, u32[]{:S(2)}) %copy-start) | copy-done | bytes 2621464
  41.2 38.5 %collective-permute-done.2.r_ref = bf16[3088,512]{1,0:T(8,128)(2,1)} collective-permute-done((bf16[3088,512]{1,0:T(8,128)(2,1)}, bf16[3088,512]{1,0:T(8,128)(2,1)}, u32[]{:S(2)}, u32[]{:S(2)}) %collective-permute-start.2) | collective-permute-done | bytes 3162144 | tf_op jit(solution)/shard_map/ppermute | solution.py:607
  79.7 0.0 copy-done.2
  79.7 8.1 %raw_product.1.refs_2_ = f32[384,640]{1,0:T(8,128)S(1)} custom-call(bf16[3088,512]{1,0:T(8,128)(2,1)} %collective-permute-done.2.r_ref, bf16[640,2048]{1,0:T(8,128)(2,1)S(1)} %get-tuple-element.15.rest_0_.refs_1_, bf16[640,2048]{1,0:T(8,128)(2,1)} %copy-done, f32[640,640]{1,0:T(8,128)S(1)} %get-tuple-element.14.rest_2_), custom_call_target="tpu_custom_call" | custom-call | flops 1 | bytes 1 | tf_op jit(solution)/shard_map/raw_product/pallas_call | solution.py:229
  87.8 1.0 fusion.12
  88.8 4.5 %collective-permute-start.3 = (bf16[256,640]{1,0:T(8,128)(2,1)}, bf16[256,640]{1,0:T(8,128)(2,1)S(1)}, u32[]{:S(2)}, u32[]{:S(2)}) collective-permute-start(bf16[256,640]{1,0:T(8,128)(2,1)} %get-tuple-element.18), channel_id=1, source_target_pairs={{0,1},{1,0},{2,3},{3,2},{4,5},{5,4},{6,7},{7,6},{8,9},{9,8},{10,11... | collective-permute-start | bytes 983048 | tf_op jit(solution)/shard_map/ppermute | solution.py:578
  93.3 0.0 collective-permute-start.4
  93.3 1.4 %collective-permute-start.5 = (bf16[256,640]{1,0:T(8,128)(2,1)}, bf16[256,640]{1,0:T(8,128)(2,1)}, u32[]{:S(2)}, u32[]{:S(2)}) collective-permute-start(bf16[256,640]{1,0:T(8,128)(2,1)} %get-tuple-element.20), channel_id=1, source_target_pairs={{0,3},{1,2},{2,1},{3,0},{4,7},{5,6},{6,5},{7,4},{8,11},{9,10},{10,... | collective-permute-start | bytes 983048 | tf_op jit(solution)/shard_map/ppermute | solution.py:578
  94.6 7.6 %collective-permute-done.7.refs_0_ = bf16[2048,256]{1,0:T(8,128)(2,1)} collective-permute-done((bf16[2048,256]{1,0:T(8,128)(2,1)}, bf16[2048,256]{1,0:T(8,128)(2,1)}, u32[]{:S(2)}, u32[]{:S(2)}) %collective-permute-start.7) | collective-permute-done | bytes 1048608 | tf_op jit(solution)/shard_map/ppermute | solution.py:607
  102.2 0.0 copy-start.3
  102.2 1.7 %copy-done.3 = bf16[640,2048]{1,0:T(8,128)(2,1)S(1)} copy-done((bf16[640,2048]{1,0:T(8,128)(2,1)S(1)}, bf16[640,2048]{1,0:T(8,128)(2,1)}, u32[]{:S(2)}) %copy-start.3) | copy-done | bytes 2621464
  104.0 2.1 %product.2.refs_2_ = f32[640,256]{1,0:T(8,128)S(1)} custom-call(bf16[2048,256]{1,0:T(8,128)(2,1)} %collective-permute-done.7.refs_0_, bf16[640,2048]{1,0:T(8,128)(2,1)S(1)} %copy-done.3, f32[384,640]{1,0:T(8,128)S(1)} %raw_product.1.refs_2_), custom_call_target="tpu_custom_call" | custom-call | flops 1 | bytes 1 | tf_op jit(solution)/shard_map/product/pallas_call | solution.py:548
  106.0 0.0 copy-start.1
  106.0 0.0 collective-permute-done.3
  106.0 0.0 copy-start.6
  106.1 0.0 collective-permute-done.4
  106.1 0.7 copy-done.6
  106.8 0.0 copy-start.7
  106.8 0.7 copy-done.7
  107.5 1.8 %collective-permute-done.5 = bf16[256,640]{1,0:T(8,128)(2,1)} collective-permute-done((bf16[256,640]{1,0:T(8,128)(2,1)}, bf16[256,640]{1,0:T(8,128)(2,1)}, u32[]{:S(2)}, u32[]{:S(2)}) %collective-permute-start.5) | collective-permute-done | bytes 327712 | tf_op jit(solution)/shard_map/ppermute | solution.py:578
  109.3 1.3 fusion.6.refs_3_
  110.6 13.3 %collective-permute-done.6.refs_0_ = bf16[2048,256]{1,0:T(8,128)(2,1)} collective-permute-done((bf16[2048,256]{1,0:T(8,128)(2,1)}, bf16[2048,256]{1,0:T(8,128)(2,1)}, u32[]{:S(2)}, u32[]{:S(2)}) %collective-permute-start.6) | collective-permute-done | bytes 1048608 | tf_op jit(solution)/shard_map/ppermute | solution.py:607
  123.9 0.0 copy-done.1
  123.9 2.1 %product.3 = f32[256,640]{1,0:T(8,128)S(1)} custom-call(bf16[2048,256]{1,0:T(8,128)(2,1)} %collective-permute-done.6.refs_0_, bf16[640,2048]{1,0:T(8,128)(2,1)S(1)} %copy-done.1, f32[640,256]{1,0:T(8,128)S(1)} %product.2.refs_2_, f32[256,640]{1,0:T(8,128)S(1)} %fusion.6.refs_3_), custom_call_target="tpu_custom_call" | custom-call | flops 1 | bytes 1 | tf_op jit(solution)/shard_map/product/pallas_call | solution.py:548
  126.0 0.1 collective-permute-start.8
  126.2 1.3 %collective-permute-done.8 = bf16[2,64,640]{2,1,0:T(8,128)(2,1)S(1)} collective-permute-done((bf16[2,64,640]{2,1,0:T(8,128)(2,1)S(1)}, bf16[2,64,640]{2,1,0:T(8,128)(2,1)S(1)}, u32[]{:S(2)}, u32[]{:S(2)}) %collective-permute-start.8) | collective-permute-done | bytes 163872 | tf_op jit(solution)/shard_map/ppermute | solution.py:585
  127.6 1.8 %collective-permute-start.9 = (bf16[1,64,640]{2,1,0:T(8,128)(2,1)S(1)}, bf16[1,64,640]{2,1,0:T(8,128)(2,1)S(1)}, u32[]{:S(2)}, u32[]{:S(2)}) collective-permute-start(bf16[1,64,640]{2,1,0:T(8,128)(2,1)S(1)} %dynamic-slice_convert_fusion), channel_id=1, source_target_pairs={{0,2},{1,3},{2,0},{3,1},{4,6},{5,7},{6,4},{7,5},{8,10},{9,11},{10,... | collective-permute-start | bytes 245768 | tf_op jit(solution)/shard_map/ppermute | solution.py:585
  129.4 0.8 slice_bitcast_fusion
  130.2 2.0 %collective-permute-done.9 = bf16[1,64,640]{2,1,0:T(8,128)(2,1)S(1)} collective-permute-done((bf16[1,64,640]{2,1,0:T(8,128)(2,1)S(1)}, bf16[1,64,640]{2,1,0:T(8,128)(2,1)S(1)}, u32[]{:S(2)}, u32[]{:S(2)}) %collective-permute-start.9) | collective-permute-done | bytes 81952 | tf_op jit(solution)/shard_map/ppermute | solution.py:585
  132.2 0.8 maximum_bitcast_fusion
  (5 shorter events, 0.1 us)
Async XLA Ops:
  1.3 0.8 copy-start.4
  2.0 4.6 %copy-start.5 = (bf16[1,2,64,64]{3,2,1,0:T(8,128)(2,1)S(1)}, bf16[1,2,64,64]{3,2,1,0:T(8,128)(2,1)}, u32[]{:S(2)}) copy-start(bf16[1,2,64,64]{3,2,1,0:T(8,128)(2,1)} %param.6) | copy-start | bytes 49156
  5.3 74.4 %collective-permute-start.2 = (bf16[3088,512]{1,0:T(8,128)(2,1)}, bf16[3088,512]{1,0:T(8,128)(2,1)}, u32[]{:S(2)}, u32[]{:S(2)}) collective-permute-start(bf16[3088,512]{1,0:T(8,128)(2,1)} %raw.1.refs_4_), channel_id=1, source_target_pairs={{4,0},{8,4},{12,8},{16,12},{20,16},{24,20},{28,24},{5,1},{9,5},{13... | collective-permute-start | bytes 9486344 | tf_op jit(solution)/shard_map/ppermute | solution.py:607
  13.6 12.8 %collective-permute-start.1 = (bf16[640,2048]{1,0:T(8,128)(2,1)S(1)}, bf16[640,2048]{1,0:T(8,128)(2,1)}, u32[]{:S(2)}, u32[]{:S(2)}) collective-permute-start(bf16[640,2048]{1,0:T(8,128)(2,1)S(1)} %get-tuple-element.12), channel_id=1, source_target_pairs={{1,0},{2,1},{3,2},{5,4},{6,5},{7,6},{9,8},{10,9},{11,10},{13,12},{... | collective-permute-start | bytes 7864328 | tf_op jit(solution)/shard_map/ppermute | solution.py:615
  14.9 17.6 %collective-permute-start = (bf16[640,2048]{1,0:T(8,128)(2,1)}, bf16[640,2048]{1,0:T(8,128)(2,1)}, u32[]{:S(2)}, u32[]{:S(2)}) collective-permute-start(bf16[640,2048]{1,0:T(8,128)(2,1)} %get-tuple-element.10), channel_id=1, source_target_pairs={{1,0},{2,1},{3,2},{5,4},{6,5},{7,6},{9,8},{10,9},{11,10},{13,12},{... | collective-permute-start | bytes 7864328 | tf_op jit(solution)/shard_map/ppermute | solution.py:615
  16.2 86.0 %collective-permute-start.7 = (bf16[2048,256]{1,0:T(8,128)(2,1)}, bf16[2048,256]{1,0:T(8,128)(2,1)}, u32[]{:S(2)}, u32[]{:S(2)}) collective-permute-start(bf16[2048,256]{1,0:T(8,128)(2,1)} %bitcast.4.refs_3_), channel_id=1, source_target_pairs={{4,0},{8,4},{12,8},{16,12},{20,16},{24,20},{28,24},{5,1},{9,5},{13... | collective-permute-start | bytes 3145736 | tf_op jit(solution)/shard_map/ppermute | solution.py:607
  17.5 106.3 %collective-permute-start.6 = (bf16[2048,256]{1,0:T(8,128)(2,1)}, bf16[2048,256]{1,0:T(8,128)(2,1)}, u32[]{:S(2)}, u32[]{:S(2)}) collective-permute-start(bf16[2048,256]{1,0:T(8,128)(2,1)} %bitcast.13), channel_id=1, source_target_pairs={{4,0},{8,4},{12,8},{16,12},{20,16},{24,20},{28,24},{5,1},{9,5},{13... | collective-permute-start | bytes 3145736 | tf_op jit(solution)/shard_map/ppermute | solution.py:607
  32.5 47.2 %copy-start.2 = (bf16[640,2048]{1,0:T(8,128)(2,1)}, bf16[640,2048]{1,0:T(8,128)(2,1)S(1)}, u32[]{:S(2)}) copy-start(bf16[640,2048]{1,0:T(8,128)(2,1)S(1)} %get-tuple-element.15.rest_0_.refs_1_) | copy-start | bytes 7864324
  39.7 1.5 %copy-start = (bf16[640,2048]{1,0:T(8,128)(2,1)}, bf16[640,2048]{1,0:T(8,128)(2,1)S(1)}, u32[]{:S(2)}) copy-start(bf16[640,2048]{1,0:T(8,128)(2,1)S(1)} %get-tuple-element.16.rest_1_.refs_1_) | copy-start | bytes 7864324
  88.8 17.2 %collective-permute-start.3 = (bf16[256,640]{1,0:T(8,128)(2,1)}, bf16[256,640]{1,0:T(8,128)(2,1)S(1)}, u32[]{:S(2)}, u32[]{:S(2)}) collective-permute-start(bf16[256,640]{1,0:T(8,128)(2,1)} %get-tuple-element.18), channel_id=1, source_target_pairs={{0,1},{1,0},{2,3},{3,2},{4,5},{5,4},{6,7},{7,6},{8,9},{9,8},{10,11... | collective-permute-start | bytes 983048 | tf_op jit(solution)/shard_map/ppermute | solution.py:578
  93.3 12.8 %collective-permute-start.4 = (bf16[256,640]{1,0:T(8,128)(2,1)}, bf16[256,640]{1,0:T(8,128)(2,1)S(1)}, u32[]{:S(2)}, u32[]{:S(2)}) collective-permute-start(bf16[256,640]{1,0:T(8,128)(2,1)} %get-tuple-element.19), channel_id=1, source_target_pairs={{0,2},{1,3},{2,0},{3,1},{4,6},{5,7},{6,4},{7,5},{8,10},{9,11},{10,... | collective-permute-start | bytes 983048 | tf_op jit(solution)/shard_map/ppermute | solution.py:578
  93.3 16.0 %collective-permute-start.5 = (bf16[256,640]{1,0:T(8,128)(2,1)}, bf16[256,640]{1,0:T(8,128)(2,1)}, u32[]{:S(2)}, u32[]{:S(2)}) collective-permute-start(bf16[256,640]{1,0:T(8,128)(2,1)} %get-tuple-element.20), channel_id=1, source_target_pairs={{0,3},{1,2},{2,1},{3,0},{4,7},{5,6},{6,5},{7,4},{8,11},{9,10},{10,... | collective-permute-start | bytes 983048 | tf_op jit(solution)/shard_map/ppermute | solution.py:578
  102.2 1.7 %copy-start.3 = (bf16[640,2048]{1,0:T(8,128)(2,1)S(1)}, bf16[640,2048]{1,0:T(8,128)(2,1)}, u32[]{:S(2)}) copy-start(bf16[640,2048]{1,0:T(8,128)(2,1)} %copy-done.2) | copy-start | bytes 7864324
  106.0 17.8 %copy-start.1 = (bf16[640,2048]{1,0:T(8,128)(2,1)S(1)}, bf16[640,2048]{1,0:T(8,128)(2,1)}, u32[]{:S(2)}) copy-start(bf16[640,2048]{1,0:T(8,128)(2,1)} %copy-done) | copy-start | bytes 7864324
  106.0 0.7 copy-start.6
  106.8 0.7 copy-start.7
  126.0 1.5 %collective-permute-start.8 = (bf16[2,64,640]{2,1,0:T(8,128)(2,1)S(1)}, bf16[2,64,640]{2,1,0:T(8,128)(2,1)S(1)}, u32[]{:S(2)}, u32[]{:S(2)}) collective-permute-start(bf16[2,64,640]{2,1,0:T(8,128)(2,1)S(1)} %fusion.14), channel_id=1, source_target_pairs={{0,1},{1,0},{2,3},{3,2},{4,5},{5,4},{6,7},{7,6},{8,9},{9,8},{10,11... | collective-permute-start | bytes 491528 | tf_op jit(solution)/shard_map/ppermute | solution.py:585
  127.6 4.6 %collective-permute-start.9 = (bf16[1,64,640]{2,1,0:T(8,128)(2,1)S(1)}, bf16[1,64,640]{2,1,0:T(8,128)(2,1)S(1)}, u32[]{:S(2)}, u32[]{:S(2)}) collective-permute-start(bf16[1,64,640]{2,1,0:T(8,128)(2,1)S(1)} %dynamic-slice_convert_fusion), channel_id=1, source_target_pairs={{0,2},{1,3},{2,0},{3,1},{4,6},{5,7},{6,4},{7,5},{8,10},{9,11},{10,... | collective-permute-start | bytes 245768 | tf_op jit(solution)/shard_map/ppermute | solution.py:585

commit v7 on v6

--- a/solution.py
+++ b/solution.py
@@ -13,6 +13,7 @@
 CHUNKS = (384, 256)
 PIECES = 2
 IN_STEPS = 4
+CUTS = (3, 1)
 
 
 def dot(a, b, dims=((1,), (0,))):
@@ -110,44 +111,39 @@
         copy.wait()
 
 
-def raw_kernel(live_ref, g_ref, y_ref, out_ref, rows_ref, tile_ref, tail_ref, in_sems, out_sems, *, slices):
+def raw_kernel(live_ref, g_ref, y_ref, out_ref, rows_ref, tile_ref, tail_ref, tile_sem, in_sems, out_sems, *, slices):
     count, size = rows_ref.shape
     tile = tile_ref.shape[0]
     tail, wide = tail_ref.shape
     blocks = size // wide
+    fetch_tile = pltpu.make_async_copy(g_ref.at[1], tile_ref, tile_sem)
+    fetch_tile.start()
     fetch = []
     to = 0
     for i, (start, n) in enumerate(slices):
         fetch.append(pltpu.make_async_copy(y_ref.at[pl.ds(start, n)], rows_ref.at[pl.ds(to, n)], in_sems.at[i]))
+        fetch[-1].start()
         to += n
-    for copy in fetch:
-        copy.start()
-    fetch_tile = pltpu.make_async_copy(g_ref.at[1], tile_ref, in_sems.at[len(slices)])
-    fetch_tile.start()
+    fetch_tile.wait()
     live = live_ref[0].astype(F32).astype(BF)
-    store = []
+    tail_ref[...] = jnp.zeros((tail, wide), BF)
+    for i in range(tile // tail):
+        tail_ref[:, i * 128 : i * 128 + tile] = tile_ref[i * tail : (i + 1) * tail] * live
+    store = [pltpu.make_async_copy(tail_ref, out_ref.at[pl.ds(count * blocks, tail)], out_sems.at[0])]
+    store[0].start()
     to = 0
     for k, (_, n) in enumerate(slices):
         fetch[k].wait()
-        rows_ref[to : to + n] = rows_ref[to : to + n] * live
         for i in range(blocks):
             store.append(
                 pltpu.make_async_copy(
                     rows_ref.at[pl.ds(to, n), pl.ds(i * wide, wide)],
                     out_ref.at[pl.ds(i * count + to, n)],
-                    out_sems.at[k * blocks + i],
+                    out_sems.at[len(store)],
                 )
             )
             store[-1].start()
         to += n
-    fetch_tile.wait()
-    tail_ref[...] = jnp.zeros((tail, wide), BF)
-    for i in range(tile // tail):
-        tail_ref[:, i * 128 : i * 128 + tile] = tile_ref[i * tail : (i + 1) * tail]
-    store.append(
-        pltpu.make_async_copy(tail_ref, out_ref.at[pl.ds(count * blocks, tail)], out_sems.at[len(slices) * blocks])
-    )
-    store[-1].start()
     for copy in store:
         copy.wait()
 
@@ -165,7 +161,7 @@
     size = y.shape[1]
     tile = mats.shape[1]
     shape = raw_shape(count, size, tile)
-    some = pl.BlockSpec(memory_space=pl.ANY)
+    some = pl.BlockSpec(memory_space=pltpu.HBM)
     return pl.pallas_call(
         lambda *refs: raw_kernel(*refs, slices=slices),
         in_specs=[pl.BlockSpec(memory_space=pltpu.SMEM), some, some],
@@ -175,7 +171,8 @@
             pltpu.VMEM((count, size), BF),
             pltpu.VMEM((tile, tile), BF),
             pltpu.VMEM((RAW_TAIL, shape[1]), BF),
-            pltpu.SemaphoreType.DMA((len(slices) + 1,)),
+            pltpu.SemaphoreType.DMA(()),
+            pltpu.SemaphoreType.DMA((len(slices),)),
             pltpu.SemaphoreType.DMA((len(slices) * (size // shape[1]) + 1,)),
         ],
         compiler_params=params(),
@@ -293,9 +290,9 @@
 
 
 def both_kernel(live_ref, go_ref, gv_ref, y_ref, *rest, slices):
-    rows_ref, yt_ref, half_ref, over_ref, in_sems, out_sems = rest[-6:]
-    outs = rest[-6 - 2 * PIECES : -6]
-    half_outs, over_outs = outs[:PIECES], outs[PIECES:]
+    rows_ref, yt_ref, half_ref, over_ref, tiles_ref, in_sems, out_sems = rest[-7:]
+    outs = rest[-7 - len(CUTS) - PIECES : -7]
+    half_outs, over_outs = outs[: len(CUTS)], outs[len(CUTS) :]
     aux, size = y_ref.shape
     step = aux // IN_STEPS
     fetch = []
@@ -304,10 +301,15 @@
         fetch.append(pltpu.make_async_copy(y_ref.at[at], rows_ref.at[at], in_sems.at[i]))
     for copy in fetch:
         copy.start()
+    tiles = [pltpu.make_async_copy(g.at[1], tiles_ref.at[i], in_sems.at[IN_STEPS + i]) for i, g in enumerate((go_ref, gv_ref))]
+    for copy in tiles:
+        copy.start()
     scale = live_ref[0].astype(F32)
     live = scale.astype(BF)
-    occ_kron = spread(go_ref[1].T, SUBLANES)
-    vir_kron = (repeated(gv_ref[1].T, SPAN // gv_ref.shape[1]).astype(F32) * scale).astype(BF)
+    for copy in tiles:
+        copy.wait()
+    occ_kron = spread(tiles_ref[0].T, SUBLANES)
+    vir_kron = (repeated(tiles_ref[1].T, SPAN // gv_ref.shape[1]).astype(F32) * scale).astype(BF)
     for copy in fetch:
         copy.wait()
     store = []
@@ -316,7 +318,7 @@
         for j in range(wide // SPAN):
             at = c * wide + j * SPAN
             over_ref[c, :, j * SPAN : (j + 1) * SPAN] = dot(rows_ref[:, at : at + SPAN], vir_kron).astype(BF)
-        store.append(pltpu.make_async_copy(over_ref.at[c], out, out_sems.at[PIECES + c]))
+        store.append(pltpu.make_async_copy(over_ref.at[c], out, out_sems.at[len(CUTS) + c]))
         store[-1].start()
 
     def part_of(span):
@@ -324,10 +326,11 @@
         return (jnp.concatenate(parts, axis=0) if len(parts) > 1 else parts[0]) * live
 
     occ_group(occ_kron, yt_ref, half_ref, part_of, slice(0, yt_ref.shape[2]), size)
-    some = half_ref.shape[0] // PIECES
+    to = 0
     for c, out in enumerate(half_outs):
-        store.append(pltpu.make_async_copy(half_ref.at[pl.ds(c * some, some)], out, out_sems.at[c]))
+        store.append(pltpu.make_async_copy(half_ref.at[pl.ds(to, out.shape[0])], out, out_sems.at[c]))
         store[-1].start()
+        to += out.shape[0]
     for copy in store:
         copy.wait()
 
@@ -336,27 +339,29 @@
     aux, size = y.shape
     tile = green_occ.shape[1]
     width = sum(count for _, count in slices)
-    whole = pl.BlockSpec(memory_space=pltpu.VMEM)
     some = pl.BlockSpec(memory_space=pl.ANY)
+    fixed = pl.BlockSpec(memory_space=pltpu.HBM)
+    parts = [tile * n // sum(CUTS) for n in CUTS]
     outs = pl.pallas_call(
         lambda *refs: both_kernel(*refs, slices=slices),
-        in_specs=[pl.BlockSpec(memory_space=pltpu.SMEM), whole, whole, some, *unused(before)],
-        out_specs=[some] * (2 * PIECES),
-        out_shape=[jax.ShapeDtypeStruct((tile // PIECES, tile, width), BF)] * PIECES
+        in_specs=[pl.BlockSpec(memory_space=pltpu.SMEM), fixed, fixed, some, *unused(before)],
+        out_specs=[some] * (len(CUTS) + PIECES),
+        out_shape=[jax.ShapeDtypeStruct((n, tile, width), BF) for n in parts]
         + [jax.ShapeDtypeStruct((aux, size // PIECES), BF)] * PIECES,
         scratch_shapes=[
             pltpu.VMEM((aux, size), BF),
             pltpu.VMEM((tile, tile, width), BF),
             pltpu.VMEM((tile, tile, width), BF),
             pltpu.VMEM((PIECES, aux, size // PIECES), BF),
-            pltpu.SemaphoreType.DMA((IN_STEPS,)),
-            pltpu.SemaphoreType.DMA((2 * PIECES,)),
+            pltpu.VMEM((2, tile, tile), BF),
+            pltpu.SemaphoreType.DMA((IN_STEPS + 2,)),
+            pltpu.SemaphoreType.DMA((len(CUTS) + PIECES,)),
         ],
         compiler_params=params(),
         cost_estimate=cost(2 * width * size * tile * SUBLANES, 8 * aux * size),
         name="both_halves",
     )(live, green_occ, green_vir, y, *before)
-    return [half.reshape(-1, width) for half in outs[:PIECES]], outs[PIECES:]
+    return [half.reshape(-1, width) for half in outs[: len(CUTS)]], outs[len(CUTS) :]
 
 
 def fold_kernel(live_ref, g_ref, y_ref, shifted_ref, own_ref, *rest, started, turn):
@@ -409,9 +414,9 @@
 
 
 def both_kernel(live_ref, go_ref, gv_ref, y_ref, *rest, slices):
-    rows_ref, yt_ref, half_ref, over_ref, in_sems, out_sems = rest[-6:]
-    outs = rest[-6 - 2 * PIECES : -6]
-    half_outs, over_outs = outs[:PIECES], outs[PIECES:]
+    rows_ref, yt_ref, half_ref, over_ref, tiles_ref, in_sems, out_sems = rest[-7:]
+    outs = rest[-7 - len(CUTS) - PIECES : -7]
+    half_outs, over_outs = outs[: len(CUTS)], outs[len(CUTS) :]
     aux, size = y_ref.shape
     step = aux // IN_STEPS
     fetch = []
@@ -420,10 +425,15 @@
         fetch.append(pltpu.make_async_copy(y_ref.at[at], rows_ref.at[at], in_sems.at[i]))
     for copy in fetch:
         copy.start()
+    tiles = [pltpu.make_async_copy(g.at[1], tiles_ref.at[i], in_sems.at[IN_STEPS + i]) for i, g in enumerate((go_ref, gv_ref))]
+    for copy in tiles:
+        copy.start()
     scale = live_ref[0].astype(F32)
     live = scale.astype(BF)
-    occ_kron = spread(go_ref[1].T, SUBLANES)
-    vir_kron = (repeated(gv_ref[1].T, SPAN // gv_ref.shape[1]).astype(F32) * scale).astype(BF)
+    for copy in tiles:
+        copy.wait()
+    occ_kron = spread(tiles_ref[0].T, SUBLANES)
+    vir_kron = (repeated(tiles_ref[1].T, SPAN // gv_ref.shape[1]).astype(F32) * scale).astype(BF)
     for copy in fetch:
         copy.wait()
     store = []
@@ -432,7 +442,7 @@
         for j in range(wide // SPAN):
             at = c * wide + j * SPAN
             over_ref[c, :, j * SPAN : (j + 1) * SPAN] = dot(rows_ref[:, at : at + SPAN], vir_kron).astype(BF)
-        store.append(pltpu.make_async_copy(over_ref.at[c], out, out_sems.at[PIECES + c]))
+        store.append(pltpu.make_async_copy(over_ref.at[c], out, out_sems.at[len(CUTS) + c]))
         store[-1].start()
 
     def part_of(span):
@@ -440,10 +450,11 @@
         return (jnp.concatenate(parts, axis=0) if len(parts) > 1 else parts[0]) * live
 
     occ_group(occ_kron, yt_ref, half_ref, part_of, slice(0, yt_ref.shape[2]), size)
-    some = half_ref.shape[0] // PIECES
+    to = 0
     for c, out in enumerate(half_outs):
-        store.append(pltpu.make_async_copy(half_ref.at[pl.ds(c * some, some)], out, out_sems.at[c]))
+        store.append(pltpu.make_async_copy(half_ref.at[pl.ds(to, out.shape[0])], out, out_sems.at[c]))
         store[-1].start()
+        to += out.shape[0]
     for copy in store:
         copy.wait()
 
@@ -452,27 +463,29 @@
     aux, size = y.shape
     tile = green_occ.shape[1]
     width = sum(count for _, count in slices)
-    whole = pl.BlockSpec(memory_space=pltpu.VMEM)
     some = pl.BlockSpec(memory_space=pl.ANY)
+    fixed = pl.BlockSpec(memory_space=pltpu.HBM)
+    parts = [tile * n // sum(CUTS) for n in CUTS]
     outs = pl.pallas_call(
         lambda *refs: both_kernel(*refs, slices=slices),
-        in_specs=[pl.BlockSpec(memory_space=pltpu.SMEM), whole, whole, some, *unused(before)],
-        out_specs=[some] * (2 * PIECES),
-        out_shape=[jax.ShapeDtypeStruct((tile // PIECES, tile, width), BF)] * PIECES
+        in_specs=[pl.BlockSpec(memory_space=pltpu.SMEM), fixed, fixed, some, *unused(before)],
+        out_specs=[some] * (len(CUTS) + PIECES),
+        out_shape=[jax.ShapeDtypeStruct((n, tile, width), BF) for n in parts]
         + [jax.ShapeDtypeStruct((aux, size // PIECES), BF)] * PIECES,
         scratch_shapes=[
             pltpu.VMEM((aux, size), BF),
             pltpu.VMEM((tile, tile, width), BF),
             pltpu.VMEM((tile, tile, width), BF),
             pltpu.VMEM((PIECES, aux, size // PIECES), BF),
-            pltpu.SemaphoreType.DMA((IN_STEPS,)),
-            pltpu.SemaphoreType.DMA((2 * PIECES,)),
+            pltpu.VMEM((2, tile, tile), BF),
+            pltpu.SemaphoreType.DMA((IN_STEPS + 2,)),
+            pltpu.SemaphoreType.DMA((len(CUTS) + PIECES,)),
         ],
         compiler_params=params(),
         cost_estimate=cost(2 * width * size * tile * SUBLANES, 8 * aux * size),
         name="both_halves",
     )(live, green_occ, green_vir, y, *before)
-    return [half.reshape(-1, width) for half in outs[:PIECES]], outs[PIECES:]
+    return [half.reshape(-1, width) for half in outs[: len(CUTS)]], outs[len(CUTS) :]
 
 
 def vir_kernel(live_ref, g_ref, y_ref, *rest, n_added):
@@ -516,49 +529,48 @@
     )(live, mat, y, *added, *before)
 
 
-def product_kernel(x_ref, *rest, pieces, steps, started, turn):
+def product_kernel(x_ref, *rest, pieces, steps, at, started):
     z_refs = rest[:pieces]
     out_ref, acc_ref = rest[-2:]
     step = pl.program_id(0)
+
+    @pl.when(step == 0)
+    def _():
+        acc_ref[...] = rest[pieces][...].T if started else jnp.zeros(acc_ref.shape, F32)
+
     for i, z_ref in enumerate(z_refs):
-        for first in (True, False) if i == 0 else (False,):
-
-            @pl.when(step == 0 if first else jnp.logical_and(step > 0, step // steps == i))
-            def _(z_ref=z_ref, first=first):
-                got = dot(z_ref[...], x_ref[...])
-                if not first:
-                    got = acc_ref[...] + got
-                elif started:
-                    got = rest[pieces][...] + got
-                acc_ref[...] = got
+
+        @pl.when((step + at) // steps == i)
+        def _(z_ref=z_ref):
+            acc_ref[...] += dot(z_ref[...], x_ref[...])
 
     @pl.when(step == pl.num_programs(0) - 1)
     def _():
-        out_ref[...] = acc_ref[...].T if turn else acc_ref[...]
-
-
-def product(zs, x, at=0, so_far=None, turn=True, before=()):
+        out_ref[...] = acc_ref[...].T
+
+
+def product(zs, x, start, so_far=None, before=()):
     aux, size = zs[0].shape
     width = x.shape[1]
-    span = next(n * SPAN for n in (8, 4, 1) if size % (n * SPAN) == 0)
-    steps = size // span
-    piece = lambda k: pl.BlockSpec((aux, span), lambda i: (0, jnp.clip(i - k * steps, 0, steps - 1)))
+    span = size // 2
+    zs, at = zs[start // size :], start % size // span
     added = [] if so_far is None else [so_far]
-    shape = (width, aux) if turn else (aux, width)
+    whole = pl.BlockSpec((width, aux), lambda i: (0, 0))
+    piece = lambda k: pl.BlockSpec((aux, span), lambda i: (0, jnp.clip(i + at - 2 * k, 0, 1)))
     return pl.pallas_call(
-        lambda *refs: product_kernel(*refs, pieces=len(zs), steps=steps, started=bool(added), turn=turn),
-        grid=(len(zs) * steps,),
+        lambda *refs: product_kernel(*refs, pieces=len(zs), steps=2, at=at, started=bool(added)),
+        grid=(x.shape[0] // span,),
         in_specs=[
-            pl.BlockSpec((span, width), lambda i: (at // span + i, 0)),
+            pl.BlockSpec((span, width), lambda i: (i, 0)),
             *(piece(k) for k in range(len(zs))),
-            *[pl.BlockSpec((aux, width), lambda i: (0, 0))] * len(added),
+            *[whole] * len(added),
             *unused(before),
         ],
-        out_specs=pl.BlockSpec(shape, lambda i: (0, 0)),
-        out_shape=jax.ShapeDtypeStruct(shape, F32),
+        out_specs=whole,
+        out_shape=jax.ShapeDtypeStruct((width, aux), F32),
         scratch_shapes=[pltpu.VMEM((aux, width), F32)],
         compiler_params=params(),
-        cost_estimate=cost(2 * aux * size * width, 2 * size * (aux + width)),
+        cost_estimate=cost(2 * aux * x.shape[0] * width, 2 * x.shape[0] * (aux + width)),
         name="product",
     )(x, *zs, *added, *before)
 
@@ -621,17 +633,18 @@
     for i in range(PIECES):
         z, diag = fold(live, green_vir[0], y, i, shifted[i], own, diag, i == PIECES - 1)
         zs.append(z)
-    blocks, order = [], [[diag]] * PIECES
+    blocks, order = [], [[diag]] * len(ending)
     if chunked:
         early = raw_product(unfolded, zs, green_occ.shape[2], before=[diag])
         both_done = scattered([diag, early], "col", True)
         chi_d, blocks = both_done[: aux // cols], [both_done[aux // cols :]]
-        order = [[early]] * (PIECES - 1) + [[both_done]]
+        order = [[early]] * (len(ending) - 1) + [[both_done]]
     else:
         chi_d = scattered([diag], "col", True)
-    ended = None
-    for i, half in enumerate(ending):
-        ended = product(zs[i : i + 1], half, 0, ended, i == PIECES - 1, before=order[i])
+    ended, start = None, 0
+    for half, wait in zip(ending, order):
+        ended = product(zs, half, start, ended, before=wait)
+        start += half.shape[0]
     blocks.append(scattered([ended], "col", False))
     return chi_d[None], jnp.concatenate(blocks)[None]
 

time: 133 us -> 133 us (level)
  local copies, waits for them, and re-layouts: 6.28 us -> 4.84 us
    ppermute x3, waiting for transfers between devices: 1.76 us -> 0.01 us  [scattered(): lax.ppermute(given, axis, [(i, i ^ reach) for i in range(size)]).astype(F32)]
    unnamed x16 -> x12, local copies, waits for them, and re-layouts: 5.44 us -> 3.99 us
    ppermute x3, waiting for transfers between devices: 59.4 us -> 60.8 us  [body(): send = lambda half: lax.ppermute(half, 'row', up_row)]
  transfers between devices with their start and end apart: 10 -> 10, of which waited for: 6 -> 5; matrix products, arithmetic and copies ran while one was open for 2% -> 2% of each run, Pallas kernels for 29% -> 30%
where the time goes in v7:
time: 133 us; the launch traced here: 132 us
  waiting for transfers between devices  64.1 us (48%)
  Pallas kernels  44.6 us (34%)
  starting transfers between devices  14.1 us (11%)
  local copies, waits for them, and re-layouts  4.84 us (4%)
  other arithmetic  3.12 us (2%)
  between operations  1.59 us (1%)
    ppermute x3, waiting for transfers between devices, body(): send = lambda half: lax.ppermute(half, 'row', up_row)  60.8 us
    pallas_call x2, Pallas kernels, fold(): pl.pallas_call(lambda *refs: fold_kernel(*refs, started=bool(added), turn...  13.3 us
    pallas_call x1, Pallas kernels, raw_product(): pl.pallas_call(raw_product_kernel, in_specs=[*[pl.BlockSpec(memory_space=...  8.08 us
    pallas_call x1, Pallas kernels, occ(): pl.pallas_call(lambda *refs: occ_kernel(*refs, groups=groups, which=which...  7.6 us
    pallas_call x1, Pallas kernels, both(): pl.pallas_call(lambda *refs: both_kernel(*refs, slices=slices), in_specs=...  6.97 us
    ppermute x3, starting transfers between devices, scattered(): lax.ppermute(given, axis, [(i, i ^ reach) for i in range(size)]).astype(F32)  5.77 us
    pallas_call x2, Pallas kernels, product(): pl.pallas_call(lambda *refs: product_kernel(*refs, pieces=len(zs), steps=...  5.52 us
    unnamed x12, local copies, waits for them, and re-layouts  3.99 us
  transfers between devices with their start and end apart: 10, of which 5 were waited for; matrix products, arithmetic and copies ran while one was open for 2% of the time, Pallas kernels for 30%

profile of v7, /device:TPU:0, one launch (start us, length us, event | category | flops | bytes accessed | tf_op | source)
XLA Modules:
  0.0 132.3 jit_solution(15305969440051179739)
XLA Ops:
  1.3 0.0 copy-start.4
  1.3 0.7 copy-done.4
  2.0 0.0 copy-start.5
  2.0 3.2 %raw.1.refs_4_ = bf16[3088,512]{1,0:T(8,128)(2,1)} custom-call(s32[1]{0:T(128)} %bitcast.38.refs_0_, bf16[2,64,64]{2,1,0:T(8,128)(2,1)S(1)} %bitcast.49, bf16[640,4096]{1,0:T(8,128)(2,1)} %bitcast.55), custom_call_target="tpu_custom_call" | custom-call | flops 1 | bytes 1 | tf_op jit(solution)/shard_map/raw/pallas_call | solution.py:165
  5.2 1.3 collective-permute-start.2
  6.5 0.0 copy-done.5
  6.5 7.0 %both_halves.1 = (bf16[48,64,256]{2,1,0:T(8,128)(2,1)}, bf16[16,64,256]{2,1,0:T(8,128)(2,1)}, bf16[640,2048]{1,0:T(8,128)(2,1)S(1)}, bf16[640,2048]{1,0:T(8,128)(2,1)}) custom-call(s32[1]{0:T(128)} %bitcast.39.refs_0_, bf16[2,64,64]{2,1,0:T(8,128)(2,1)S(1)} %bitcast.50, bf16[2,64,64]{2,1,0:T(8,128)(2,1)S(1)} %bitcast.52, bf16[640,4096]{1,0:T(8,128)(2,1)} %bitcast.56, ...), custom_call_target="tpu_custom_call" | custom-call | flops 1 | bytes 1 | tf_op jit(solution)/shard_map/both_halves/pallas_call | solution.py:469
  13.5 1.3 collective-permute-start.1
  14.8 1.3 collective-permute-start
  16.1 1.3 collective-permute-start.7
  17.4 7.6 %occ.1 = bf16[64,64,640]{2,1,0:T(8,128)(2,1)} custom-call(s32[1]{0:T(128)} %bitcast.40.refs_0_, bf16[2,64,64]{2,1,0:T(8,128)(2,1)S(1)} %bitcast.51, bf16[640,4096]{1,0:T(8,128)(2,1)} %bitcast.57, bf16[3072,256]{1,0:T(8,128)(2,1)} %bitcast.4.refs_3_), custom_call_target="tpu_custom_call" | custom-call | flops 1 | bytes 1 | tf_op jit(solution)/shard_map/occ/pallas_call | solution.py:268
  25.0 0.0 collective-permute-done.1.refs_3_
  25.0 6.1 %fold.2 = (bf16[640,2048]{1,0:T(8,128)(2,1)S(1)}, f32[640,640]{1,0:T(8,128)S(1)}) custom-call(s32[1]{0:T(128)} %bitcast.41.refs_0_, bf16[2,64,64]{2,1,0:T(8,128)(2,1)S(1)} %bitcast.53, bf16[640,4096]{1,0:T(8,128)(2,1)} %bitcast.58, bf16[640,2048]{1,0:T(8,128)(2,1)} %collective-permute-done.1.refs_3_, bf16[4096,640]{1,0:T(8,128)(2,1)} %bitcast.60), custom_call_target="tpu_custom_call" | custom-call | flops 1 | bytes 1 | tf_op jit(solution)/shard_map/fold/pallas_call | solution.py:395
  31.1 0.0 copy-start.2
  31.1 0.0 collective-permute-done.refs_3_
  31.1 7.2 %fold.3 = (bf16[640,2048]{1,0:T(8,128)(2,1)S(1)}, f32[640,640]{1,0:T(8,128)S(1)}) custom-call(s32[1]{0:T(128)} %bitcast.42.refs_0_, bf16[2,64,64]{2,1,0:T(8,128)(2,1)S(1)} %bitcast.54, bf16[640,4096]{1,0:T(8,128)(2,1)} %bitcast.59, bf16[640,2048]{1,0:T(8,128)(2,1)} %collective-permute-done.refs_3_, bf16[4096,640]{1,0:T(8,128)(2,1)} %bitcast.61, ...), custom_call_target="tpu_custom_call" | custom-call | flops 1 | bytes 1 | tf_op jit(solution)/shard_map/fold/pallas_call | solution.py:395
  38.3 0.0 copy-start
  38.3 1.5 %copy-done = bf16[640,2048]{1,0:T(8,128)(2,1)} copy-done((bf16[640,2048]{1,0:T(8,128)(2,1)}, bf16[640,2048]{1,0:T(8,128)(2,1)S(1)}, u32[]{:S(2)}) %copy-start) | copy-done | bytes 2621464
  39.8 39.8 %collective-permute-done.2.r_ref = bf16[3088,512]{1,0:T(8,128)(2,1)} collective-permute-done((bf16[3088,512]{1,0:T(8,128)(2,1)}, bf16[3088,512]{1,0:T(8,128)(2,1)}, u32[]{:S(2)}, u32[]{:S(2)}) %collective-permute-start.2) | collective-permute-done | bytes 3162144 | tf_op jit(solution)/shard_map/ppermute | solution.py:619
  79.6 0.0 copy-done.2
  79.7 8.1 %raw_product.1.refs_3_ = f32[384,640]{1,0:T(8,128)S(1)} custom-call(bf16[3088,512]{1,0:T(8,128)(2,1)} %collective-permute-done.2.r_ref, bf16[640,2048]{1,0:T(8,128)(2,1)S(1)} %get-tuple-element.15.rest_0_.refs_1_, bf16[640,2048]{1,0:T(8,128)(2,1)} %copy-done, f32[640,640]{1,0:T(8,128)S(1)} %get-tuple-element.14.rest_2_), custom_call_target="tpu_custom_call" | custom-call | flops 1 | bytes 1 | tf_op jit(solution)/shard_map/raw_product/pallas_call | solution.py:226
  87.7 0.8 fusion.12
  88.6 4.4 %collective-permute-start.3 = (bf16[256,640]{1,0:T(8,128)(2,1)}, bf16[256,640]{1,0:T(8,128)(2,1)}, u32[]{:S(2)}, u32[]{:S(2)}) collective-permute-start(bf16[256,640]{1,0:T(8,128)(2,1)} %get-tuple-element.18), channel_id=1, source_target_pairs={{0,1},{1,0},{2,3},{3,2},{4,5},{5,4},{6,7},{7,6},{8,9},{9,8},{10,11... | collective-permute-start | bytes 983048 | tf_op jit(solution)/shard_map/ppermute | solution.py:590
  93.0 0.0 collective-permute-start.4
  93.0 1.4 %collective-permute-start.5 = (bf16[256,640]{1,0:T(8,128)(2,1)S(1)}, bf16[256,640]{1,0:T(8,128)(2,1)}, u32[]{:S(2)}, u32[]{:S(2)}) collective-permute-start(bf16[256,640]{1,0:T(8,128)(2,1)S(1)} %get-tuple-element.20), channel_id=1, source_target_pairs={{0,3},{1,2},{2,1},{3,0},{4,7},{5,6},{6,5},{7,4},{8,11},{9,10},{10,... | collective-permute-start | bytes 983048 | tf_op jit(solution)/shard_map/ppermute | solution.py:590
  94.3 1.3 collective-permute-start.6
  95.7 17.7 %collective-permute-done.7.refs_0_ = bf16[3072,256]{1,0:T(8,128)(2,1)} collective-permute-done((bf16[3072,256]{1,0:T(8,128)(2,1)}, bf16[3072,256]{1,0:T(8,128)(2,1)}, u32[]{:S(2)}, u32[]{:S(2)}) %collective-permute-start.7) | collective-permute-done | bytes 1572896 | tf_op jit(solution)/shard_map/ppermute | solution.py:619
  113.4 0.0 copy-start.3
  113.4 1.7 %copy-done.3 = bf16[640,2048]{1,0:T(8,128)(2,1)S(1)} copy-done((bf16[640,2048]{1,0:T(8,128)(2,1)S(1)}, bf16[640,2048]{1,0:T(8,128)(2,1)}, u32[]{:S(2)}) %copy-start.3) | copy-done | bytes 2621464
  115.1 3.9 %product.2.refs_2_ = f32[256,640]{1,0:T(8,128)S(1)} custom-call(bf16[3072,256]{1,0:T(8,128)(2,1)} %collective-permute-done.7.refs_0_, bf16[640,2048]{1,0:T(8,128)(2,1)S(1)} %copy-done.3, bf16[640,2048]{1,0:T(8,128)(2,1)} %copy-done, f32[384,640]{1,0:T(8,128)S(1)} %raw_product.1.refs_3_), custom_call_target="tpu_custom_call" | custom-call | flops 1 | bytes 1 | tf_op jit(solution)/shard_map/product/pallas_call | solution.py:560
  119.0 0.0 copy-start.1
  119.0 0.0 collective-permute-done.3
  119.0 0.0 collective-permute-done.4
  119.0 0.0 collective-permute-done.5
  119.0 1.5 %fusion.6.refs_3_ = f32[256,640]{1,0:T(8,128)S(1)} fusion(s32[]{:T(128)S(6)} %select_n.43, f32[4,160,640]{2,1,0:T(8,128)S(1)} %bitcast.46, f32[4,96,640]{2,1,0:T(8,128)S(1)} %bitcast.44, bf16[256,640]{1,0:T(8,128)(2,1)} %collective-permute-done.5, bf16[256,640]{1,0:T(8,128)(2,1)} %collective-permute-done.4, bf16[256,640]{1,0:T(8,128)(2,1)} %collective-permute-done.3), kind=kLoop, calls=%fused_computation.14 | loop fusion | flops 1146880 | bytes 4259844 | tf_op jit(solution)/shard_map/add | solution.py:590
  120.5 3.2 %collective-permute-done.6.refs_0_ = bf16[1024,256]{1,0:T(8,128)(2,1)} collective-permute-done((bf16[1024,256]{1,0:T(8,128)(2,1)}, bf16[1024,256]{1,0:T(8,128)(2,1)}, u32[]{:S(2)}, u32[]{:S(2)}) %collective-permute-start.6) | collective-permute-done | bytes 524320 | tf_op jit(solution)/shard_map/ppermute | solution.py:619
  123.8 0.0 copy-done.1
  123.8 1.6 %product.3 = f32[256,640]{1,0:T(8,128)S(1)} custom-call(bf16[1024,256]{1,0:T(8,128)(2,1)} %collective-permute-done.6.refs_0_, bf16[640,2048]{1,0:T(8,128)(2,1)S(1)} %copy-done.1, f32[256,640]{1,0:T(8,128)S(1)} %product.2.refs_2_, f32[256,640]{1,0:T(8,128)S(1)} %fusion.6.refs_3_), custom_call_target="tpu_custom_call" | custom-call | flops 1 | bytes 1 | tf_op jit(solution)/shard_map/product/pallas_call | solution.py:560
  125.4 0.1 collective-permute-start.8
  125.5 1.3 %collective-permute-done.8 = bf16[2,64,640]{2,1,0:T(8,128)(2,1)S(1)} collective-permute-done((bf16[2,64,640]{2,1,0:T(8,128)(2,1)S(1)}, bf16[2,64,640]{2,1,0:T(8,128)(2,1)S(1)}, u32[]{:S(2)}, u32[]{:S(2)}) %collective-permute-start.8) | collective-permute-done | bytes 163872 | tf_op jit(solution)/shard_map/ppermute | solution.py:597
  126.9 1.8 %collective-permute-start.9 = (bf16[1,64,640]{2,1,0:T(8,128)(2,1)S(1)}, bf16[1,64,640]{2,1,0:T(8,128)(2,1)S(1)}, u32[]{:S(2)}, u32[]{:S(2)}) collective-permute-start(bf16[1,64,640]{2,1,0:T(8,128)(2,1)S(1)} %dynamic-slice_convert_fusion), channel_id=1, source_target_pairs={{0,2},{1,3},{2,0},{3,1},{4,6},{5,7},{6,4},{7,5},{8,10},{9,11},{10,... | collective-permute-start | bytes 245768 | tf_op jit(solution)/shard_map/ppermute | solution.py:597
  128.8 0.8 slice_bitcast_fusion
  129.6 2.0 %collective-permute-done.9 = bf16[1,64,640]{2,1,0:T(8,128)(2,1)S(1)} collective-permute-done((bf16[1,64,640]{2,1,0:T(8,128)(2,1)S(1)}, bf16[1,64,640]{2,1,0:T(8,128)(2,1)S(1)}, u32[]{:S(2)}, u32[]{:S(2)}) %collective-permute-start.9) | collective-permute-done | bytes 81952 | tf_op jit(solution)/shard_map/ppermute | solution.py:597
  131.5 0.8 maximum_bitcast_fusion
  (5 shorter events, 0.1 us)
Async XLA Ops:
  1.3 0.8 copy-start.4
  2.0 4.5 %copy-start.5 = (bf16[1,2,64,64]{3,2,1,0:T(8,128)(2,1)S(1)}, bf16[1,2,64,64]{3,2,1,0:T(8,128)(2,1)}, u32[]{:S(2)}) copy-start(bf16[1,2,64,64]{3,2,1,0:T(8,128)(2,1)} %param.6) | copy-start | bytes 49156
  5.2 74.4 %collective-permute-start.2 = (bf16[3088,512]{1,0:T(8,128)(2,1)}, bf16[3088,512]{1,0:T(8,128)(2,1)}, u32[]{:S(2)}, u32[]{:S(2)}) collective-permute-start(bf16[3088,512]{1,0:T(8,128)(2,1)} %raw.1.refs_4_), channel_id=1, source_target_pairs={{4,0},{8,4},{12,8},{16,12},{20,16},{24,20},{28,24},{5,1},{9,5},{13... | collective-permute-start | bytes 9486344 | tf_op jit(solution)/shard_map/ppermute | solution.py:619
  13.5 11.5 %collective-permute-start.1 = (bf16[640,2048]{1,0:T(8,128)(2,1)S(1)}, bf16[640,2048]{1,0:T(8,128)(2,1)}, u32[]{:S(2)}, u32[]{:S(2)}) collective-permute-start(bf16[640,2048]{1,0:T(8,128)(2,1)S(1)} %get-tuple-element.12), channel_id=1, source_target_pairs={{1,0},{2,1},{3,2},{5,4},{6,5},{7,6},{9,8},{10,9},{11,10},{13,12},{... | collective-permute-start | bytes 7864328 | tf_op jit(solution)/shard_map/ppermute | solution.py:627
  14.8 16.3 %collective-permute-start = (bf16[640,2048]{1,0:T(8,128)(2,1)}, bf16[640,2048]{1,0:T(8,128)(2,1)}, u32[]{:S(2)}, u32[]{:S(2)}) collective-permute-start(bf16[640,2048]{1,0:T(8,128)(2,1)} %get-tuple-element.10), channel_id=1, source_target_pairs={{1,0},{2,1},{3,2},{5,4},{6,5},{7,6},{9,8},{10,9},{11,10},{13,12},{... | collective-permute-start | bytes 7864328 | tf_op jit(solution)/shard_map/ppermute | solution.py:627
  16.1 97.3 %collective-permute-start.7 = (bf16[3072,256]{1,0:T(8,128)(2,1)}, bf16[3072,256]{1,0:T(8,128)(2,1)}, u32[]{:S(2)}, u32[]{:S(2)}) collective-permute-start(bf16[3072,256]{1,0:T(8,128)(2,1)} %bitcast.4.refs_3_), channel_id=1, source_target_pairs={{4,0},{8,4},{12,8},{16,12},{20,16},{24,20},{28,24},{5,1},{9,5},{13... | collective-permute-start | bytes 4718600 | tf_op jit(solution)/shard_map/ppermute | solution.py:619
  31.1 48.6 %copy-start.2 = (bf16[640,2048]{1,0:T(8,128)(2,1)}, bf16[640,2048]{1,0:T(8,128)(2,1)S(1)}, u32[]{:S(2)}) copy-start(bf16[640,2048]{1,0:T(8,128)(2,1)S(1)} %get-tuple-element.15.rest_0_.refs_1_) | copy-start | bytes 7864324
  38.3 1.5 %copy-start = (bf16[640,2048]{1,0:T(8,128)(2,1)}, bf16[640,2048]{1,0:T(8,128)(2,1)S(1)}, u32[]{:S(2)}) copy-start(bf16[640,2048]{1,0:T(8,128)(2,1)S(1)} %get-tuple-element.16.rest_1_.refs_2_.refs_1_) | copy-start | bytes 7864324
  88.6 30.4 %collective-permute-start.3 = (bf16[256,640]{1,0:T(8,128)(2,1)}, bf16[256,640]{1,0:T(8,128)(2,1)}, u32[]{:S(2)}, u32[]{:S(2)}) collective-permute-start(bf16[256,640]{1,0:T(8,128)(2,1)} %get-tuple-element.18), channel_id=1, source_target_pairs={{0,1},{1,0},{2,3},{3,2},{4,5},{5,4},{6,7},{7,6},{8,9},{9,8},{10,11... | collective-permute-start | bytes 983048 | tf_op jit(solution)/shard_map/ppermute | solution.py:590
  93.0 26.0 %collective-permute-start.4 = (bf16[256,640]{1,0:T(8,128)(2,1)S(1)}, bf16[256,640]{1,0:T(8,128)(2,1)}, u32[]{:S(2)}, u32[]{:S(2)}) collective-permute-start(bf16[256,640]{1,0:T(8,128)(2,1)S(1)} %get-tuple-element.19), channel_id=1, source_target_pairs={{0,2},{1,3},{2,0},{3,1},{4,6},{5,7},{6,4},{7,5},{8,10},{9,11},{10,... | collective-permute-start | bytes 983048 | tf_op jit(solution)/shard_map/ppermute | solution.py:590
  93.0 26.0 %collective-permute-start.5 = (bf16[256,640]{1,0:T(8,128)(2,1)S(1)}, bf16[256,640]{1,0:T(8,128)(2,1)}, u32[]{:S(2)}, u32[]{:S(2)}) collective-permute-start(bf16[256,640]{1,0:T(8,128)(2,1)S(1)} %get-tuple-element.20), channel_id=1, source_target_pairs={{0,3},{1,2},{2,1},{3,0},{4,7},{5,6},{6,5},{7,4},{8,11},{9,10},{10,... | collective-permute-start | bytes 983048 | tf_op jit(solution)/shard_map/ppermute | solution.py:590
  94.3 29.4 %collective-permute-start.6 = (bf16[1024,256]{1,0:T(8,128)(2,1)}, bf16[1024,256]{1,0:T(8,128)(2,1)}, u32[]{:S(2)}, u32[]{:S(2)}) collective-permute-start(bf16[1024,256]{1,0:T(8,128)(2,1)} %bitcast.13), channel_id=1, source_target_pairs={{4,0},{8,4},{12,8},{16,12},{20,16},{24,20},{28,24},{5,1},{9,5},{13... | collective-permute-start | bytes 1572872 | tf_op jit(solution)/shard_map/ppermute | solution.py:619
  113.4 1.7 %copy-start.3 = (bf16[640,2048]{1,0:T(8,128)(2,1)S(1)}, bf16[640,2048]{1,0:T(8,128)(2,1)}, u32[]{:S(2)}) copy-start(bf16[640,2048]{1,0:T(8,128)(2,1)} %copy-done.2) | copy-start | bytes 7864324
  119.0 4.8 %copy-start.1 = (bf16[640,2048]{1,0:T(8,128)(2,1)S(1)}, bf16[640,2048]{1,0:T(8,128)(2,1)}, u32[]{:S(2)}) copy-start(bf16[640,2048]{1,0:T(8,128)(2,1)} %copy-done) | copy-start | bytes 7864324
  125.4 1.5 %collective-permute-start.8 = (bf16[2,64,640]{2,1,0:T(8,128)(2,1)S(1)}, bf16[2,64,640]{2,1,0:T(8,128)(2,1)S(1)}, u32[]{:S(2)}, u32[]{:S(2)}) collective-permute-start(bf16[2,64,640]{2,1,0:T(8,128)(2,1)S(1)} %fusion.14), channel_id=1, source_target_pairs={{0,1},{1,0},{2,3},{3,2},{4,5},{5,4},{6,7},{7,6},{8,9},{9,8},{10,11... | collective-permute-start | bytes 491528 | tf_op jit(solution)/shard_map/ppermute | solution.py:597
  126.9 4.6 %collective-permute-start.9 = (bf16[1,64,640]{2,1,0:T(8,128)(2,1)S(1)}, bf16[1,64,640]{2,1,0:T(8,128)(2,1)S(1)}, u32[]{:S(2)}, u32[]{:S(2)}) collective-permute-start(bf16[1,64,640]{2,1,0:T(8,128)(2,1)S(1)} %dynamic-slice_convert_fusion), channel_id=1, source_target_pairs={{0,2},{1,3},{2,0},{3,1},{4,6},{5,7},{6,4},{7,5},{8,10},{9,11},{10,... | collective-permute-start | bytes 245768 | tf_op jit(solution)/shard_map/ppermute | solution.py:597

commit v8 on v7

--- a/solution.py
+++ b/solution.py
@@ -645,7 +645,7 @@
     for half, wait in zip(ending, order):
         ended = product(zs, half, start, ended, before=wait)
         start += half.shape[0]
-    blocks.append(scattered([ended], "col", False))
+    blocks.append(scattered([ended], "col", True))
     return chi_d[None], jnp.concatenate(blocks)[None]
 
 

time: 133 us -> 132 us (level)
    ppermute x3 -> x6, waiting for transfers between devices: 0.01 us -> 3.57 us  [scattered(): lax.ppermute(given, axis, [(i, i ^ reach) for i in range(size)]).astype(F32)]
    ppermute x2 -> x0, waiting for transfers between devices: 3.29 us -> none  [scattered(): got = lax.ppermute(given, axis, [(i, i ^ reach) for i in range(size)])]
    ppermute x3 -> x6, starting transfers between devices: 5.77 us -> 7.95 us  [scattered(): lax.ppermute(given, axis, [(i, i ^ reach) for i in range(size)]).astype(F32)]
    ppermute x2 -> x0, starting transfers between devices: 1.9 us -> none  [scattered(): got = lax.ppermute(given, axis, [(i, i ^ reach) for i in range(size)])]
  transfers between devices with their start and end apart: 10 -> 11, of which waited for: 5 -> 5; matrix products, arithmetic and copies ran while one was open for 2% -> 2% of each run, Pallas kernels for 30% -> 30%
where the time goes in v8:
time: 132 us
  waiting for transfers between devices  64.3 us (49%)
  Pallas kernels  43.5 us (33%)
  starting transfers between devices  14.4 us (11%)
  local copies, waits for them, and re-layouts  4.83 us (4%)
  other arithmetic  3.17 us (2%)
  between operations  1.51 us (1%)
    ppermute x3, waiting for transfers between devices, body(): send = lambda half: lax.ppermute(half, 'row', up_row)  60.7 us
    pallas_call x2, Pallas kernels, fold(): pl.pallas_call(lambda *refs: fold_kernel(*refs, started=bool(added), turn...  13.3 us
    pallas_call x1, Pallas kernels, raw_product(): pl.pallas_call(raw_product_kernel, in_specs=[*[pl.BlockSpec(memory_space=...  8.08 us
    ppermute x6, starting transfers between devices, scattered(): lax.ppermute(given, axis, [(i, i ^ reach) for i in range(size)]).astype(F32)  7.95 us
    pallas_call x1, Pallas kernels, occ(): pl.pallas_call(lambda *refs: occ_kernel(*refs, groups=groups, which=which...  7.59 us
    pallas_call x1, Pallas kernels, both(): pl.pallas_call(lambda *refs: both_kernel(*refs, slices=slices), in_specs=...  6.94 us
    pallas_call x2, Pallas kernels, product(): pl.pallas_call(lambda *refs: product_kernel(*refs, pieces=len(zs), steps=...  4.48 us
    unnamed x12, local copies, waits for them, and re-layouts  3.99 us
  transfers between devices with their start and end apart: 11, of which 5 were waited for; matrix products, arithmetic and copies ran while one was open for 2% of the time, Pallas kernels for 30%

profile of v8, /device:TPU:0, one launch (start us, length us, event | category | flops | bytes accessed | tf_op | source)
XLA Modules:
  0.0 131.7 jit_solution(9390043549376791306)
XLA Ops:
  1.3 0.0 copy-start.4
  1.3 0.7 copy-done.4
  2.0 0.0 copy-start.5
  2.0 3.2 %raw.1.refs_4_ = bf16[3088,512]{1,0:T(8,128)(2,1)} custom-call(s32[1]{0:T(128)} %bitcast.40.refs_0_, bf16[2,64,64]{2,1,0:T(8,128)(2,1)S(1)} %bitcast.51, bf16[640,4096]{1,0:T(8,128)(2,1)} %bitcast.57), custom_call_target="tpu_custom_call" | custom-call | flops 1 | bytes 1 | tf_op jit(solution)/shard_map/raw/pallas_call | solution.py:165
  5.2 1.3 collective-permute-start.2
  6.5 0.0 copy-done.5
  6.6 6.9 %both_halves.1 = (bf16[48,64,256]{2,1,0:T(8,128)(2,1)}, bf16[16,64,256]{2,1,0:T(8,128)(2,1)}, bf16[640,2048]{1,0:T(8,128)(2,1)S(1)}, bf16[640,2048]{1,0:T(8,128)(2,1)}) custom-call(s32[1]{0:T(128)} %bitcast.41.refs_0_, bf16[2,64,64]{2,1,0:T(8,128)(2,1)S(1)} %bitcast.52, bf16[2,64,64]{2,1,0:T(8,128)(2,1)S(1)} %bitcast.54, bf16[640,4096]{1,0:T(8,128)(2,1)} %bitcast.58, ...), custom_call_target="tpu_custom_call" | custom-call | flops 1 | bytes 1 | tf_op jit(solution)/shard_map/both_halves/pallas_call | solution.py:469
  13.5 1.3 collective-permute-start.1
  14.8 1.3 collective-permute-start
  16.1 1.3 collective-permute-start.7
  17.4 7.6 %occ.1 = bf16[64,64,640]{2,1,0:T(8,128)(2,1)} custom-call(s32[1]{0:T(128)} %bitcast.42.refs_0_, bf16[2,64,64]{2,1,0:T(8,128)(2,1)S(1)} %bitcast.53, bf16[640,4096]{1,0:T(8,128)(2,1)} %bitcast.59, bf16[3072,256]{1,0:T(8,128)(2,1)} %bitcast.4.refs_3_), custom_call_target="tpu_custom_call" | custom-call | flops 1 | bytes 1 | tf_op jit(solution)/shard_map/occ/pallas_call | solution.py:268
  25.0 0.0 collective-permute-done.1.refs_3_
  25.0 6.1 %fold.2 = (bf16[640,2048]{1,0:T(8,128)(2,1)S(1)}, f32[640,640]{1,0:T(8,128)S(1)}) custom-call(s32[1]{0:T(128)} %bitcast.43.refs_0_, bf16[2,64,64]{2,1,0:T(8,128)(2,1)S(1)} %bitcast.55, bf16[640,4096]{1,0:T(8,128)(2,1)} %bitcast.60, bf16[640,2048]{1,0:T(8,128)(2,1)} %collective-permute-done.1.refs_3_, bf16[4096,640]{1,0:T(8,128)(2,1)} %bitcast.62), custom_call_target="tpu_custom_call" | custom-call | flops 1 | bytes 1 | tf_op jit(solution)/shard_map/fold/pallas_call | solution.py:395
  31.1 0.0 copy-start.2
  31.1 0.0 collective-permute-done.refs_3_
  31.1 7.2 %fold.3 = (bf16[640,2048]{1,0:T(8,128)(2,1)S(1)}, f32[640,640]{1,0:T(8,128)S(1)}) custom-call(s32[1]{0:T(128)} %bitcast.44.refs_0_, bf16[2,64,64]{2,1,0:T(8,128)(2,1)S(1)} %bitcast.56, bf16[640,4096]{1,0:T(8,128)(2,1)} %bitcast.61, bf16[640,2048]{1,0:T(8,128)(2,1)} %collective-permute-done.refs_3_, bf16[4096,640]{1,0:T(8,128)(2,1)} %bitcast.63, ...), custom_call_target="tpu_custom_call" | custom-call | flops 1 | bytes 1 | tf_op jit(solution)/shard_map/fold/pallas_call | solution.py:395
  38.3 0.0 copy-start
  38.3 1.5 %copy-done = bf16[640,2048]{1,0:T(8,128)(2,1)} copy-done((bf16[640,2048]{1,0:T(8,128)(2,1)}, bf16[640,2048]{1,0:T(8,128)(2,1)S(1)}, u32[]{:S(2)}) %copy-start) | copy-done | bytes 2621464
  39.8 39.9 %collective-permute-done.2.r_ref = bf16[3088,512]{1,0:T(8,128)(2,1)} collective-permute-done((bf16[3088,512]{1,0:T(8,128)(2,1)}, bf16[3088,512]{1,0:T(8,128)(2,1)}, u32[]{:S(2)}, u32[]{:S(2)}) %collective-permute-start.2) | collective-permute-done | bytes 3162144 | tf_op jit(solution)/shard_map/ppermute | solution.py:619
  79.7 0.0 copy-done.2
  79.7 8.1 %raw_product.1.refs_3_ = f32[384,640]{1,0:T(8,128)S(1)} custom-call(bf16[3088,512]{1,0:T(8,128)(2,1)} %collective-permute-done.2.r_ref, bf16[640,2048]{1,0:T(8,128)(2,1)S(1)} %get-tuple-element.15.rest_0_.refs_1_, bf16[640,2048]{1,0:T(8,128)(2,1)} %copy-done, f32[640,640]{1,0:T(8,128)S(1)} %get-tuple-element.14.rest_2_), custom_call_target="tpu_custom_call" | custom-call | flops 1 | bytes 1 | tf_op jit(solution)/shard_map/raw_product/pallas_call | solution.py:226
  87.8 1.0 fusion.12
  88.8 4.4 %collective-permute-start.3 = (bf16[256,640]{1,0:T(8,128)(2,1)}, bf16[256,640]{1,0:T(8,128)(2,1)S(1)}, u32[]{:S(2)}, u32[]{:S(2)}) collective-permute-start(bf16[256,640]{1,0:T(8,128)(2,1)} %get-tuple-element.18), channel_id=1, source_target_pairs={{0,1},{1,0},{2,3},{3,2},{4,5},{5,4},{6,7},{7,6},{8,9},{9,8},{10,11... | collective-permute-start | bytes 983048 | tf_op jit(solution)/shard_map/ppermute | solution.py:590
  93.2 0.0 collective-permute-start.4
  93.2 1.4 %collective-permute-start.5 = (bf16[256,640]{1,0:T(8,128)(2,1)}, bf16[256,640]{1,0:T(8,128)(2,1)}, u32[]{:S(2)}, u32[]{:S(2)}) collective-permute-start(bf16[256,640]{1,0:T(8,128)(2,1)} %get-tuple-element.20), channel_id=1, source_target_pairs={{0,3},{1,2},{2,1},{3,0},{4,7},{5,6},{6,5},{7,4},{8,11},{9,10},{10,... | collective-permute-start | bytes 983048 | tf_op jit(solution)/shard_map/ppermute | solution.py:590
  94.5 1.3 collective-permute-start.6
  95.8 17.6 %collective-permute-done.7.refs_0_ = bf16[3072,256]{1,0:T(8,128)(2,1)} collective-permute-done((bf16[3072,256]{1,0:T(8,128)(2,1)}, bf16[3072,256]{1,0:T(8,128)(2,1)}, u32[]{:S(2)}, u32[]{:S(2)}) %collective-permute-start.7) | collective-permute-done | bytes 1572896 | tf_op jit(solution)/shard_map/ppermute | solution.py:619
  113.4 0.0 copy-start.3
  113.4 1.7 %copy-done.3 = bf16[640,2048]{1,0:T(8,128)(2,1)S(1)} copy-done((bf16[640,2048]{1,0:T(8,128)(2,1)S(1)}, bf16[640,2048]{1,0:T(8,128)(2,1)}, u32[]{:S(2)}) %copy-start.3) | copy-done | bytes 2621464
  115.1 3.9 %product.2.refs_2_ = f32[256,640]{1,0:T(8,128)S(1)} custom-call(bf16[3072,256]{1,0:T(8,128)(2,1)} %collective-permute-done.7.refs_0_, bf16[640,2048]{1,0:T(8,128)(2,1)S(1)} %copy-done.3, bf16[640,2048]{1,0:T(8,128)(2,1)} %copy-done, f32[384,640]{1,0:T(8,128)S(1)} %raw_product.1.refs_3_), custom_call_target="tpu_custom_call" | custom-call | flops 1 | bytes 1 | tf_op jit(solution)/shard_map/product/pallas_call | solution.py:560
  119.0 0.0 copy-start.1
  119.1 0.0 collective-permute-done.3
  119.1 0.0 collective-permute-done.4
  119.1 0.0 collective-permute-done.5
  119.1 1.4 %fusion.6.refs_3_ = f32[256,640]{1,0:T(8,128)S(1)} fusion(s32[]{:T(128)S(6)} %select_n.18, f32[4,160,640]{2,1,0:T(8,128)S(1)} %bitcast.48, f32[4,96,640]{2,1,0:T(8,128)S(1)} %bitcast.46, bf16[256,640]{1,0:T(8,128)(2,1)} %collective-permute-done.5, bf16[256,640]{1,0:T(8,128)(2,1)} %collective-permute-done.4, bf16[256,640]{1,0:T(8,128)(2,1)S(1)} %collective-permute-done.3), kind=kLoop, calls=%fused_computation.14 | loop fusion | flops 1146880 | bytes 4259844 | tf_op jit(solution)/shard_map/add | solution.py:590
  120.4 3.2 %collective-permute-done.6.refs_0_ = bf16[1024,256]{1,0:T(8,128)(2,1)S(1)} collective-permute-done((bf16[1024,256]{1,0:T(8,128)(2,1)}, bf16[1024,256]{1,0:T(8,128)(2,1)S(1)}, u32[]{:S(2)}, u32[]{:S(2)}) %collective-permute-start.6) | collective-permute-done | bytes 524320 | tf_op jit(solution)/shard_map/ppermute | solution.py:619
  123.7 0.0 copy-done.1
  123.7 0.6 product.3
  124.3 0.4 collective-permute-start.10
  124.7 1.6 %collective-permute-start.8 = (bf16[64,640]{1,0:T(8,128)(2,1)S(1)}, bf16[64,640]{1,0:T(8,128)(2,1)S(1)}, u32[]{:S(2)}, u32[]{:S(2)}) collective-permute-start(bf16[64,640]{1,0:T(8,128)(2,1)S(1)} %get-tuple-element.21), channel_id=1, source_target_pairs={{0,1},{1,0},{2,3},{3,2},{4,5},{5,4},{6,7},{7,6},{8,9},{9,8},{10,11... | collective-permute-start | bytes 245768 | tf_op jit(solution)/shard_map/ppermute | solution.py:590
  126.3 0.3 collective-permute-start.9
  126.5 0.8 slice_bitcast_fusion
  127.3 1.5 %collective-permute-done.10 = bf16[64,640]{1,0:T(8,128)(2,1)S(1)} collective-permute-done((bf16[64,640]{1,0:T(8,128)(2,1)S(1)}, bf16[64,640]{1,0:T(8,128)(2,1)S(1)}, u32[]{:S(2)}, u32[]{:S(2)}) %collective-permute-start.10) | collective-permute-done | bytes 81952 | tf_op jit(solution)/shard_map/ppermute | solution.py:590
  128.8 0.0 collective-permute-done.8
  128.8 2.1 %collective-permute-done.9 = bf16[64,640]{1,0:T(8,128)(2,1)S(1)} collective-permute-done((bf16[64,640]{1,0:T(8,128)(2,1)S(1)}, bf16[64,640]{1,0:T(8,128)(2,1)S(1)}, u32[]{:S(2)}, u32[]{:S(2)}) %collective-permute-start.9) | collective-permute-done | bytes 81952 | tf_op jit(solution)/shard_map/ppermute | solution.py:590
  130.9 0.8 maximum_bitcast_fusion
  (3 shorter events, 0.1 us)
Async XLA Ops:
  1.3 0.8 copy-start.4
  2.0 4.5 %copy-start.5 = (bf16[1,2,64,64]{3,2,1,0:T(8,128)(2,1)S(1)}, bf16[1,2,64,64]{3,2,1,0:T(8,128)(2,1)}, u32[]{:S(2)}) copy-start(bf16[1,2,64,64]{3,2,1,0:T(8,128)(2,1)} %param.6) | copy-start | bytes 49156
  5.2 74.4 %collective-permute-start.2 = (bf16[3088,512]{1,0:T(8,128)(2,1)}, bf16[3088,512]{1,0:T(8,128)(2,1)}, u32[]{:S(2)}, u32[]{:S(2)}) collective-permute-start(bf16[3088,512]{1,0:T(8,128)(2,1)} %raw.1.refs_4_), channel_id=1, source_target_pairs={{4,0},{8,4},{12,8},{16,12},{20,16},{24,20},{28,24},{5,1},{9,5},{13... | collective-permute-start | bytes 9486344 | tf_op jit(solution)/shard_map/ppermute | solution.py:619
  13.5 11.5 %collective-permute-start.1 = (bf16[640,2048]{1,0:T(8,128)(2,1)S(1)}, bf16[640,2048]{1,0:T(8,128)(2,1)}, u32[]{:S(2)}, u32[]{:S(2)}) collective-permute-start(bf16[640,2048]{1,0:T(8,128)(2,1)S(1)} %get-tuple-element.12), channel_id=1, source_target_pairs={{1,0},{2,1},{3,2},{5,4},{6,5},{7,6},{9,8},{10,9},{11,10},{13,12},{... | collective-permute-start | bytes 7864328 | tf_op jit(solution)/shard_map/ppermute | solution.py:627
  14.8 16.3 %collective-permute-start = (bf16[640,2048]{1,0:T(8,128)(2,1)}, bf16[640,2048]{1,0:T(8,128)(2,1)}, u32[]{:S(2)}, u32[]{:S(2)}) collective-permute-start(bf16[640,2048]{1,0:T(8,128)(2,1)} %get-tuple-element.10), channel_id=1, source_target_pairs={{1,0},{2,1},{3,2},{5,4},{6,5},{7,6},{9,8},{10,9},{11,10},{13,12},{... | collective-permute-start | bytes 7864328 | tf_op jit(solution)/shard_map/ppermute | solution.py:627
  16.1 97.3 %collective-permute-start.7 = (bf16[3072,256]{1,0:T(8,128)(2,1)}, bf16[3072,256]{1,0:T(8,128)(2,1)}, u32[]{:S(2)}, u32[]{:S(2)}) collective-permute-start(bf16[3072,256]{1,0:T(8,128)(2,1)} %bitcast.4.refs_3_), channel_id=1, source_target_pairs={{4,0},{8,4},{12,8},{16,12},{20,16},{24,20},{28,24},{5,1},{9,5},{13... | collective-permute-start | bytes 4718600 | tf_op jit(solution)/shard_map/ppermute | solution.py:619
  31.1 48.6 %copy-start.2 = (bf16[640,2048]{1,0:T(8,128)(2,1)}, bf16[640,2048]{1,0:T(8,128)(2,1)S(1)}, u32[]{:S(2)}) copy-start(bf16[640,2048]{1,0:T(8,128)(2,1)S(1)} %get-tuple-element.15.rest_0_.refs_1_) | copy-start | bytes 7864324
  38.3 1.5 %copy-start = (bf16[640,2048]{1,0:T(8,128)(2,1)}, bf16[640,2048]{1,0:T(8,128)(2,1)S(1)}, u32[]{:S(2)}) copy-start(bf16[640,2048]{1,0:T(8,128)(2,1)S(1)} %get-tuple-element.16.rest_1_.refs_2_.refs_1_) | copy-start | bytes 7864324
  88.8 30.3 %collective-permute-start.3 = (bf16[256,640]{1,0:T(8,128)(2,1)}, bf16[256,640]{1,0:T(8,128)(2,1)S(1)}, u32[]{:S(2)}, u32[]{:S(2)}) collective-permute-start(bf16[256,640]{1,0:T(8,128)(2,1)} %get-tuple-element.18), channel_id=1, source_target_pairs={{0,1},{1,0},{2,3},{3,2},{4,5},{5,4},{6,7},{7,6},{8,9},{9,8},{10,11... | collective-permute-start | bytes 983048 | tf_op jit(solution)/shard_map/ppermute | solution.py:590
  93.2 25.9 %collective-permute-start.4 = (bf16[256,640]{1,0:T(8,128)(2,1)}, bf16[256,640]{1,0:T(8,128)(2,1)}, u32[]{:S(2)}, u32[]{:S(2)}) collective-permute-start(bf16[256,640]{1,0:T(8,128)(2,1)} %get-tuple-element.19), channel_id=1, source_target_pairs={{0,2},{1,3},{2,0},{3,1},{4,6},{5,7},{6,4},{7,5},{8,10},{9,11},{10,... | collective-permute-start | bytes 983048 | tf_op jit(solution)/shard_map/ppermute | solution.py:590
  93.2 25.9 %collective-permute-start.5 = (bf16[256,640]{1,0:T(8,128)(2,1)}, bf16[256,640]{1,0:T(8,128)(2,1)}, u32[]{:S(2)}, u32[]{:S(2)}) collective-permute-start(bf16[256,640]{1,0:T(8,128)(2,1)} %get-tuple-element.20), channel_id=1, source_target_pairs={{0,3},{1,2},{2,1},{3,0},{4,7},{5,6},{6,5},{7,4},{8,11},{9,10},{10,... | collective-permute-start | bytes 983048 | tf_op jit(solution)/shard_map/ppermute | solution.py:590
  94.5 29.2 %collective-permute-start.6 = (bf16[1024,256]{1,0:T(8,128)(2,1)}, bf16[1024,256]{1,0:T(8,128)(2,1)S(1)}, u32[]{:S(2)}, u32[]{:S(2)}) collective-permute-start(bf16[1024,256]{1,0:T(8,128)(2,1)} %bitcast.13), channel_id=1, source_target_pairs={{4,0},{8,4},{12,8},{16,12},{20,16},{24,20},{28,24},{5,1},{9,5},{13... | collective-permute-start | bytes 1572872 | tf_op jit(solution)/shard_map/ppermute | solution.py:619
  113.4 1.7 %copy-start.3 = (bf16[640,2048]{1,0:T(8,128)(2,1)S(1)}, bf16[640,2048]{1,0:T(8,128)(2,1)}, u32[]{:S(2)}) copy-start(bf16[640,2048]{1,0:T(8,128)(2,1)} %copy-done.2) | copy-start | bytes 7864324
  119.0 4.7 %copy-start.1 = (bf16[640,2048]{1,0:T(8,128)(2,1)S(1)}, bf16[640,2048]{1,0:T(8,128)(2,1)}, u32[]{:S(2)}) copy-start(bf16[640,2048]{1,0:T(8,128)(2,1)} %copy-done) | copy-start | bytes 7864324
  124.3 4.5 %collective-permute-start.10 = (bf16[64,640]{1,0:T(8,128)(2,1)S(1)}, bf16[64,640]{1,0:T(8,128)(2,1)S(1)}, u32[]{:S(2)}, u32[]{:S(2)}) collective-permute-start(bf16[64,640]{1,0:T(8,128)(2,1)S(1)} %get-tuple-element.22), channel_id=1, source_target_pairs={{0,3},{1,2},{2,1},{3,0},{4,7},{5,6},{6,5},{7,4},{8,11},{9,10},{10,... | collective-permute-start | bytes 245768 | tf_op jit(solution)/shard_map/ppermute | solution.py:590
  124.7 4.1 %collective-permute-start.8 = (bf16[64,640]{1,0:T(8,128)(2,1)S(1)}, bf16[64,640]{1,0:T(8,128)(2,1)S(1)}, u32[]{:S(2)}, u32[]{:S(2)}) collective-permute-start(bf16[64,640]{1,0:T(8,128)(2,1)S(1)} %get-tuple-element.21), channel_id=1, source_target_pairs={{0,1},{1,0},{2,3},{3,2},{4,5},{5,4},{6,7},{7,6},{8,9},{9,8},{10,11... | collective-permute-start | bytes 245768 | tf_op jit(solution)/shard_map/ppermute | solution.py:590
  126.3 4.6 %collective-permute-start.9 = (bf16[64,640]{1,0:T(8,128)(2,1)S(1)}, bf16[64,640]{1,0:T(8,128)(2,1)S(1)}, u32[]{:S(2)}, u32[]{:S(2)}) collective-permute-start(bf16[64,640]{1,0:T(8,128)(2,1)S(1)} %get-tuple-element.23), channel_id=1, source_target_pairs={{0,2},{1,3},{2,0},{3,1},{4,6},{5,7},{6,4},{7,5},{8,10},{9,11},{10,... | collective-permute-start | bytes 245768 | tf_op jit(solution)/shard_map/ppermute | solution.py:590

commit v9 on v8

--- a/solution.py
+++ b/solution.py
@@ -10,7 +10,7 @@
 VMEM_BYTES = 48 * 1024 * 1024
 SPAN = 256
 SUBLANES = 8
-CHUNKS = (384, 256)
+LANES = 128
 PIECES = 2
 IN_STEPS = 4
 CUTS = (3, 1)
@@ -601,9 +601,10 @@
 
 def chunks_of(aux, owners):
     each = aux // owners
-    parts = [n // owners for n in CHUNKS]
-    if aux == sum(CHUNKS) and all(n % (16 * owners) == 0 for n in CHUNKS):
-        cuts = [sum(parts[:i]) for i in range(len(parts) + 1)]
+    final = aux * 2 // 5 // LANES * LANES
+    parts = [(aux - final) // owners, final // owners]
+    if final and (aux - final) % LANES == 0 and all(n % (16 * owners) == 0 for n in (aux - final, final)):
+        cuts = [0, parts[0], each]
         return [[(j * each + a, b - a) for j in range(owners)] for a, b in zip(cuts, cuts[1:])]
     return [[(0, aux)]]
 

time: 132 us -> 132 us (level)
  no operation moved by 1% of the time
where the time goes in v9:
time: 132 us
  waiting for transfers between devices  64.3 us (49%)
  Pallas kernels  43.5 us (33%)
  starting transfers between devices  14.4 us (11%)
  local copies, waits for them, and re-layouts  4.83 us (4%)
  other arithmetic  3.17 us (2%)
  between operations  1.51 us (1%)
    ppermute x3, waiting for transfers between devices, body(): send = lambda half: lax.ppermute(half, 'row', up_row)  60.7 us
    pallas_call x2, Pallas kernels, fold(): pl.pallas_call(lambda *refs: fold_kernel(*refs, started=bool(added), turn...  13.3 us
    pallas_call x1, Pallas kernels, raw_product(): pl.pallas_call(raw_product_kernel, in_specs=[*[pl.BlockSpec(memory_space=...  8.08 us
    ppermute x6, starting transfers between devices, scattered(): lax.ppermute(given, axis, [(i, i ^ reach) for i in range(size)]).astype(F32)  7.95 us
    pallas_call x1, Pallas kernels, occ(): pl.pallas_call(lambda *refs: occ_kernel(*refs, groups=groups, which=which...  7.59 us
    pallas_call x1, Pallas kernels, both(): pl.pallas_call(lambda *refs: both_kernel(*refs, slices=slices), in_specs=...  6.94 us
    pallas_call x2, Pallas kernels, product(): pl.pallas_call(lambda *refs: product_kernel(*refs, pieces=len(zs), steps=...  4.48 us
    unnamed x12, local copies, waits for them, and re-layouts  3.99 us
  transfers between devices with their start and end apart: 11, of which 5 were waited for; matrix products, arithmetic and copies ran while one was open for 2% of the time, Pallas kernels for 30%

profile of v9, /device:TPU:0, one launch (start us, length us, event | category | flops | bytes accessed | tf_op | source)
XLA Modules:
  0.0 131.7 jit_solution(9390043549376791306)
XLA Ops:
  1.3 0.0 copy-start.4
  1.3 0.7 copy-done.4
  2.0 0.0 copy-start.5
  2.0 3.2 %raw.1.refs_4_ = bf16[3088,512]{1,0:T(8,128)(2,1)} custom-call(s32[1]{0:T(128)} %bitcast.40.refs_0_, bf16[2,64,64]{2,1,0:T(8,128)(2,1)S(1)} %bitcast.51, bf16[640,4096]{1,0:T(8,128)(2,1)} %bitcast.57), custom_call_target="tpu_custom_call" | custom-call | flops 1 | bytes 1 | tf_op jit(solution)/shard_map/raw/pallas_call | solution.py:165
  5.2 1.3 collective-permute-start.2
  6.5 0.0 copy-done.5
  6.6 6.9 %both_halves.1 = (bf16[48,64,256]{2,1,0:T(8,128)(2,1)}, bf16[16,64,256]{2,1,0:T(8,128)(2,1)}, bf16[640,2048]{1,0:T(8,128)(2,1)S(1)}, bf16[640,2048]{1,0:T(8,128)(2,1)}) custom-call(s32[1]{0:T(128)} %bitcast.41.refs_0_, bf16[2,64,64]{2,1,0:T(8,128)(2,1)S(1)} %bitcast.52, bf16[2,64,64]{2,1,0:T(8,128)(2,1)S(1)} %bitcast.54, bf16[640,4096]{1,0:T(8,128)(2,1)} %bitcast.58, ...), custom_call_target="tpu_custom_call" | custom-call | flops 1 | bytes 1 | tf_op jit(solution)/shard_map/both_halves/pallas_call | solution.py:469
  13.5 1.3 collective-permute-start.1
  14.8 1.3 collective-permute-start
  16.1 1.3 collective-permute-start.7
  17.4 7.6 %occ.1 = bf16[64,64,640]{2,1,0:T(8,128)(2,1)} custom-call(s32[1]{0:T(128)} %bitcast.42.refs_0_, bf16[2,64,64]{2,1,0:T(8,128)(2,1)S(1)} %bitcast.53, bf16[640,4096]{1,0:T(8,128)(2,1)} %bitcast.59, bf16[3072,256]{1,0:T(8,128)(2,1)} %bitcast.4.refs_3_), custom_call_target="tpu_custom_call" | custom-call | flops 1 | bytes 1 | tf_op jit(solution)/shard_map/occ/pallas_call | solution.py:268
  25.0 0.0 collective-permute-done.1.refs_3_
  25.0 6.1 %fold.2 = (bf16[640,2048]{1,0:T(8,128)(2,1)S(1)}, f32[640,640]{1,0:T(8,128)S(1)}) custom-call(s32[1]{0:T(128)} %bitcast.43.refs_0_, bf16[2,64,64]{2,1,0:T(8,128)(2,1)S(1)} %bitcast.55, bf16[640,4096]{1,0:T(8,128)(2,1)} %bitcast.60, bf16[640,2048]{1,0:T(8,128)(2,1)} %collective-permute-done.1.refs_3_, bf16[4096,640]{1,0:T(8,128)(2,1)} %bitcast.62), custom_call_target="tpu_custom_call" | custom-call | flops 1 | bytes 1 | tf_op jit(solution)/shard_map/fold/pallas_call | solution.py:395
  31.1 0.0 copy-start.2
  31.1 0.0 collective-permute-done.refs_3_
  31.1 7.2 %fold.3 = (bf16[640,2048]{1,0:T(8,128)(2,1)S(1)}, f32[640,640]{1,0:T(8,128)S(1)}) custom-call(s32[1]{0:T(128)} %bitcast.44.refs_0_, bf16[2,64,64]{2,1,0:T(8,128)(2,1)S(1)} %bitcast.56, bf16[640,4096]{1,0:T(8,128)(2,1)} %bitcast.61, bf16[640,2048]{1,0:T(8,128)(2,1)} %collective-permute-done.refs_3_, bf16[4096,640]{1,0:T(8,128)(2,1)} %bitcast.63, ...), custom_call_target="tpu_custom_call" | custom-call | flops 1 | bytes 1 | tf_op jit(solution)/shard_map/fold/pallas_call | solution.py:395
  38.3 0.0 copy-start
  38.3 1.5 %copy-done = bf16[640,2048]{1,0:T(8,128)(2,1)} copy-done((bf16[640,2048]{1,0:T(8,128)(2,1)}, bf16[640,2048]{1,0:T(8,128)(2,1)S(1)}, u32[]{:S(2)}) %copy-start) | copy-done | bytes 2621464
  39.8 39.9 %collective-permute-done.2.r_ref = bf16[3088,512]{1,0:T(8,128)(2,1)} collective-permute-done((bf16[3088,512]{1,0:T(8,128)(2,1)}, bf16[3088,512]{1,0:T(8,128)(2,1)}, u32[]{:S(2)}, u32[]{:S(2)}) %collective-permute-start.2) | collective-permute-done | bytes 3162144 | tf_op jit(solution)/shard_map/ppermute | solution.py:620
  79.7 0.0 copy-done.2
  79.7 8.1 %raw_product.1.refs_3_ = f32[384,640]{1,0:T(8,128)S(1)} custom-call(bf16[3088,512]{1,0:T(8,128)(2,1)} %collective-permute-done.2.r_ref, bf16[640,2048]{1,0:T(8,128)(2,1)S(1)} %get-tuple-element.15.rest_0_.refs_1_, bf16[640,2048]{1,0:T(8,128)(2,1)} %copy-done, f32[640,640]{1,0:T(8,128)S(1)} %get-tuple-element.14.rest_2_), custom_call_target="tpu_custom_call" | custom-call | flops 1 | bytes 1 | tf_op jit(solution)/shard_map/raw_product/pallas_call | solution.py:226
  87.8 1.0 fusion.12
  88.8 4.4 %collective-permute-start.3 = (bf16[256,640]{1,0:T(8,128)(2,1)}, bf16[256,640]{1,0:T(8,128)(2,1)S(1)}, u32[]{:S(2)}, u32[]{:S(2)}) collective-permute-start(bf16[256,640]{1,0:T(8,128)(2,1)} %get-tuple-element.18), channel_id=1, source_target_pairs={{0,1},{1,0},{2,3},{3,2},{4,5},{5,4},{6,7},{7,6},{8,9},{9,8},{10,11... | collective-permute-start | bytes 983048 | tf_op jit(solution)/shard_map/ppermute | solution.py:590
  93.2 0.0 collective-permute-start.4
  93.2 1.4 %collective-permute-start.5 = (bf16[256,640]{1,0:T(8,128)(2,1)}, bf16[256,640]{1,0:T(8,128)(2,1)}, u32[]{:S(2)}, u32[]{:S(2)}) collective-permute-start(bf16[256,640]{1,0:T(8,128)(2,1)} %get-tuple-element.20), channel_id=1, source_target_pairs={{0,3},{1,2},{2,1},{3,0},{4,7},{5,6},{6,5},{7,4},{8,11},{9,10},{10,... | collective-permute-start | bytes 983048 | tf_op jit(solution)/shard_map/ppermute | solution.py:590
  94.5 1.3 collective-permute-start.6
  95.8 17.6 %collective-permute-done.7.refs_0_ = bf16[3072,256]{1,0:T(8,128)(2,1)} collective-permute-done((bf16[3072,256]{1,0:T(8,128)(2,1)}, bf16[3072,256]{1,0:T(8,128)(2,1)}, u32[]{:S(2)}, u32[]{:S(2)}) %collective-permute-start.7) | collective-permute-done | bytes 1572896 | tf_op jit(solution)/shard_map/ppermute | solution.py:620
  113.4 0.0 copy-start.3
  113.4 1.7 %copy-done.3 = bf16[640,2048]{1,0:T(8,128)(2,1)S(1)} copy-done((bf16[640,2048]{1,0:T(8,128)(2,1)S(1)}, bf16[640,2048]{1,0:T(8,128)(2,1)}, u32[]{:S(2)}) %copy-start.3) | copy-done | bytes 2621464
  115.1 3.9 %product.2.refs_2_ = f32[256,640]{1,0:T(8,128)S(1)} custom-call(bf16[3072,256]{1,0:T(8,128)(2,1)} %collective-permute-done.7.refs_0_, bf16[640,2048]{1,0:T(8,128)(2,1)S(1)} %copy-done.3, bf16[640,2048]{1,0:T(8,128)(2,1)} %copy-done, f32[384,640]{1,0:T(8,128)S(1)} %raw_product.1.refs_3_), custom_call_target="tpu_custom_call" | custom-call | flops 1 | bytes 1 | tf_op jit(solution)/shard_map/product/pallas_call | solution.py:560
  119.0 0.0 copy-start.1
  119.1 0.0 collective-permute-done.3
  119.1 0.0 collective-permute-done.4
  119.1 0.0 collective-permute-done.5
  119.1 1.4 %fusion.6.refs_3_ = f32[256,640]{1,0:T(8,128)S(1)} fusion(s32[]{:T(128)S(6)} %select_n.18, f32[4,160,640]{2,1,0:T(8,128)S(1)} %bitcast.48, f32[4,96,640]{2,1,0:T(8,128)S(1)} %bitcast.46, bf16[256,640]{1,0:T(8,128)(2,1)} %collective-permute-done.5, bf16[256,640]{1,0:T(8,128)(2,1)} %collective-permute-done.4, bf16[256,640]{1,0:T(8,128)(2,1)S(1)} %collective-permute-done.3), kind=kLoop, calls=%fused_computation.14 | loop fusion | flops 1146880 | bytes 4259844 | tf_op jit(solution)/shard_map/add | solution.py:590
  120.4 3.2 %collective-permute-done.6.refs_0_ = bf16[1024,256]{1,0:T(8,128)(2,1)S(1)} collective-permute-done((bf16[1024,256]{1,0:T(8,128)(2,1)}, bf16[1024,256]{1,0:T(8,128)(2,1)S(1)}, u32[]{:S(2)}, u32[]{:S(2)}) %collective-permute-start.6) | collective-permute-done | bytes 524320 | tf_op jit(solution)/shard_map/ppermute | solution.py:620
  123.7 0.0 copy-done.1
  123.7 0.6 product.3
  124.3 0.4 collective-permute-start.10
  124.7 1.6 %collective-permute-start.8 = (bf16[64,640]{1,0:T(8,128)(2,1)S(1)}, bf16[64,640]{1,0:T(8,128)(2,1)S(1)}, u32[]{:S(2)}, u32[]{:S(2)}) collective-permute-start(bf16[64,640]{1,0:T(8,128)(2,1)S(1)} %get-tuple-element.21), channel_id=1, source_target_pairs={{0,1},{1,0},{2,3},{3,2},{4,5},{5,4},{6,7},{7,6},{8,9},{9,8},{10,11... | collective-permute-start | bytes 245768 | tf_op jit(solution)/shard_map/ppermute | solution.py:590
  126.3 0.3 collective-permute-start.9
  126.5 0.8 slice_bitcast_fusion
  127.3 1.5 %collective-permute-done.10 = bf16[64,640]{1,0:T(8,128)(2,1)S(1)} collective-permute-done((bf16[64,640]{1,0:T(8,128)(2,1)S(1)}, bf16[64,640]{1,0:T(8,128)(2,1)S(1)}, u32[]{:S(2)}, u32[]{:S(2)}) %collective-permute-start.10) | collective-permute-done | bytes 81952 | tf_op jit(solution)/shard_map/ppermute | solution.py:590
  128.8 0.0 collective-permute-done.8
  128.8 2.1 %collective-permute-done.9 = bf16[64,640]{1,0:T(8,128)(2,1)S(1)} collective-permute-done((bf16[64,640]{1,0:T(8,128)(2,1)S(1)}, bf16[64,640]{1,0:T(8,128)(2,1)S(1)}, u32[]{:S(2)}, u32[]{:S(2)}) %collective-permute-start.9) | collective-permute-done | bytes 81952 | tf_op jit(solution)/shard_map/ppermute | solution.py:590
  130.9 0.8 maximum_bitcast_fusion
  (3 shorter events, 0.1 us)
Async XLA Ops:
  1.3 0.8 copy-start.4
  2.0 4.5 %copy-start.5 = (bf16[1,2,64,64]{3,2,1,0:T(8,128)(2,1)S(1)}, bf16[1,2,64,64]{3,2,1,0:T(8,128)(2,1)}, u32[]{:S(2)}) copy-start(bf16[1,2,64,64]{3,2,1,0:T(8,128)(2,1)} %param.6) | copy-start | bytes 49156
  5.2 74.4 %collective-permute-start.2 = (bf16[3088,512]{1,0:T(8,128)(2,1)}, bf16[3088,512]{1,0:T(8,128)(2,1)}, u32[]{:S(2)}, u32[]{:S(2)}) collective-permute-start(bf16[3088,512]{1,0:T(8,128)(2,1)} %raw.1.refs_4_), channel_id=1, source_target_pairs={{4,0},{8,4},{12,8},{16,12},{20,16},{24,20},{28,24},{5,1},{9,5},{13... | collective-permute-start | bytes 9486344 | tf_op jit(solution)/shard_map/ppermute | solution.py:620
  13.5 11.5 %collective-permute-start.1 = (bf16[640,2048]{1,0:T(8,128)(2,1)S(1)}, bf16[640,2048]{1,0:T(8,128)(2,1)}, u32[]{:S(2)}, u32[]{:S(2)}) collective-permute-start(bf16[640,2048]{1,0:T(8,128)(2,1)S(1)} %get-tuple-element.12), channel_id=1, source_target_pairs={{1,0},{2,1},{3,2},{5,4},{6,5},{7,6},{9,8},{10,9},{11,10},{13,12},{... | collective-permute-start | bytes 7864328 | tf_op jit(solution)/shard_map/ppermute | solution.py:628
  14.8 16.3 %collective-permute-start = (bf16[640,2048]{1,0:T(8,128)(2,1)}, bf16[640,2048]{1,0:T(8,128)(2,1)}, u32[]{:S(2)}, u32[]{:S(2)}) collective-permute-start(bf16[640,2048]{1,0:T(8,128)(2,1)} %get-tuple-element.10), channel_id=1, source_target_pairs={{1,0},{2,1},{3,2},{5,4},{6,5},{7,6},{9,8},{10,9},{11,10},{13,12},{... | collective-permute-start | bytes 7864328 | tf_op jit(solution)/shard_map/ppermute | solution.py:628
  16.1 97.3 %collective-permute-start.7 = (bf16[3072,256]{1,0:T(8,128)(2,1)}, bf16[3072,256]{1,0:T(8,128)(2,1)}, u32[]{:S(2)}, u32[]{:S(2)}) collective-permute-start(bf16[3072,256]{1,0:T(8,128)(2,1)} %bitcast.4.refs_3_), channel_id=1, source_target_pairs={{4,0},{8,4},{12,8},{16,12},{20,16},{24,20},{28,24},{5,1},{9,5},{13... | collective-permute-start | bytes 4718600 | tf_op jit(solution)/shard_map/ppermute | solution.py:620
  31.1 48.6 %copy-start.2 = (bf16[640,2048]{1,0:T(8,128)(2,1)}, bf16[640,2048]{1,0:T(8,128)(2,1)S(1)}, u32[]{:S(2)}) copy-start(bf16[640,2048]{1,0:T(8,128)(2,1)S(1)} %get-tuple-element.15.rest_0_.refs_1_) | copy-start | bytes 7864324
  38.3 1.5 %copy-start = (bf16[640,2048]{1,0:T(8,128)(2,1)}, bf16[640,2048]{1,0:T(8,128)(2,1)S(1)}, u32[]{:S(2)}) copy-start(bf16[640,2048]{1,0:T(8,128)(2,1)S(1)} %get-tuple-element.16.rest_1_.refs_2_.refs_1_) | copy-start | bytes 7864324
  88.8 30.3 %collective-permute-start.3 = (bf16[256,640]{1,0:T(8,128)(2,1)}, bf16[256,640]{1,0:T(8,128)(2,1)S(1)}, u32[]{:S(2)}, u32[]{:S(2)}) collective-permute-start(bf16[256,640]{1,0:T(8,128)(2,1)} %get-tuple-element.18), channel_id=1, source_target_pairs={{0,1},{1,0},{2,3},{3,2},{4,5},{5,4},{6,7},{7,6},{8,9},{9,8},{10,11... | collective-permute-start | bytes 983048 | tf_op jit(solution)/shard_map/ppermute | solution.py:590
  93.2 25.9 %collective-permute-start.4 = (bf16[256,640]{1,0:T(8,128)(2,1)}, bf16[256,640]{1,0:T(8,128)(2,1)}, u32[]{:S(2)}, u32[]{:S(2)}) collective-permute-start(bf16[256,640]{1,0:T(8,128)(2,1)} %get-tuple-element.19), channel_id=1, source_target_pairs={{0,2},{1,3},{2,0},{3,1},{4,6},{5,7},{6,4},{7,5},{8,10},{9,11},{10,... | collective-permute-start | bytes 983048 | tf_op jit(solution)/shard_map/ppermute | solution.py:590
  93.2 25.9 %collective-permute-start.5 = (bf16[256,640]{1,0:T(8,128)(2,1)}, bf16[256,640]{1,0:T(8,128)(2,1)}, u32[]{:S(2)}, u32[]{:S(2)}) collective-permute-start(bf16[256,640]{1,0:T(8,128)(2,1)} %get-tuple-element.20), channel_id=1, source_target_pairs={{0,3},{1,2},{2,1},{3,0},{4,7},{5,6},{6,5},{7,4},{8,11},{9,10},{10,... | collective-permute-start | bytes 983048 | tf_op jit(solution)/shard_map/ppermute | solution.py:590
  94.5 29.2 %collective-permute-start.6 = (bf16[1024,256]{1,0:T(8,128)(2,1)}, bf16[1024,256]{1,0:T(8,128)(2,1)S(1)}, u32[]{:S(2)}, u32[]{:S(2)}) collective-permute-start(bf16[1024,256]{1,0:T(8,128)(2,1)} %bitcast.13), channel_id=1, source_target_pairs={{4,0},{8,4},{12,8},{16,12},{20,16},{24,20},{28,24},{5,1},{9,5},{13... | collective-permute-start | bytes 1572872 | tf_op jit(solution)/shard_map/ppermute | solution.py:620
  113.4 1.7 %copy-start.3 = (bf16[640,2048]{1,0:T(8,128)(2,1)S(1)}, bf16[640,2048]{1,0:T(8,128)(2,1)}, u32[]{:S(2)}) copy-start(bf16[640,2048]{1,0:T(8,128)(2,1)} %copy-done.2) | copy-start | bytes 7864324
  119.0 4.7 %copy-start.1 = (bf16[640,2048]{1,0:T(8,128)(2,1)S(1)}, bf16[640,2048]{1,0:T(8,128)(2,1)}, u32[]{:S(2)}) copy-start(bf16[640,2048]{1,0:T(8,128)(2,1)} %copy-done) | copy-start | bytes 7864324
  124.3 4.5 %collective-permute-start.10 = (bf16[64,640]{1,0:T(8,128)(2,1)S(1)}, bf16[64,640]{1,0:T(8,128)(2,1)S(1)}, u32[]{:S(2)}, u32[]{:S(2)}) collective-permute-start(bf16[64,640]{1,0:T(8,128)(2,1)S(1)} %get-tuple-element.22), channel_id=1, source_target_pairs={{0,3},{1,2},{2,1},{3,0},{4,7},{5,6},{6,5},{7,4},{8,11},{9,10},{10,... | collective-permute-start | bytes 245768 | tf_op jit(solution)/shard_map/ppermute | solution.py:590
  124.7 4.1 %collective-permute-start.8 = (bf16[64,640]{1,0:T(8,128)(2,1)S(1)}, bf16[64,640]{1,0:T(8,128)(2,1)S(1)}, u32[]{:S(2)}, u32[]{:S(2)}) collective-permute-start(bf16[64,640]{1,0:T(8,128)(2,1)S(1)} %get-tuple-element.21), channel_id=1, source_target_pairs={{0,1},{1,0},{2,3},{3,2},{4,5},{5,4},{6,7},{7,6},{8,9},{9,8},{10,11... | collective-permute-start | bytes 245768 | tf_op jit(solution)/shard_map/ppermute | solution.py:590
  126.3 4.6 %collective-permute-start.9 = (bf16[64,640]{1,0:T(8,128)(2,1)S(1)}, bf16[64,640]{1,0:T(8,128)(2,1)S(1)}, u32[]{:S(2)}, u32[]{:S(2)}) collective-permute-start(bf16[64,640]{1,0:T(8,128)(2,1)S(1)} %get-tuple-element.23), channel_id=1, source_target_pairs={{0,2},{1,3},{2,0},{3,1},{4,6},{5,7},{6,4},{7,5},{8,10},{9,11},{10,... | collective-permute-start | bytes 245768 | tf_op jit(solution)/shard_map/ppermute | solution.py:590

commit v10 on v9

--- a/solution.py
+++ b/solution.py
@@ -622,7 +622,8 @@
     chunked = len(chunks) > 1
     last = ()
     if chunked:
-        last = [raw(live, green_occ[0], y, chunks[0])]
+        halved = [(a + i, n // 2) for a, n in chunks[0] for i in (0, n // 2)] if chunks[0][0][1] % 32 == 0 else chunks[0]
+        last = [raw(live, green_occ[0], y, halved)]
         unfolded = send(last[0])
     halves, over = both(live, green_occ[0], green_vir[0], y, chunks[-1], last)
     shifted = [lax.ppermute(piece, "col", up_col) for piece in over]

time: 132 us -> 132 us (level)
  no operation moved by 1% of the time
where the time goes in v10:
time: 132 us
  waiting for transfers between devices  64.3 us (49%)
  Pallas kernels  43.7 us (33%)
  starting transfers between devices  14.4 us (11%)
  local copies, waits for them, and re-layouts  4.83 us (4%)
  other arithmetic  3.17 us (2%)
  between operations  1.51 us (1%)
    ppermute x3, waiting for transfers between devices, body(): send = lambda half: lax.ppermute(half, 'row', up_row)  60.7 us
    pallas_call x2, Pallas kernels, fold(): pl.pallas_call(lambda *refs: fold_kernel(*refs, started=bool(added), turn...  13.3 us
    pallas_call x1, Pallas kernels, raw_product(): pl.pallas_call(raw_product_kernel, in_specs=[*[pl.BlockSpec(memory_space=...  8.08 us
    ppermute x6, starting transfers between devices, scattered(): lax.ppermute(given, axis, [(i, i ^ reach) for i in range(size)]).astype(F32)  7.94 us
    pallas_call x1, Pallas kernels, occ(): pl.pallas_call(lambda *refs: occ_kernel(*refs, groups=groups, which=which...  7.6 us
    pallas_call x1, Pallas kernels, both(): pl.pallas_call(lambda *refs: both_kernel(*refs, slices=slices), in_specs=...  6.94 us
    pallas_call x2, Pallas kernels, product(): pl.pallas_call(lambda *refs: product_kernel(*refs, pieces=len(zs), steps=...  4.48 us
    unnamed x12, local copies, waits for them, and re-layouts  3.99 us
  transfers between devices with their start and end apart: 11, of which 5 were waited for; matrix products, arithmetic and copies ran while one was open for 2% of the time, Pallas kernels for 30%

profile of v10, /device:TPU:0, one launch (start us, length us, event | category | flops | bytes accessed | tf_op | source)
XLA Modules:
  0.0 131.9 jit_solution(902055979406481378)
XLA Ops:
  1.3 0.0 copy-start.4
  1.3 0.7 copy-done.4
  2.0 0.0 copy-start.5
  2.0 3.4 %raw.1.refs_4_ = bf16[3088,512]{1,0:T(8,128)(2,1)} custom-call(s32[1]{0:T(128)} %bitcast.40.refs_0_, bf16[2,64,64]{2,1,0:T(8,128)(2,1)S(1)} %bitcast.51, bf16[640,4096]{1,0:T(8,128)(2,1)} %bitcast.57), custom_call_target="tpu_custom_call" | custom-call | flops 1 | bytes 1 | tf_op jit(solution)/shard_map/raw/pallas_call | solution.py:165
  5.4 1.3 collective-permute-start.2
  6.7 0.0 copy-done.5
  6.7 6.9 %both_halves.1 = (bf16[48,64,256]{2,1,0:T(8,128)(2,1)}, bf16[16,64,256]{2,1,0:T(8,128)(2,1)}, bf16[640,2048]{1,0:T(8,128)(2,1)S(1)}, bf16[640,2048]{1,0:T(8,128)(2,1)}) custom-call(s32[1]{0:T(128)} %bitcast.41.refs_0_, bf16[2,64,64]{2,1,0:T(8,128)(2,1)S(1)} %bitcast.52, bf16[2,64,64]{2,1,0:T(8,128)(2,1)S(1)} %bitcast.54, bf16[640,4096]{1,0:T(8,128)(2,1)} %bitcast.58, ...), custom_call_target="tpu_custom_call" | custom-call | flops 1 | bytes 1 | tf_op jit(solution)/shard_map/both_halves/pallas_call | solution.py:469
  13.7 1.3 collective-permute-start.1
  15.0 1.3 collective-permute-start
  16.3 1.3 collective-permute-start.7
  17.6 7.6 %occ.1 = bf16[64,64,640]{2,1,0:T(8,128)(2,1)} custom-call(s32[1]{0:T(128)} %bitcast.42.refs_0_, bf16[2,64,64]{2,1,0:T(8,128)(2,1)S(1)} %bitcast.53, bf16[640,4096]{1,0:T(8,128)(2,1)} %bitcast.59, bf16[3072,256]{1,0:T(8,128)(2,1)} %bitcast.4.refs_3_), custom_call_target="tpu_custom_call" | custom-call | flops 1 | bytes 1 | tf_op jit(solution)/shard_map/occ/pallas_call | solution.py:268
  25.2 0.0 collective-permute-done.1.refs_3_
  25.2 6.1 %fold.2 = (bf16[640,2048]{1,0:T(8,128)(2,1)S(1)}, f32[640,640]{1,0:T(8,128)S(1)}) custom-call(s32[1]{0:T(128)} %bitcast.43.refs_0_, bf16[2,64,64]{2,1,0:T(8,128)(2,1)S(1)} %bitcast.55, bf16[640,4096]{1,0:T(8,128)(2,1)} %bitcast.60, bf16[640,2048]{1,0:T(8,128)(2,1)} %collective-permute-done.1.refs_3_, bf16[4096,640]{1,0:T(8,128)(2,1)} %bitcast.62), custom_call_target="tpu_custom_call" | custom-call | flops 1 | bytes 1 | tf_op jit(solution)/shard_map/fold/pallas_call | solution.py:395
  31.3 0.0 copy-start.2
  31.3 0.0 collective-permute-done.refs_3_
  31.3 7.2 %fold.3 = (bf16[640,2048]{1,0:T(8,128)(2,1)S(1)}, f32[640,640]{1,0:T(8,128)S(1)}) custom-call(s32[1]{0:T(128)} %bitcast.44.refs_0_, bf16[2,64,64]{2,1,0:T(8,128)(2,1)S(1)} %bitcast.56, bf16[640,4096]{1,0:T(8,128)(2,1)} %bitcast.61, bf16[640,2048]{1,0:T(8,128)(2,1)} %collective-permute-done.refs_3_, bf16[4096,640]{1,0:T(8,128)(2,1)} %bitcast.63, ...), custom_call_target="tpu_custom_call" | custom-call | flops 1 | bytes 1 | tf_op jit(solution)/shard_map/fold/pallas_call | solution.py:395
  38.5 0.0 copy-start
  38.5 1.5 %copy-done = bf16[640,2048]{1,0:T(8,128)(2,1)} copy-done((bf16[640,2048]{1,0:T(8,128)(2,1)}, bf16[640,2048]{1,0:T(8,128)(2,1)S(1)}, u32[]{:S(2)}) %copy-start) | copy-done | bytes 2621464
  40.0 39.9 %collective-permute-done.2.r_ref = bf16[3088,512]{1,0:T(8,128)(2,1)} collective-permute-done((bf16[3088,512]{1,0:T(8,128)(2,1)}, bf16[3088,512]{1,0:T(8,128)(2,1)}, u32[]{:S(2)}, u32[]{:S(2)}) %collective-permute-start.2) | collective-permute-done | bytes 3162144 | tf_op jit(solution)/shard_map/ppermute | solution.py:620
  79.8 0.0 copy-done.2
  79.9 8.1 %raw_product.1.refs_3_ = f32[384,640]{1,0:T(8,128)S(1)} custom-call(bf16[3088,512]{1,0:T(8,128)(2,1)} %collective-permute-done.2.r_ref, bf16[640,2048]{1,0:T(8,128)(2,1)S(1)} %get-tuple-element.15.rest_0_.refs_1_, bf16[640,2048]{1,0:T(8,128)(2,1)} %copy-done, f32[640,640]{1,0:T(8,128)S(1)} %get-tuple-element.14.rest_2_), custom_call_target="tpu_custom_call" | custom-call | flops 1 | bytes 1 | tf_op jit(solution)/shard_map/raw_product/pallas_call | solution.py:226
  87.9 1.0 fusion.12
  88.9 4.4 %collective-permute-start.3 = (bf16[256,640]{1,0:T(8,128)(2,1)}, bf16[256,640]{1,0:T(8,128)(2,1)S(1)}, u32[]{:S(2)}, u32[]{:S(2)}) collective-permute-start(bf16[256,640]{1,0:T(8,128)(2,1)} %get-tuple-element.18), channel_id=1, source_target_pairs={{0,1},{1,0},{2,3},{3,2},{4,5},{5,4},{6,7},{7,6},{8,9},{9,8},{10,11... | collective-permute-start | bytes 983048 | tf_op jit(solution)/shard_map/ppermute | solution.py:590
  93.3 0.0 collective-permute-start.4
  93.3 1.4 %collective-permute-start.5 = (bf16[256,640]{1,0:T(8,128)(2,1)}, bf16[256,640]{1,0:T(8,128)(2,1)}, u32[]{:S(2)}, u32[]{:S(2)}) collective-permute-start(bf16[256,640]{1,0:T(8,128)(2,1)} %get-tuple-element.20), channel_id=1, source_target_pairs={{0,3},{1,2},{2,1},{3,0},{4,7},{5,6},{6,5},{7,4},{8,11},{9,10},{10,... | collective-permute-start | bytes 983048 | tf_op jit(solution)/shard_map/ppermute | solution.py:590
  94.7 1.3 collective-permute-start.6
  96.0 17.6 %collective-permute-done.7.refs_0_ = bf16[3072,256]{1,0:T(8,128)(2,1)} collective-permute-done((bf16[3072,256]{1,0:T(8,128)(2,1)}, bf16[3072,256]{1,0:T(8,128)(2,1)}, u32[]{:S(2)}, u32[]{:S(2)}) %collective-permute-start.7) | collective-permute-done | bytes 1572896 | tf_op jit(solution)/shard_map/ppermute | solution.py:620
  113.6 0.0 copy-start.3
  113.6 1.7 %copy-done.3 = bf16[640,2048]{1,0:T(8,128)(2,1)S(1)} copy-done((bf16[640,2048]{1,0:T(8,128)(2,1)S(1)}, bf16[640,2048]{1,0:T(8,128)(2,1)}, u32[]{:S(2)}) %copy-start.3) | copy-done | bytes 2621464
  115.3 3.9 %product.2.refs_2_ = f32[256,640]{1,0:T(8,128)S(1)} custom-call(bf16[3072,256]{1,0:T(8,128)(2,1)} %collective-permute-done.7.refs_0_, bf16[640,2048]{1,0:T(8,128)(2,1)S(1)} %copy-done.3, bf16[640,2048]{1,0:T(8,128)(2,1)} %copy-done, f32[384,640]{1,0:T(8,128)S(1)} %raw_product.1.refs_3_), custom_call_target="tpu_custom_call" | custom-call | flops 1 | bytes 1 | tf_op jit(solution)/shard_map/product/pallas_call | solution.py:560
  119.2 0.0 copy-start.1
  119.2 0.0 collective-permute-done.3
  119.2 0.0 collective-permute-done.4
  119.2 0.0 collective-permute-done.5
  119.3 1.4 %fusion.6.refs_3_ = f32[256,640]{1,0:T(8,128)S(1)} fusion(s32[]{:T(128)S(6)} %select_n.18, f32[4,160,640]{2,1,0:T(8,128)S(1)} %bitcast.48, f32[4,96,640]{2,1,0:T(8,128)S(1)} %bitcast.46, bf16[256,640]{1,0:T(8,128)(2,1)} %collective-permute-done.5, bf16[256,640]{1,0:T(8,128)(2,1)} %collective-permute-done.4, bf16[256,640]{1,0:T(8,128)(2,1)S(1)} %collective-permute-done.3), kind=kLoop, calls=%fused_computation.14 | loop fusion | flops 1146880 | bytes 4259844 | tf_op jit(solution)/shard_map/add | solution.py:590
  120.6 3.2 %collective-permute-done.6.refs_0_ = bf16[1024,256]{1,0:T(8,128)(2,1)S(1)} collective-permute-done((bf16[1024,256]{1,0:T(8,128)(2,1)}, bf16[1024,256]{1,0:T(8,128)(2,1)S(1)}, u32[]{:S(2)}, u32[]{:S(2)}) %collective-permute-start.6) | collective-permute-done | bytes 524320 | tf_op jit(solution)/shard_map/ppermute | solution.py:620
  123.9 0.0 copy-done.1
  123.9 0.6 product.3
  124.5 0.4 collective-permute-start.10
  124.9 1.5 %collective-permute-start.8 = (bf16[64,640]{1,0:T(8,128)(2,1)S(1)}, bf16[64,640]{1,0:T(8,128)(2,1)S(1)}, u32[]{:S(2)}, u32[]{:S(2)}) collective-permute-start(bf16[64,640]{1,0:T(8,128)(2,1)S(1)} %get-tuple-element.21), channel_id=1, source_target_pairs={{0,1},{1,0},{2,3},{3,2},{4,5},{5,4},{6,7},{7,6},{8,9},{9,8},{10,11... | collective-permute-start | bytes 245768 | tf_op jit(solution)/shard_map/ppermute | solution.py:590
  126.4 0.3 collective-permute-start.9
  126.7 0.8 slice_bitcast_fusion
  127.5 1.5 %collective-permute-done.10 = bf16[64,640]{1,0:T(8,128)(2,1)S(1)} collective-permute-done((bf16[64,640]{1,0:T(8,128)(2,1)S(1)}, bf16[64,640]{1,0:T(8,128)(2,1)S(1)}, u32[]{:S(2)}, u32[]{:S(2)}) %collective-permute-start.10) | collective-permute-done | bytes 81952 | tf_op jit(solution)/shard_map/ppermute | solution.py:590
  129.0 0.0 collective-permute-done.8
  129.0 2.1 %collective-permute-done.9 = bf16[64,640]{1,0:T(8,128)(2,1)S(1)} collective-permute-done((bf16[64,640]{1,0:T(8,128)(2,1)S(1)}, bf16[64,640]{1,0:T(8,128)(2,1)S(1)}, u32[]{:S(2)}, u32[]{:S(2)}) %collective-permute-start.9) | collective-permute-done | bytes 81952 | tf_op jit(solution)/shard_map/ppermute | solution.py:590
  131.1 0.8 maximum_bitcast_fusion
  (3 shorter events, 0.1 us)
Async XLA Ops:
  1.3 0.8 copy-start.4
  2.0 4.7 %copy-start.5 = (bf16[1,2,64,64]{3,2,1,0:T(8,128)(2,1)S(1)}, bf16[1,2,64,64]{3,2,1,0:T(8,128)(2,1)}, u32[]{:S(2)}) copy-start(bf16[1,2,64,64]{3,2,1,0:T(8,128)(2,1)} %param.6) | copy-start | bytes 49156
  5.4 74.4 %collective-permute-start.2 = (bf16[3088,512]{1,0:T(8,128)(2,1)}, bf16[3088,512]{1,0:T(8,128)(2,1)}, u32[]{:S(2)}, u32[]{:S(2)}) collective-permute-start(bf16[3088,512]{1,0:T(8,128)(2,1)} %raw.1.refs_4_), channel_id=1, source_target_pairs={{4,0},{8,4},{12,8},{16,12},{20,16},{24,20},{28,24},{5,1},{9,5},{13... | collective-permute-start | bytes 9486344 | tf_op jit(solution)/shard_map/ppermute | solution.py:620
  13.7 11.5 %collective-permute-start.1 = (bf16[640,2048]{1,0:T(8,128)(2,1)S(1)}, bf16[640,2048]{1,0:T(8,128)(2,1)}, u32[]{:S(2)}, u32[]{:S(2)}) collective-permute-start(bf16[640,2048]{1,0:T(8,128)(2,1)S(1)} %get-tuple-element.12), channel_id=1, source_target_pairs={{1,0},{2,1},{3,2},{5,4},{6,5},{7,6},{9,8},{10,9},{11,10},{13,12},{... | collective-permute-start | bytes 7864328 | tf_op jit(solution)/shard_map/ppermute | solution.py:629
  15.0 16.3 %collective-permute-start = (bf16[640,2048]{1,0:T(8,128)(2,1)}, bf16[640,2048]{1,0:T(8,128)(2,1)}, u32[]{:S(2)}, u32[]{:S(2)}) collective-permute-start(bf16[640,2048]{1,0:T(8,128)(2,1)} %get-tuple-element.10), channel_id=1, source_target_pairs={{1,0},{2,1},{3,2},{5,4},{6,5},{7,6},{9,8},{10,9},{11,10},{13,12},{... | collective-permute-start | bytes 7864328 | tf_op jit(solution)/shard_map/ppermute | solution.py:629
  16.3 97.3 %collective-permute-start.7 = (bf16[3072,256]{1,0:T(8,128)(2,1)}, bf16[3072,256]{1,0:T(8,128)(2,1)}, u32[]{:S(2)}, u32[]{:S(2)}) collective-permute-start(bf16[3072,256]{1,0:T(8,128)(2,1)} %bitcast.4.refs_3_), channel_id=1, source_target_pairs={{4,0},{8,4},{12,8},{16,12},{20,16},{24,20},{28,24},{5,1},{9,5},{13... | collective-permute-start | bytes 4718600 | tf_op jit(solution)/shard_map/ppermute | solution.py:620
  31.3 48.6 %copy-start.2 = (bf16[640,2048]{1,0:T(8,128)(2,1)}, bf16[640,2048]{1,0:T(8,128)(2,1)S(1)}, u32[]{:S(2)}) copy-start(bf16[640,2048]{1,0:T(8,128)(2,1)S(1)} %get-tuple-element.15.rest_0_.refs_1_) | copy-start | bytes 7864324
  38.5 1.5 %copy-start = (bf16[640,2048]{1,0:T(8,128)(2,1)}, bf16[640,2048]{1,0:T(8,128)(2,1)S(1)}, u32[]{:S(2)}) copy-start(bf16[640,2048]{1,0:T(8,128)(2,1)S(1)} %get-tuple-element.16.rest_1_.refs_2_.refs_1_) | copy-start | bytes 7864324
  88.9 30.3 %collective-permute-start.3 = (bf16[256,640]{1,0:T(8,128)(2,1)}, bf16[256,640]{1,0:T(8,128)(2,1)S(1)}, u32[]{:S(2)}, u32[]{:S(2)}) collective-permute-start(bf16[256,640]{1,0:T(8,128)(2,1)} %get-tuple-element.18), channel_id=1, source_target_pairs={{0,1},{1,0},{2,3},{3,2},{4,5},{5,4},{6,7},{7,6},{8,9},{9,8},{10,11... | collective-permute-start | bytes 983048 | tf_op jit(solution)/shard_map/ppermute | solution.py:590
  93.3 25.9 %collective-permute-start.4 = (bf16[256,640]{1,0:T(8,128)(2,1)}, bf16[256,640]{1,0:T(8,128)(2,1)}, u32[]{:S(2)}, u32[]{:S(2)}) collective-permute-start(bf16[256,640]{1,0:T(8,128)(2,1)} %get-tuple-element.19), channel_id=1, source_target_pairs={{0,2},{1,3},{2,0},{3,1},{4,6},{5,7},{6,4},{7,5},{8,10},{9,11},{10,... | collective-permute-start | bytes 983048 | tf_op jit(solution)/shard_map/ppermute | solution.py:590
  93.3 25.9 %collective-permute-start.5 = (bf16[256,640]{1,0:T(8,128)(2,1)}, bf16[256,640]{1,0:T(8,128)(2,1)}, u32[]{:S(2)}, u32[]{:S(2)}) collective-permute-start(bf16[256,640]{1,0:T(8,128)(2,1)} %get-tuple-element.20), channel_id=1, source_target_pairs={{0,3},{1,2},{2,1},{3,0},{4,7},{5,6},{6,5},{7,4},{8,11},{9,10},{10,... | collective-permute-start | bytes 983048 | tf_op jit(solution)/shard_map/ppermute | solution.py:590
  94.7 29.2 %collective-permute-start.6 = (bf16[1024,256]{1,0:T(8,128)(2,1)}, bf16[1024,256]{1,0:T(8,128)(2,1)S(1)}, u32[]{:S(2)}, u32[]{:S(2)}) collective-permute-start(bf16[1024,256]{1,0:T(8,128)(2,1)} %bitcast.13), channel_id=1, source_target_pairs={{4,0},{8,4},{12,8},{16,12},{20,16},{24,20},{28,24},{5,1},{9,5},{13... | collective-permute-start | bytes 1572872 | tf_op jit(solution)/shard_map/ppermute | solution.py:620
  113.6 1.7 %copy-start.3 = (bf16[640,2048]{1,0:T(8,128)(2,1)S(1)}, bf16[640,2048]{1,0:T(8,128)(2,1)}, u32[]{:S(2)}) copy-start(bf16[640,2048]{1,0:T(8,128)(2,1)} %copy-done.2) | copy-start | bytes 7864324
  119.2 4.6 %copy-start.1 = (bf16[640,2048]{1,0:T(8,128)(2,1)S(1)}, bf16[640,2048]{1,0:T(8,128)(2,1)}, u32[]{:S(2)}) copy-start(bf16[640,2048]{1,0:T(8,128)(2,1)} %copy-done) | copy-start | bytes 7864324
  124.5 4.5 %collective-permute-start.10 = (bf16[64,640]{1,0:T(8,128)(2,1)S(1)}, bf16[64,640]{1,0:T(8,128)(2,1)S(1)}, u32[]{:S(2)}, u32[]{:S(2)}) collective-permute-start(bf16[64,640]{1,0:T(8,128)(2,1)S(1)} %get-tuple-element.22), channel_id=1, source_target_pairs={{0,3},{1,2},{2,1},{3,0},{4,7},{5,6},{6,5},{7,4},{8,11},{9,10},{10,... | collective-permute-start | bytes 245768 | tf_op jit(solution)/shard_map/ppermute | solution.py:590
  124.9 4.1 %collective-permute-start.8 = (bf16[64,640]{1,0:T(8,128)(2,1)S(1)}, bf16[64,640]{1,0:T(8,128)(2,1)S(1)}, u32[]{:S(2)}, u32[]{:S(2)}) collective-permute-start(bf16[64,640]{1,0:T(8,128)(2,1)S(1)} %get-tuple-element.21), channel_id=1, source_target_pairs={{0,1},{1,0},{2,3},{3,2},{4,5},{5,4},{6,7},{7,6},{8,9},{9,8},{10,11... | collective-permute-start | bytes 245768 | tf_op jit(solution)/shard_map/ppermute | solution.py:590
  126.4 4.6 %collective-permute-start.9 = (bf16[64,640]{1,0:T(8,128)(2,1)S(1)}, bf16[64,640]{1,0:T(8,128)(2,1)S(1)}, u32[]{:S(2)}, u32[]{:S(2)}) collective-permute-start(bf16[64,640]{1,0:T(8,128)(2,1)S(1)} %get-tuple-element.23), channel_id=1, source_target_pairs={{0,2},{1,3},{2,0},{3,1},{4,6},{5,7},{6,4},{7,5},{8,10},{9,11},{10,... | collective-permute-start | bytes 245768 | tf_op jit(solution)/shard_map/ppermute | solution.py:590
